TPU v7x, 32 devices: a whole 2x2x4 slice. The times are simulated.
32 devices in a mesh: tm: 4 (over y, x), space: 2 (over core), head: 4 (over z).
Axes of the slice: x: 2, y: 2, z: 4, core: 2. Of those that a mesh axis runs over, the one named last changes fastest.
Arguments:
- query: bfloat16 [4, 8, 80, 5120], P('tm', 'space', None, 'head'), may hold values from -5 to 5
- key: bfloat16 [4, 8, 80, 5120], P('tm', 'space', None, 'head'), may hold values from -5 to 5
- value: bfloat16 [4, 8, 80, 5120], P('tm', 'space', None, 'head'), may hold values from -6 to 6
- window: int32 [4, 4], replicated, may hold values from -1 to 4, as said below
- out_weight: bfloat16 [5120, 5120], P('head'), may hold values from -0.078125 to 0.078125
Outputs:
- projected: bfloat16 [4, 8, 80, 5120], P('tm', 'space', None, 'head')
Inputs may be any that keep to these rules, and one draw needn't show every extreme that they name: window[f, f] = 4 for every frame f.
All inputs are finite; a program needn't handle non-finite values.
Results may differ from a plain program's by a relative error of at most 0.023.
Values may be sent and summed in bfloat16 or wider, within the bound.
No kernel may reach another device: no remote copies, remote signals or barrier semaphores. Data moves between devices by JAX's collectives and lax.ppermute only.
A program may use at most 128 MiB of HBM per device.

v0:
```python
import math

import jax
import jax.numpy as jnp
from jax import lax
from jax.sharding import PartitionSpec as P

HD = 128
HALO = 4


NEG_FILL = -1e30


def padded_2(x, sides, width):
    for axis, dim in sides:
        size, length = (lax.axis_size(axis), x.shape[dim])
        up = [(i, (i + 1) % size) for i in range(size - 1)]
        down = [(j, i) for i, j in up]
        last = lax.slice_in_dim(x, length - width, length, axis=dim)
        first = lax.slice_in_dim(x, 0, width, axis=dim)
        before = lax.ppermute(last, axis, up)
        after = lax.ppermute(first, axis, down)
        x = jnp.concatenate([before, x, after], axis=dim)
    return x


def frame_mask(widths, query_rows, key_rows, total_rows, width):
    count = widths.shape[0]
    distance = jnp.abs(query_rows[:, None] - key_rows[None, :])
    inside_grid = (key_rows >= 0) & (key_rows < total_rows)
    inside = (
        (widths[:, None, None] >= 0)
        & (distance[None] <= widths[:, None, None])
        & inside_grid[None, None, :]
    )
    span_rows = key_rows.shape[0]
    full = jnp.broadcast_to(
        inside[:, :, None, :, None], (count, query_rows.shape[0], width, span_rows, width)
    )
    return full.reshape(count * query_rows.shape[0] * width, span_rows * width)


def absorb(state, queries, keys, values, mask):
    run_max, run_sum, run_acc = state
    scale = 1.0 / math.sqrt(HD)
    scores = jnp.einsum("qhd,khd->hqk", queries, keys, preferred_element_type=jnp.float32) * scale
    new_max = jnp.maximum(run_max, jnp.max(jnp.where(mask[None], scores, NEG_FILL), axis=-1))
    weights = jnp.where(mask[None], jnp.exp(scores - new_max[..., None]), 0.0)
    factor = jnp.exp(run_max - new_max)
    new_sum = run_sum * factor + jnp.sum(weights, axis=-1)
    new_acc = run_acc * factor[..., None] + jnp.einsum(
        "hqk,khd->hqd", weights.astype(jnp.bfloat16), values, preferred_element_type=jnp.float32
    )
    return (new_max, new_sum, new_acc)


def absorb_frame(state, queries, widths, kv_frame, query_rows, key_rows, total_rows):
    span_rows, width, feats = (kv_frame.shape[1], kv_frame.shape[2], kv_frame.shape[3])
    heads_dev = feats // HD
    keys = kv_frame[0].reshape(span_rows * width, heads_dev, HD)
    values = kv_frame[1].reshape(span_rows * width, heads_dev, HD)
    mask = frame_mask(widths, query_rows, key_rows, total_rows, width)
    return absorb(state, queries, keys, values, mask)


def empty_state(heads_dev, count):
    return (
        jnp.full((heads_dev, count), NEG_FILL, jnp.float32),
        jnp.zeros((heads_dev, count), jnp.float32),
        jnp.zeros((heads_dev, count, HD), jnp.float32),
    )


def body(query, key, value, window, out_weight):
    frames_dev, rows_dev, width, feats = query.shape
    heads_dev = feats // HD
    qcount = frames_dev * rows_dev * width
    total_rows = rows_dev * lax.axis_size("space")
    first_row = lax.axis_index("space") * rows_dev
    first_frame = lax.axis_index("tm") * frames_dev
    query_rows = first_row + jnp.arange(rows_dev, dtype=jnp.int32)
    stacked = jnp.stack([key, value])
    padded = padded_2(stacked, (("space", 2),), HALO)
    key_rows = first_row - HALO + jnp.arange(rows_dev + 2 * HALO, dtype=jnp.int32)
    my_windows = lax.dynamic_slice_in_dim(window, first_frame, frames_dev, 0)
    queries = query.reshape(qcount, heads_dev, HD)
    piece = lax.all_gather(padded, "tm", axis=1, tiled=True)

    def one_frame(carry, offset):
        kv_frame = lax.dynamic_index_in_dim(piece, offset, 1, False)
        widths = lax.dynamic_index_in_dim(my_windows, offset, 1, False)
        return (
            absorb_frame(carry, queries, widths, kv_frame, query_rows, key_rows, total_rows),
            None,
        )

    result, unused = lax.scan(
        one_frame, empty_state(heads_dev, qcount), jnp.arange(piece.shape[1], dtype=jnp.int32)
    )
    run_max, run_sum, run_acc = result
    attended = (
        (run_acc / run_sum[..., None])
        .transpose(1, 0, 2)
        .reshape(qcount, feats)
        .astype(jnp.bfloat16)
    )
    share_rows = out_weight.shape[1] // lax.axis_size("head")
    mixed = lax.psum_scatter(
        lax.dot_general(
            out_weight, attended, (((0,), (1,)), ((), ())), preferred_element_type=jnp.float32
        ).astype(jnp.bfloat16),
        "head",
        scatter_dimension=0,
        tiled=True,
    ).astype(jnp.float32)
    return mixed.T.reshape(frames_dev, rows_dev, width, share_rows).astype(jnp.bfloat16)


def solution(mesh):
    placed = (
        P("tm", "space", None, "head"),
        P("tm", "space", None, "head"),
        P("tm", "space", None, "head"),
        P(),
        P("head", None),
    )
    return jax.shard_map(
        body, mesh=mesh, in_specs=placed, out_specs=P("tm", "space", None, "head"), check_vma=False
    )
```

profile of v0, /device:TPU:0, one launch (start us, length us, event | category | flops | bytes accessed | tf_op | source)
XLA Modules:
  0.0 483.2 jit_solution(14042234804960686492)
XLA Ops:
  22.4 181.0 %all-gather.2.cloned.1.call-done = bf16[2,4,12,80,1280]{4,3,2,1,0:T(8,128)(2,1)} async-done(((bf16[2,1,12,80,1280]{4,3,2,1,0:T(8,128)(2,1)}), bf16[2,4,12,80,1280]{4,3,2,1,0:T(8,128)(2,1)}) %all-gather.2.cloned.1.call-update) | async-done | bytes 19660816 | tf_op jit(solution)/shard_map/all_gather | solution.py:88
  203.4 197.0 %while.15 = (s32[]{:T(128)}, f32[10,320]{1,0:T(8,128)S(1)}, f32[10,320]{1,0:T(8,128)S(1)}, f32[10,320,128]{2,1,0:T(8,128)}, s32[4]{0:T(128)S(1)}, /*index=5*/s32...) while((s32[]{:T(128)}, f32[10,320]{1,0:T(8,128)S(1)}, ...), condition=%wide.region_3.4_spmd.clone, body=%wide.region_0.3_spmd.clone.sunk | while | flops 1607901184 | bytes 68198984 | solution.py:98
  209.5 4.2 constant_dynamic-slice_fusion.5
  213.8 5.8 %squeeze.19 = bf16[960,10,128]{2,1,0:T(8,128)(2,1)} reshape(bf16[1,1,12,80,1280]{4,3,2,1,0:T(8,128)(2,1)} %get-tuple-element.218) | data formatting | bytes 4915200 | tf_op jit(solution)/shard_map/while/body/eval_jaxpr/reshape;while/body/eval_jaxpr/squeeze | solution.py:61
  219.5 10.4 %fusion.45 = (f32[10,320]{1,0:T(8,128)S(1)}, f32[10,960,320]{1,2,0:T(8,128)}) fusion(pred[320,960]{1,0:T(8,128)(4,1)S(1)} %copy.32, bf16[320,10,128]{2,0,1:T(8,128)(2,1)} %get-tuple-element.259, bf16[960,10,128]{2,1,0:T(8,128)(2,1)} %squeeze.19), kind=kOutput, calls=%fused_computation.4.clone.1 | convolution fusion | flops 795644800 | bytes 15884800 | tf_op jit(solution)/shard_map/while/body/eval_jaxpr/qhd,khd->hqk/dot_general | solution.py:47
  230.0 8.6 %fusion.46 = f32[10,320]{1,0:T(8,128)S(1)} fusion(f32[10,960,320]{1,2,0:T(8,128)} %get-tuple-element.220, f32[10,320]{1,0:T(8,128)S(1)} %select_maximum_fusion.2, pred[320,960]{1,0:T(8,128)(4,1)S(1)} %copy.32), kind=kLoop, calls=%fused_computation.8.clone.1 | loop fusion | flops 12284800 | bytes 12620800 | tf_op jit(solution)/shard_map/while/body/eval_jaxpr/reduce_sum | solution.py:51
  242.2 10.2 %fusion.48 = f32[10,320,128]{2,1,0:T(8,128)} fusion(f32[10,320,128]{2,1,0:T(8,128)} %get-tuple-element.241, bf16[960,10,128]{2,1,0:T(8,128)(2,1)} %squeeze.20, f32[10,960,320]{1,2,0:T(8,128)} %get-tuple-element.220, f32[10,320]{1,0:T(8,128)S(1)} %select_maximum_fusion.2, pred[320,960]{1,0:T(8,128)(4,1)S(1)} %copy.32, ...), kind=kOutput, calls=%fused_computation.15.clone.1 | convolution fusion | flops 799948800 | bytes 18355200 | tf_op jit(solution)/shard_map/while/body/eval_jaxpr/hqk,khd->hqd/dot_general | solution.py:52
  258.6 4.2 constant_dynamic-slice_fusion.5
  262.8 5.8 %squeeze.19 = bf16[960,10,128]{2,1,0:T(8,128)(2,1)} reshape(bf16[1,1,12,80,1280]{4,3,2,1,0:T(8,128)(2,1)} %get-tuple-element.218) | data formatting | bytes 4915200 | tf_op jit(solution)/shard_map/while/body/eval_jaxpr/reshape;while/body/eval_jaxpr/squeeze | solution.py:61
  268.6 10.4 %fusion.45 = (f32[10,320]{1,0:T(8,128)S(1)}, f32[10,960,320]{1,2,0:T(8,128)}) fusion(pred[320,960]{1,0:T(8,128)(4,1)S(1)} %copy.32, bf16[320,10,128]{2,0,1:T(8,128)(2,1)} %get-tuple-element.259, bf16[960,10,128]{2,1,0:T(8,128)(2,1)} %squeeze.19), kind=kOutput, calls=%fused_computation.4.clone.1 | convolution fusion | flops 795644800 | bytes 15884800 | tf_op jit(solution)/shard_map/while/body/eval_jaxpr/qhd,khd->hqk/dot_general | solution.py:47
  279.0 8.6 %fusion.46 = f32[10,320]{1,0:T(8,128)S(1)} fusion(f32[10,960,320]{1,2,0:T(8,128)} %get-tuple-element.220, f32[10,320]{1,0:T(8,128)S(1)} %select_maximum_fusion.2, pred[320,960]{1,0:T(8,128)(4,1)S(1)} %copy.32), kind=kLoop, calls=%fused_computation.8.clone.1 | loop fusion | flops 12284800 | bytes 12620800 | tf_op jit(solution)/shard_map/while/body/eval_jaxpr/reduce_sum | solution.py:51
  291.3 10.4 %fusion.48 = f32[10,320,128]{2,1,0:T(8,128)} fusion(f32[10,320,128]{2,1,0:T(8,128)} %get-tuple-element.241, bf16[960,10,128]{2,1,0:T(8,128)(2,1)} %squeeze.20, f32[10,960,320]{1,2,0:T(8,128)} %get-tuple-element.220, f32[10,320]{1,0:T(8,128)S(1)} %select_maximum_fusion.2, pred[320,960]{1,0:T(8,128)(4,1)S(1)} %copy.32, ...), kind=kOutput, calls=%fused_computation.15.clone.1 | convolution fusion | flops 799948800 | bytes 18355200 | tf_op jit(solution)/shard_map/while/body/eval_jaxpr/hqk,khd->hqd/dot_general | solution.py:52
  307.9 4.2 constant_dynamic-slice_fusion.5
  312.1 5.8 %squeeze.19 = bf16[960,10,128]{2,1,0:T(8,128)(2,1)} reshape(bf16[1,1,12,80,1280]{4,3,2,1,0:T(8,128)(2,1)} %get-tuple-element.218) | data formatting | bytes 4915200 | tf_op jit(solution)/shard_map/while/body/eval_jaxpr/reshape;while/body/eval_jaxpr/squeeze | solution.py:61
  317.9 10.4 %fusion.45 = (f32[10,320]{1,0:T(8,128)S(1)}, f32[10,960,320]{1,2,0:T(8,128)}) fusion(pred[320,960]{1,0:T(8,128)(4,1)S(1)} %copy.32, bf16[320,10,128]{2,0,1:T(8,128)(2,1)} %get-tuple-element.259, bf16[960,10,128]{2,1,0:T(8,128)(2,1)} %squeeze.19), kind=kOutput, calls=%fused_computation.4.clone.1 | convolution fusion | flops 795644800 | bytes 15884800 | tf_op jit(solution)/shard_map/while/body/eval_jaxpr/qhd,khd->hqk/dot_general | solution.py:47
  328.3 8.6 %fusion.46 = f32[10,320]{1,0:T(8,128)S(1)} fusion(f32[10,960,320]{1,2,0:T(8,128)} %get-tuple-element.220, f32[10,320]{1,0:T(8,128)S(1)} %select_maximum_fusion.2, pred[320,960]{1,0:T(8,128)(4,1)S(1)} %copy.32), kind=kLoop, calls=%fused_computation.8.clone.1 | loop fusion | flops 12284800 | bytes 12620800 | tf_op jit(solution)/shard_map/while/body/eval_jaxpr/reduce_sum | solution.py:51
  340.6 10.4 %fusion.48 = f32[10,320,128]{2,1,0:T(8,128)} fusion(f32[10,320,128]{2,1,0:T(8,128)} %get-tuple-element.241, bf16[960,10,128]{2,1,0:T(8,128)(2,1)} %squeeze.20, f32[10,960,320]{1,2,0:T(8,128)} %get-tuple-element.220, f32[10,320]{1,0:T(8,128)S(1)} %select_maximum_fusion.2, pred[320,960]{1,0:T(8,128)(4,1)S(1)} %copy.32, ...), kind=kOutput, calls=%fused_computation.15.clone.1 | convolution fusion | flops 799948800 | bytes 18355200 | tf_op jit(solution)/shard_map/while/body/eval_jaxpr/hqk,khd->hqd/dot_general | solution.py:52
  357.2 4.2 constant_dynamic-slice_fusion.5
  361.4 5.8 %squeeze.19 = bf16[960,10,128]{2,1,0:T(8,128)(2,1)} reshape(bf16[1,1,12,80,1280]{4,3,2,1,0:T(8,128)(2,1)} %get-tuple-element.218) | data formatting | bytes 4915200 | tf_op jit(solution)/shard_map/while/body/eval_jaxpr/reshape;while/body/eval_jaxpr/squeeze | solution.py:61
  367.2 10.4 %fusion.45 = (f32[10,320]{1,0:T(8,128)S(1)}, f32[10,960,320]{1,2,0:T(8,128)}) fusion(pred[320,960]{1,0:T(8,128)(4,1)S(1)} %copy.32, bf16[320,10,128]{2,0,1:T(8,128)(2,1)} %get-tuple-element.259, bf16[960,10,128]{2,1,0:T(8,128)(2,1)} %squeeze.19), kind=kOutput, calls=%fused_computation.4.clone.1 | convolution fusion | flops 795644800 | bytes 15884800 | tf_op jit(solution)/shard_map/while/body/eval_jaxpr/qhd,khd->hqk/dot_general | solution.py:47
  377.6 8.6 %fusion.46 = f32[10,320]{1,0:T(8,128)S(1)} fusion(f32[10,960,320]{1,2,0:T(8,128)} %get-tuple-element.220, f32[10,320]{1,0:T(8,128)S(1)} %select_maximum_fusion.2, pred[320,960]{1,0:T(8,128)(4,1)S(1)} %copy.32), kind=kLoop, calls=%fused_computation.8.clone.1 | loop fusion | flops 12284800 | bytes 12620800 | tf_op jit(solution)/shard_map/while/body/eval_jaxpr/reduce_sum | solution.py:51
  389.9 10.4 %fusion.48 = f32[10,320,128]{2,1,0:T(8,128)} fusion(f32[10,320,128]{2,1,0:T(8,128)} %get-tuple-element.241, bf16[960,10,128]{2,1,0:T(8,128)(2,1)} %squeeze.20, f32[10,960,320]{1,2,0:T(8,128)} %get-tuple-element.220, f32[10,320]{1,0:T(8,128)S(1)} %select_maximum_fusion.2, pred[320,960]{1,0:T(8,128)(4,1)S(1)} %copy.32, ...), kind=kOutput, calls=%fused_computation.15.clone.1 | convolution fusion | flops 799948800 | bytes 18355200 | tf_op jit(solution)/shard_map/while/body/eval_jaxpr/hqk,khd->hqd/dot_general | solution.py:52
  402.9 10.9 %fusion.25 = bf16[5120,320]{0,1:T(8,128)(2,1)} fusion(bf16[320,1280]{0,1:T(8,128)(2,1)S(1)} %bitcast.58, bf16[1280,5120]{1,0:T(8,128)(2,1)} %param.11), kind=kOutput, calls=%fused_computation.32 | convolution fusion | flops 4195942400 | bytes 17203200 | tf_op jit(solution)/shard_map/dot_general | solution.py:110
  413.9 62.4 %reduce-scatter.2.cloned.1.call-done = bf16[1280,320]{0,1:T(8,128)(2,1)} async-done(((bf16[5120,320]{0,1:T(8,128)(2,1)}), bf16[1280,320]{0,1:T(8,128)(2,1)}) %reduce-scatter.2.cloned.1.call-update) | async-done | bytes 819216 | tf_op jit(solution)/shard_map/reduce_scatter | solution.py:109
  (81 shorter events, 49.9 us)
Async XLA Ops:
  6.5 15.8 %copy-start = (s32[4,4]{1,0:T(4,128)S(1)}, s32[4,4]{1,0:T(4,128)}, u32[]{:S(2)}) copy-start(s32[4,4]{1,0:T(4,128)} %param.10) | copy-start | bytes 196
  6.5 196.8 %all-gather.2.cloned.1.call-start = ((), (), s32[]{:S(2)}) async-start(), calls=%async_computation.1 | async-start | bytes 24576000 | tf_op jit(solution)/shard_map/all_gather | solution.py:88
  8.1 5.5 %collective-permute-start = (bf16[2,1,4,80,1280]{4,3,2,1,0:T(8,128)(2,1)S(1)}, bf16[2,1,4,80,1280]{4,3,2,1,0:T(8,128)(2,1)S(1)}, u32[]{:S(2)}, u32[]{:S(2)}) collective-permute-start(bf16[2,1,4,80,1280]{4,3,2,1,0:T(8,128)(2,1)S(1)} %pad_maximum_fusion.1), channel_id=1, source_target_pairs={{0,4},{1,5},{2,6},{3,7},{8,12},{9,13},{10,14},{11,15},{16,20},{17,... | collective-permute-start | bytes 4915208 | tf_op jit(solution)/shard_map/ppermute | solution.py:22
  10.6 5.4 %collective-permute-start.1 = (bf16[2,1,4,80,1280]{4,3,2,1,0:T(8,128)(2,1)S(1)}, bf16[2,1,4,80,1280]{4,3,2,1,0:T(8,128)(2,1)S(1)}, u32[]{:S(2)}, u32[]{:S(2)}) collective-permute-start(bf16[2,1,4,80,1280]{4,3,2,1,0:T(8,128)(2,1)S(1)} %pad_maximum_fusion.1), channel_id=1, source_target_pairs={{4,0},{5,1},{6,2},{7,3},{12,8},{13,9},{14,10},{15,11},{20,16},{21,... | collective-permute-start | bytes 4915208 | tf_op jit(solution)/shard_map/ppermute | solution.py:23
  19.6 1.1 copy-start.2
  19.6 456.7 %reduce-scatter.2.cloned.1.call-start = ((), (), s32[]{:S(2)}) async-start(), calls=%async_computation.2 | async-start | bytes 4096000 | tf_op jit(solution)/shard_map/reduce_scatter | solution.py:109
  402.9 73.4 %copy-start.1 = (s32[4,4]{1,0:T(4,128)S(1)}, s32[4,4]{1,0:T(4,128)}, u32[]{:S(2)}) copy-start(s32[4,4]{1,0:T(4,128)} %param.10) | copy-start | bytes 196
Sparse Core Ops, SparseCore 0:
  19.7 183.5 all-gather.1
  414.0 62.2 reduce-scatter.1
where the time goes:
time: 484 us; the launch traced here: 483 us
  waiting for transfers between devices  248 us (51%)
  matrix products  94.2 us (19%)
  local copies, waits for them, and re-layouts  66.9 us (14%)
  other arithmetic  49.6 us (10%)
  between operations  13.5 us (3%)
  loops' own time  7.59 us (2%)
    all_gather x1, waiting for transfers between devices, body(): piece = lax.all_gather(padded, 'tm', axis=1, tiled=True)  181 us
    reduce_scatter x1, waiting for transfers between devices, body(): lax.psum_scatter(lax.dot_general(out_weight, attended, (((0,), (1,)), (()...  62.4 us
    dot_general x4, matrix products, absorb(): jnp.einsum('qhd,khd->hqk', queries, keys, preferred_element_type=jnp.floa...  41.8 us
    dot_general x4, matrix products, absorb(): jnp.einsum('hqk,khd->hqd', weights.astype(jnp.bfloat16), values, preferre...  41.5 us
    reduce_sum x4, other arithmetic, absorb(): new_sum = run_sum * factor + jnp.sum(weights, axis=-1)  34.5 us
    squeeze x4, local copies, waits for them, and re-layouts, absorb_frame(): keys = kv_frame[0].reshape(span_rows * width, heads_dev, HD)  23.1 us
    slice x4, local copies, waits for them, and re-layouts, absorb_frame(): values = kv_frame[1].reshape(span_rows * width, heads_dev, HD)  16.9 us
    squeeze x4, local copies, waits for them, and re-layouts, absorb_frame(): values = kv_frame[1].reshape(span_rows * width, heads_dev, HD)  14.4 us
  transfers between devices with their start and end apart: 4, of which 4 were waited for; matrix products, arithmetic and copies ran while one was open for 0% of the time, Pallas kernels for 0%

commit v1 on v0

--- a/solution.py
+++ b/solution.py
@@ -3,13 +3,251 @@
 import jax
 import jax.numpy as jnp
 from jax import lax
+from jax.experimental import pallas as pl
+from jax.experimental.pallas import tpu as pltpu
 from jax.sharding import PartitionSpec as P
 
 HD = 128
 HALO = 4
-
-
 NEG_FILL = -1e30
+CHUNKS = 2
+VMEM = pltpu.CompilerParams(vmem_limit_bytes=40 * 1024 * 1024)
+
+
+def pack_kernel(t_ref, q_ref, k_ref, v_ref, *outs, full, share, row):
+    t = t_ref[0]
+    tokens = q_ref.shape[0]
+    partners = len(outs) // (1 + CHUNKS)
+    part = tokens // CHUNKS
+    for m in range(partners):
+        chip = t ^ m
+        heads = [chip * full + i for i in range(full)] + [partners * full + chip // share]
+        lanes = [pl.ds(pl.multiple_of(h * HD, HD), HD) for h in heads]
+        kv = outs[m]
+        for i, lane in enumerate(lanes):
+            kv[pl.ds(i * tokens, tokens)] = k_ref[:, lane]
+            kv[pl.ds((full + 1 + i) * tokens, tokens)] = v_ref[:, lane]
+        for c in range(CHUNKS):
+            q = outs[(1 + c) * partners + m]
+            for i in range(full):
+                q[pl.ds(i * part, part)] = q_ref[pl.ds(c * part, part), lanes[i]]
+            start = pl.multiple_of(c * part + (chip % share) * row, 16)
+            q[pl.ds(full * part, row)] = q_ref[pl.ds(start, row), lanes[full]]
+
+
+def pack(t, q, k, v, partners, full, share, row):
+    tokens = q.shape[0]
+    part = tokens // CHUNKS
+    slabs = 2 * (full + 1) * tokens
+    queries = full * part + row
+    whole = pl.BlockSpec(memory_space=pltpu.VMEM)
+    shapes = [jax.ShapeDtypeStruct((slabs, HD), q.dtype)] * partners
+    shapes += [jax.ShapeDtypeStruct((queries, HD), q.dtype)] * (partners * CHUNKS)
+
+    def kernel(*refs):
+        pack_kernel(*refs, full=full, share=share, row=row)
+
+    return pl.pallas_call(
+        kernel,
+        out_shape=shapes,
+        in_specs=[pl.BlockSpec(memory_space=pltpu.SMEM), whole, whole, whole],
+        out_specs=[whole] * len(shapes),
+        compiler_params=VMEM,
+        name="pack",
+    )(t, q, k, v)
+
+
+def attend_kernel(bias_ref, *refs, partners, slots, row, units):
+    queries = refs[:partners]
+    near = refs[partners : 2 * partners]
+    far = refs[2 * partners : 3 * partners]
+    outs = refs[3 * partners : 4 * partners]
+    keys, values, scores, sems = refs[4 * partners :]
+    tokens = near[0].shape[0] // (2 * slots)
+    count = keys.shape[1]
+    copies = []
+    for slot in range(slots):
+        for m in range(partners):
+            for side, source in enumerate((near[m], far[m])):
+                place = pl.ds((2 * m + side) * tokens, tokens)
+                for kind, target in enumerate((keys.at[slot, place], values.at[slot, place, pl.ds(0, HD)])):
+                    start = (kind * slots + slot) * tokens
+                    copy = pltpu.make_async_copy(
+                        source.at[pl.ds(start, tokens)], target, sems.at[len(copies)]
+                    )
+                    copy.start()
+                    copies.append(copy)
+    values[:, :, HD:] = jnp.ones((slots, count, HD), values.dtype)
+    for copy in copies:
+        copy.wait()
+    factor = math.log2(math.e) / math.sqrt(HD)
+    per_slot = units // (slots - 1) if units > 1 else 1
+
+    def unit(u, carry):
+        slot = u // per_slot
+        at = pl.ds(pl.multiple_of(u * row, 16), row)
+        for m in range(partners):
+            s = lax.dot_general(
+                queries[m][at], keys[slot], (((1,), (1,)), ((), ())), preferred_element_type=jnp.float32
+            )
+            s = s + bias_ref[u * partners + m]
+            top = jnp.max(s, axis=-1, keepdims=True)
+            weights = jnp.exp2((s - top) * factor).astype(jnp.bfloat16)
+            summed = jnp.dot(weights, values[slot], preferred_element_type=jnp.float32)
+            outs[m][at] = (summed[:, :HD] / summed[:, HD:]).astype(jnp.bfloat16)
+        return carry
+
+    lax.fori_loop(0, units, unit, 0)
+
+
+def attend(bias, queries, near, far, slots, row):
+    partners = len(queries)
+    units = queries[0].shape[0] // row
+    tokens = near[0].shape[0] // (2 * slots)
+    count = 2 * partners * tokens
+    whole = pl.BlockSpec(memory_space=pltpu.VMEM)
+    anywhere = pl.BlockSpec(memory_space=pl.ANY)
+
+    def kernel(*refs):
+        attend_kernel(*refs, partners=partners, slots=slots, row=row, units=units)
+
+    work = units * partners * row * count
+    return pl.pallas_call(
+        kernel,
+        out_shape=[jax.ShapeDtypeStruct(q.shape, q.dtype) for q in queries],
+        in_specs=[whole] * (1 + partners) + [anywhere] * (2 * partners),
+        out_specs=[whole] * partners,
+        scratch_shapes=[
+            pltpu.VMEM((slots, count, HD), jnp.bfloat16),
+            pltpu.VMEM((slots, count, 2 * HD), jnp.bfloat16),
+            pltpu.VMEM((row, count), jnp.float32),
+            pltpu.SemaphoreType.DMA((4 * slots * partners,)),
+        ],
+        compiler_params=VMEM,
+        cost_estimate=pl.CostEstimate(
+            flops=work * HD * 4, bytes_accessed=count * HD * 4 * slots, transcendentals=work
+        ),
+        name="attend",
+    )(bias, *queries, *near, *far)
+
+
+def project_kernel(t_ref, *refs, partners, full, share, row):
+    parts = refs[:partners]
+    weight, out, mixed = refs[partners:]
+    part = mixed.shape[0]
+
+    @pl.when(pl.program_id(0) == 0)
+    def gather():
+        for m in range(partners):
+            chip = t_ref[0] ^ m
+            for i in range(full):
+                lane = pl.ds(pl.multiple_of((chip * full + i) * HD, HD), HD)
+                mixed[:, lane] = parts[m][pl.ds(i * part, part)]
+            lane = pl.ds(pl.multiple_of((partners * full + chip // share) * HD, HD), HD)
+            rows = pl.ds(pl.multiple_of((chip % share) * row, 16), row)
+            mixed[rows, lane] = parts[m][pl.ds(full * part, row)]
+
+    out[0] = jnp.dot(mixed[...], weight[...], preferred_element_type=jnp.float32).astype(out.dtype)
+
+
+def project(t, parts, weight, shares, full, share, row):
+    partners = len(parts)
+    feats, width = weight.shape
+    part = (parts[0].shape[0] - row) // full
+    block = width // shares
+    whole = pl.BlockSpec(memory_space=pltpu.VMEM)
+
+    def kernel(*refs):
+        project_kernel(*refs, partners=partners, full=full, share=share, row=row)
+
+    return pl.pallas_call(
+        kernel,
+        grid=(shares,),
+        out_shape=jax.ShapeDtypeStruct((shares, part, block), jnp.bfloat16),
+        in_specs=[pl.BlockSpec(memory_space=pltpu.SMEM)]
+        + [whole] * partners
+        + [pl.BlockSpec((feats, block), lambda i: (0, i))],
+        out_specs=pl.BlockSpec((1, part, block), lambda i: (i, 0, 0)),
+        scratch_shapes=[pltpu.VMEM((part, feats), jnp.bfloat16)],
+        compiler_params=VMEM,
+        cost_estimate=pl.CostEstimate(
+            flops=2 * part * feats * width, bytes_accessed=2 * feats * width, transcendentals=0
+        ),
+        name="project",
+    )(t, *parts, weight)
+
+
+def scatter_sum(mixed, axis):
+    size = lax.axis_size(axis)
+    place = lax.axis_index(axis)
+
+    def share(d):
+        return lax.dynamic_index_in_dim(mixed, jnp.clip(d, 0, size - 1), 0, False)
+
+    right = left = None
+    for step in range(1, size):
+        go_right = share(place + size - step)
+        go_left = share(place - size + step)
+        if right is not None:
+            go_right, go_left = go_right + right, go_left + left
+        right = lax.ppermute(go_right, axis, [(i, i + 1) for i in range(step)])
+        left = lax.ppermute(go_left, axis, [(size - 1 - i, size - 2 - i) for i in range(step)])
+    return share(place) + right + left
+
+
+def exchange_plan(query, key, value, window, out_weight):
+    frames_dev, rows_dev, width, feats = query.shape
+    partners = lax.axis_size("tm")
+    heads = feats // HD
+    full = heads // partners
+    share = partners // (heads - full * partners)
+    t = lax.axis_index("tm").astype(jnp.int32)
+    s = lax.axis_index("space").astype(jnp.int32)
+    tokens = rows_dev * width
+    rows_part = rows_dev // CHUNKS
+    t1 = t.reshape(1)
+
+    packed = pack(
+        t1, *(a.reshape(tokens, feats) for a in (query, key, value)), partners, full, share, width
+    )
+    near, asked = packed[:partners], packed[partners:]
+
+    def swap(x, m):
+        return x if m == 0 else lax.ppermute(x, "tm", [(i, i ^ m) for i in range(partners)])
+
+    near = [swap(x, m) for m, x in enumerate(near)]
+    far = [lax.ppermute(x, "space", [(0, 1), (1, 0)]) for x in near]
+
+    order = t ^ jnp.arange(partners, dtype=jnp.int32)
+    widths = window[order][:, order]
+    units = full * rows_part + 1
+    key_rows = jnp.concatenate([rows_dev * side + jnp.arange(rows_dev, dtype=jnp.int32) for side in (s, 1 - s)])
+    unit_rows = jnp.concatenate([jnp.arange(units - 1, dtype=jnp.int32) % rows_part, (t % share)[None]])
+    query_rows = rows_dev * s + rows_part * jnp.arange(CHUNKS, dtype=jnp.int32)[:, None] + unit_rows[None]
+    distance = jnp.abs(query_rows[:, :, None] - key_rows)[:, :, None, None, :]
+    wide = widths[None, None, :, :, None]
+    bias = jnp.where((wide >= 0) & (distance <= wide), 0.0, NEG_FILL).astype(jnp.float32)
+    bias = jnp.repeat(bias, width, axis=-1).reshape(CHUNKS, units * partners, 1, -1)
+
+    outputs = []
+    for c in range(CHUNKS):
+        queries = [swap(x, m) for m, x in enumerate(asked[c * partners : (c + 1) * partners])]
+        done = attend(bias[c], queries, near, far, full + 1, width)
+        done = [swap(x, m) for m, x in enumerate(done)]
+        mixed = project(t1, done, out_weight, lax.axis_size("head"), full, share, width)
+        outputs.append(scatter_sum(mixed, "head"))
+    return jnp.concatenate(outputs, axis=0).reshape(frames_dev, rows_dev, width, -1)
+
+
+def can_exchange(mesh, query, key, value, window, out_weight):
+    partners, sides = mesh.shape["tm"], mesh.shape["space"]
+    frames, rows, width, feats = query.shape
+    heads = feats // HD // mesh.shape["head"]
+    rows_dev = rows // sides
+    rest = heads % partners
+    if partners & (partners - 1) or sides != 2 or frames != partners or rest == 0 or heads < partners:
+        return False
+    return partners % rest == 0 and rows_dev == CHUNKS * (partners // rest) and width % 16 == 0
 
 
 def padded_2(x, sides, width):
@@ -72,7 +310,7 @@
     )
 
 
-def body(query, key, value, window, out_weight):
+def gather_plan(query, key, value, window, out_weight):
     frames_dev, rows_dev, width, feats = query.shape
     heads_dev = feats // HD
     qcount = frames_dev * rows_dev * width
@@ -125,6 +363,11 @@
         P(),
         P("head", None),
     )
-    return jax.shard_map(
-        body, mesh=mesh, in_specs=placed, out_specs=P("tm", "space", None, "head"), check_vma=False
-    )
+
+    def run(*args):
+        body = exchange_plan if can_exchange(mesh, *args) else gather_plan
+        return jax.shard_map(
+            body, mesh=mesh, in_specs=placed, out_specs=P("tm", "space", None, "head"), check_vma=False
+        )(*args)
+
+    return run

time: 484 us -> 171 us (0.35)
  waiting for transfers between devices: 248 us -> 58.9 us
  matrix products: 94.2 us -> 0 us
  local copies, waits for them, and re-layouts: 66.9 us -> 15.3 us
  other arithmetic: 49.6 us -> 1.92 us
  Pallas kernels: 0 us -> 47.2 us
  starting transfers between devices: 3.8 us -> 43.9 us
  between operations: 13.5 us -> 0.36 us
  loops' own time: 7.59 us -> 0 us
    all_gather x1 -> x0, waiting for transfers between devices: 181 us -> none  [body(): piece = lax.all_gather(padded, 'tm', axis=1, tiled=True)]
    dot_general x9 -> x0, matrix products: 94.2 us -> none  [the longest x4 41.8 us: absorb(): jnp.einsum('qhd,khd->hqk', queries, keys, preferred_element_type=jnp.floa...]
    reduce_scatter x1 -> x0, waiting for transfers between devices: 62.4 us -> none  [body(): lax.psum_scatter(lax.dot_general(out_weight, attended, (((0,), (1,)), (()...]
    ppermute x2 -> x31, waiting for transfers between devices: 4.1 us -> 58.9 us  [the longest x15 24.6 us: swap(): lax.ppermute(x, 'tm', [(i, i ^ m) for i in range(partners)])]
    pallas_call x0 -> x5, Pallas kernels: none -> 47.2 us  [the longest x2 32.9 us: attend(): pl.pallas_call(kernel, out_shape=[jax.ShapeDtypeStruct(q.shape, q.dtype)...]
    ppermute x2 -> x31, starting transfers between devices: 3.75 us -> 43.9 us  [the longest x6 19.4 us: scatter_sum(): right = lax.ppermute(go_right, axis, [(i, i + 1) for i in range(step)])]
    squeeze x8 -> x2, local copies, waits for them, and re-layouts: 37.5 us -> 0.13 us  [share(): return lax.dynamic_index_in_dim(mixed, jnp.clip(d, 0, size - 1), 0, False)]
    reduce_sum x4 -> x0, other arithmetic: 34.5 us -> none  [absorb(): new_sum = run_sum * factor + jnp.sum(weights, axis=-1)]
  transfers between devices with their start and end apart: 4 -> 31, of which waited for: 4 -> 9; matrix products, arithmetic and copies ran while one was open for 0% -> 4% of each run, Pallas kernels for 0% -> 27%
where the time goes in v1:
time: 171 us; the launch traced here: 168 us
  waiting for transfers between devices  58.9 us (34%)
  Pallas kernels  47.2 us (28%)
  starting transfers between devices  43.9 us (26%)
  local copies, waits for them, and re-layouts  15.3 us (9%)
  other arithmetic  1.92 us (1%)
    pallas_call x2, Pallas kernels, attend(): pl.pallas_call(kernel, out_shape=[jax.ShapeDtypeStruct(q.shape, q.dtype)...  32.9 us
    ppermute x15, waiting for transfers between devices, swap(): lax.ppermute(x, 'tm', [(i, i ^ m) for i in range(partners)])  24.6 us
    ppermute x6, starting transfers between devices, scatter_sum(): right = lax.ppermute(go_right, axis, [(i, i + 1) for i in range(step)])  19.4 us
    ppermute x15, starting transfers between devices, swap(): lax.ppermute(x, 'tm', [(i, i ^ m) for i in range(partners)])  18.7 us
    ppermute x6, waiting for transfers between devices, scatter_sum(): lax.ppermute(go_left, axis, [(size - 1 - i, size - 2 - i) for i in range(...  17.8 us
    ppermute x6, waiting for transfers between devices, scatter_sum(): right = lax.ppermute(go_right, axis, [(i, i + 1) for i in range(step)])  16.5 us
    pallas_call x2, Pallas kernels, project(): pl.pallas_call(kernel, grid=(shares,), out_shape=jax.ShapeDtypeStruct((sh...  13.1 us
    unnamed x26, local copies, waits for them, and re-layouts  9.35 us
  transfers between devices with their start and end apart: 31, of which 9 were waited for; matrix products, arithmetic and copies ran while one was open for 4% of the time, Pallas kernels for 27%

profile of v1, /device:TPU:0, one launch (start us, length us, event | category | flops | bytes accessed | tf_op | source)
XLA Modules:
  0.0 167.6 jit_solution(11205177496396591221)
XLA Ops:
  7.3 2.9 %collective-permute-start = (bf16[400,128]{1,0:T(8,128)(2,1)S(1)}, bf16[400,128]{1,0:T(8,128)(2,1)S(1)}, u32[]{:S(2)}, u32[]{:S(2)}) collective-permute-start(bf16[400,128]{1,0:T(8,128)(2,1)S(1)} %get-tuple-element.26), channel_id=1, source_target_pairs={{0,8},{8,0},{16,24},{24,16},{1,9},{9,1},{17,25},{25,17},{2,10},{10... | collective-permute-start | bytes 307208 | tf_op jit(solution)/shard_map/ppermute | solution.py:216
  10.3 2.0 %collective-permute-start.4 = (bf16[1920,128]{1,0:T(8,128)(2,1)}, bf16[1920,128]{1,0:T(8,128)(2,1)S(1)}, u32[]{:S(2)}, u32[]{:S(2)}) collective-permute-start(bf16[1920,128]{1,0:T(8,128)(2,1)} %get-tuple-element.31), channel_id=1, source_target_pairs={{0,16},{8,24},{16,0},{24,8},{1,17},{9,25},{17,1},{25,9},{2,18},{10... | collective-permute-start | bytes 1474568 | tf_op jit(solution)/shard_map/ppermute | solution.py:216
  12.3 1.4 collective-permute-start.5
  15.3 9.1 %collective-permute-done.3.refs_6_ = bf16[1920,128]{1,0:T(8,128)(2,1)S(1)} collective-permute-done((bf16[1920,128]{1,0:T(8,128)(2,1)S(1)}, bf16[1920,128]{1,0:T(8,128)(2,1)S(1)}, u32[]{:S(2)}, u32[]{:S(2)}) %collective-permute-start.3) | collective-permute-done | bytes 491552 | tf_op jit(solution)/shard_map/ppermute | solution.py:216
  25.0 10.5 %collective-permute-done.5.refs_8_ = bf16[1920,128]{1,0:T(8,128)(2,1)S(1)} collective-permute-done((bf16[1920,128]{1,0:T(8,128)(2,1)}, bf16[1920,128]{1,0:T(8,128)(2,1)S(1)}, u32[]{:S(2)}, u32[]{:S(2)}) %collective-permute-start.5) | collective-permute-done | bytes 491552 | tf_op jit(solution)/shard_map/ppermute | solution.py:216
  36.0 5.0 %collective-permute-done.1.refs_3_ = bf16[400,128]{1,0:T(8,128)(2,1)S(1)} collective-permute-done((bf16[400,128]{1,0:T(8,128)(2,1)S(1)}, bf16[400,128]{1,0:T(8,128)(2,1)S(1)}, u32[]{:S(2)}, u32[]{:S(2)}) %collective-permute-start.1) | collective-permute-done | bytes 102432 | tf_op jit(solution)/shard_map/ppermute | solution.py:216
  47.5 1.5 collective-permute-start.19
  53.8 16.9 %attend.2 = (bf16[400,128]{1,0:T(8,128)(2,1)S(1)}, bf16[400,128]{1,0:T(8,128)(2,1)S(1)}, bf16[400,128]{1,0:T(8,128)(2,1)S(1)}, bf16[400,128]{1,0:T(8,128)(2,1)S(1)}) custom-call(f32[20,1,2560]{2,1,0:T(1,128)S(1)} %broadcast_in_dim.32.refs_0_, bf16[400,128]{1,0:T(8,128)(2,1)S(1)} %copy-done.8, bf16[400,128]{1,0:T(8,128)(2,1)S(1)} %copy-done.10, ...), custom_call_target="tpu_custom_call" | custom-call | flops 2097152000 | bytes 3932160 | tf_op jit(solution)/shard_map/attend/pallas_call | solution.py:115
  70.6 1.4 collective-permute-start.10
  72.8 1.4 collective-permute-start.12
  74.2 16.0 %attend.3 = (bf16[400,128]{1,0:T(8,128)(2,1)S(1)}, bf16[400,128]{1,0:T(8,128)(2,1)S(1)}, bf16[400,128]{1,0:T(8,128)(2,1)S(1)}, bf16[400,128]{1,0:T(8,128)(2,1)S(1)}) custom-call(f32[20,1,2560]{2,1,0:T(1,128)S(1)} %broadcast_in_dim.34.refs_0_, bf16[400,128]{1,0:T(8,128)(2,1)S(1)} %get-tuple-element.37.refs_1_, ...), custom_call_target="tpu_custom_call" | custom-call | flops 2097152000 | bytes 3932160 | tf_op jit(solution)/shard_map/attend/pallas_call | solution.py:115
  90.2 1.4 collective-permute-start.22
  92.4 1.4 collective-permute-start.24
  93.8 6.5 %project.2 = bf16[4,160,1280]{2,1,0:T(8,128)(2,1)S(1)} custom-call(s32[1]{0:T(128)} %bitcast.refs_0_, bf16[400,128]{1,0:T(8,128)(2,1)S(1)} %get-tuple-element.33.refs_1_, bf16[400,128]{1,0:T(8,128)(2,1)S(1)} %collective-permute-done.10.refs_2_, bf16[400,128]{1,0:T(8,128)(2,1)S(1)} %collective-permute-done.11.refs_3_, ...), custom_call_target="tpu_custom_call" | custom-call | flops 2097152000 | bytes 13107200 | tf_op jit(solution)/shard_map/project/pallas_call | solution.py:163
  100.4 3.5 %collective-permute-start.13 = (bf16[160,1280]{1,0:T(8,128)(2,1)S(1)}, bf16[160,1280]{1,0:T(8,128)(2,1)S(1)}, u32[]{:S(2)}, u32[]{:S(2)}) collective-permute-start(bf16[160,1280]{1,0:T(8,128)(2,1)S(1)} %get-tuple-element.47), channel_id=1, source_target_pairs={{0,1},{4,5},{8,9},{12,13},{16,17},{20,21},{24,25},{28,29}} | collective-permute-start | bytes 1228808 | tf_op jit(solution)/shard_map/ppermute | solution.py:193
  104.6 6.5 %project.3 = bf16[4,160,1280]{2,1,0:T(8,128)(2,1)S(1)} custom-call(s32[1]{0:T(128)} %bitcast.refs_0_, bf16[400,128]{1,0:T(8,128)(2,1)S(1)} %get-tuple-element.41.refs_1_, bf16[400,128]{1,0:T(8,128)(2,1)S(1)} %collective-permute-done.22.refs_2_, bf16[400,128]{1,0:T(8,128)(2,1)S(1)} %collective-permute-done.23.refs_3_, ...), custom_call_target="tpu_custom_call" | custom-call | flops 2097152000 | bytes 13107200 | tf_op jit(solution)/shard_map/project/pallas_call | solution.py:163
  114.6 7.8 %collective-permute-done.25 = bf16[160,1280]{1,0:T(8,128)(2,1)S(1)} collective-permute-done((bf16[160,1280]{1,0:T(8,128)(2,1)S(1)}, bf16[160,1280]{1,0:T(8,128)(2,1)S(1)}, u32[]{:S(2)}, u32[]{:S(2)}) %collective-permute-start.25) | collective-permute-done | bytes 409632 | tf_op jit(solution)/shard_map/ppermute | solution.py:193
  122.5 4.4 %collective-permute-start.26 = (bf16[160,1280]{1,0:T(8,128)(2,1)S(1)}, bf16[160,1280]{1,0:T(8,128)(2,1)S(1)}, u32[]{:S(2)}, u32[]{:S(2)}) collective-permute-start(bf16[160,1280]{1,0:T(8,128)(2,1)S(1)} %bitcast_add_fusion.2), channel_id=1, source_target_pairs={{0,1},{1,2},{4,5},{5,6},{8,9},{9,10},{12,13},{13,14},{16,17},{17,1... | collective-permute-start | bytes 1228808 | tf_op jit(solution)/shard_map/ppermute | solution.py:193
  126.9 4.3 %collective-permute-done.14 = bf16[160,1280]{1,0:T(8,128)(2,1)S(1)} collective-permute-done((bf16[160,1280]{1,0:T(8,128)(2,1)S(1)}, bf16[160,1280]{1,0:T(8,128)(2,1)S(1)}, u32[]{:S(2)}, u32[]{:S(2)}) %collective-permute-start.14) | collective-permute-done | bytes 409632 | tf_op jit(solution)/shard_map/ppermute | solution.py:193
  131.3 4.4 %collective-permute-start.15 = (bf16[160,1280]{1,0:T(8,128)(2,1)S(1)}, bf16[160,1280]{1,0:T(8,128)(2,1)S(1)}, u32[]{:S(2)}, u32[]{:S(2)}) collective-permute-start(bf16[160,1280]{1,0:T(8,128)(2,1)S(1)} %get-tuple-element.45), channel_id=1, source_target_pairs={{0,1},{1,2},{2,3},{4,5},{5,6},{6,7},{8,9},{9,10},{10,11},{12,13},{... | collective-permute-start | bytes 1228808 | tf_op jit(solution)/shard_map/ppermute | solution.py:193
  136.5 3.5 %collective-permute-done.26 = bf16[160,1280]{1,0:T(8,128)(2,1)S(1)} collective-permute-done((bf16[160,1280]{1,0:T(8,128)(2,1)S(1)}, bf16[160,1280]{1,0:T(8,128)(2,1)S(1)}, u32[]{:S(2)}, u32[]{:S(2)}) %collective-permute-start.26) | collective-permute-done | bytes 409632 | tf_op jit(solution)/shard_map/ppermute | solution.py:193
  140.1 4.4 %collective-permute-start.27 = (bf16[160,1280]{1,0:T(8,128)(2,1)S(1)}, bf16[160,1280]{1,0:T(8,128)(2,1)S(1)}, u32[]{:S(2)}, u32[]{:S(2)}) collective-permute-start(bf16[160,1280]{1,0:T(8,128)(2,1)S(1)} %get-tuple-element.49), channel_id=1, source_target_pairs={{0,1},{1,2},{2,3},{4,5},{5,6},{6,7},{8,9},{9,10},{10,11},{12,13},{... | collective-permute-start | bytes 1228808 | tf_op jit(solution)/shard_map/ppermute | solution.py:193
  148.8 12.6 %collective-permute-done.18 = bf16[160,1280]{1,0:T(8,128)(2,1)S(1)} collective-permute-done((bf16[160,1280]{1,0:T(8,128)(2,1)S(1)}, bf16[160,1280]{1,0:T(8,128)(2,1)S(1)}, u32[]{:S(2)}, u32[]{:S(2)}) %collective-permute-start.18) | collective-permute-done | bytes 409632 | tf_op jit(solution)/shard_map/ppermute | solution.py:194
  161.5 5.1 %collective-permute-done.30 = bf16[160,1280]{1,0:T(8,128)(2,1)S(1)} collective-permute-done((bf16[160,1280]{1,0:T(8,128)(2,1)S(1)}, bf16[160,1280]{1,0:T(8,128)(2,1)S(1)}, u32[]{:S(2)}, u32[]{:S(2)}) %collective-permute-start.30) | collective-permute-done | bytes 409632 | tf_op jit(solution)/shard_map/ppermute | solution.py:194
  (101 shorter events, 33.1 us)
Async XLA Ops:
  7.3 28.3 %collective-permute-start = (bf16[400,128]{1,0:T(8,128)(2,1)S(1)}, bf16[400,128]{1,0:T(8,128)(2,1)S(1)}, u32[]{:S(2)}, u32[]{:S(2)}) collective-permute-start(bf16[400,128]{1,0:T(8,128)(2,1)S(1)} %get-tuple-element.26), channel_id=1, source_target_pairs={{0,8},{8,0},{16,24},{24,16},{1,9},{9,1},{17,25},{25,17},{2,10},{10... | collective-permute-start | bytes 307208 | tf_op jit(solution)/shard_map/ppermute | solution.py:216
  10.2 14.2 %collective-permute-start.3 = (bf16[1920,128]{1,0:T(8,128)(2,1)S(1)}, bf16[1920,128]{1,0:T(8,128)(2,1)S(1)}, u32[]{:S(2)}, u32[]{:S(2)}) collective-permute-start(bf16[1920,128]{1,0:T(8,128)(2,1)S(1)} %get-tuple-element.30), channel_id=1, source_target_pairs={{0,8},{8,0},{16,24},{24,16},{1,9},{9,1},{17,25},{25,17},{2,10},{10... | collective-permute-start | bytes 1474568 | tf_op jit(solution)/shard_map/ppermute | solution.py:216
  10.3 14.2 %collective-permute-start.4 = (bf16[1920,128]{1,0:T(8,128)(2,1)}, bf16[1920,128]{1,0:T(8,128)(2,1)S(1)}, u32[]{:S(2)}, u32[]{:S(2)}) collective-permute-start(bf16[1920,128]{1,0:T(8,128)(2,1)} %get-tuple-element.31), channel_id=1, source_target_pairs={{0,16},{8,24},{16,0},{24,8},{1,17},{9,25},{17,1},{25,9},{2,18},{10... | collective-permute-start | bytes 1474568 | tf_op jit(solution)/shard_map/ppermute | solution.py:216
  12.3 23.1 %collective-permute-start.5 = (bf16[1920,128]{1,0:T(8,128)(2,1)}, bf16[1920,128]{1,0:T(8,128)(2,1)S(1)}, u32[]{:S(2)}, u32[]{:S(2)}) collective-permute-start(bf16[1920,128]{1,0:T(8,128)(2,1)} %get-tuple-element.32), channel_id=1, source_target_pairs={{0,24},{8,16},{16,8},{24,0},{1,25},{9,17},{17,9},{25,1},{2,26},{10... | collective-permute-start | bytes 1474568 | tf_op jit(solution)/shard_map/ppermute | solution.py:216
  13.7 35.2 %collective-permute-start.6 = (bf16[1920,128]{1,0:T(8,128)(2,1)S(1)}, bf16[1920,128]{1,0:T(8,128)(2,1)S(1)}, u32[]{:S(2)}, u32[]{:S(2)}) collective-permute-start(bf16[1920,128]{1,0:T(8,128)(2,1)S(1)} %get-tuple-element.29.refs_5_), channel_id=1, source_target_pairs={{0,4},{4,0},{1,5},{5,1},{2,6},{6,2},{3,7},{7,3},{8,12},{12,8},{9,1... | collective-permute-start | bytes 1474568 | tf_op jit(solution)/shard_map/ppermute | solution.py:219
  24.4 25.2 %collective-permute-start.7 = (bf16[1920,128]{1,0:T(8,128)(2,1)S(1)}, bf16[1920,128]{1,0:T(8,128)(2,1)S(1)}, u32[]{:S(2)}, u32[]{:S(2)}) collective-permute-start(bf16[1920,128]{1,0:T(8,128)(2,1)S(1)} %collective-permute-done.3.refs_6_), channel_id=1, source_target_pairs={{0,4},{4,0},{1,5},{5,1},{2,6},{6,2},{3,7},{7,3},{8,12},{12,8},{9,1... | collective-permute-start | bytes 1474568 | tf_op jit(solution)/shard_map/ppermute | solution.py:219
  24.4 26.6 %collective-permute-start.8 = (bf16[1920,128]{1,0:T(8,128)(2,1)S(1)}, bf16[1920,128]{1,0:T(8,128)(2,1)}, u32[]{:S(2)}, u32[]{:S(2)}) collective-permute-start(bf16[1920,128]{1,0:T(8,128)(2,1)S(1)} %collective-permute-done.4.refs_7_), channel_id=1, source_target_pairs={{0,4},{4,0},{1,5},{5,1},{2,6},{6,2},{3,7},{7,3},{8,12},{12,8},{9,1... | collective-permute-start | bytes 1474568 | tf_op jit(solution)/shard_map/ppermute | solution.py:219
  35.4 15.6 %collective-permute-start.9 = (bf16[1920,128]{1,0:T(8,128)(2,1)S(1)}, bf16[1920,128]{1,0:T(8,128)(2,1)}, u32[]{:S(2)}, u32[]{:S(2)}) collective-permute-start(bf16[1920,128]{1,0:T(8,128)(2,1)S(1)} %collective-permute-done.5.refs_8_), channel_id=1, source_target_pairs={{0,4},{4,0},{1,5},{5,1},{2,6},{6,2},{3,7},{7,3},{8,12},{12,8},{9,1... | collective-permute-start | bytes 1474568 | tf_op jit(solution)/shard_map/ppermute | solution.py:219
  47.5 25.3 %collective-permute-start.19 = (bf16[400,128]{1,0:T(8,128)(2,1)}, bf16[400,128]{1,0:T(8,128)(2,1)S(1)}, u32[]{:S(2)}, u32[]{:S(2)}) collective-permute-start(bf16[400,128]{1,0:T(8,128)(2,1)} %copy-done.6), channel_id=1, source_target_pairs={{0,8},{8,0},{16,24},{24,16},{1,9},{9,1},{17,25},{25,17},{2,10},{10... | collective-permute-start | bytes 307208 | tf_op jit(solution)/shard_map/ppermute | solution.py:216
  49.0 25.2 %collective-permute-start.20 = (bf16[400,128]{1,0:T(8,128)(2,1)}, bf16[400,128]{1,0:T(8,128)(2,1)S(1)}, u32[]{:S(2)}, u32[]{:S(2)}) collective-permute-start(bf16[400,128]{1,0:T(8,128)(2,1)} %copy-done.5), channel_id=1, source_target_pairs={{0,16},{8,24},{16,0},{24,8},{1,17},{9,25},{17,1},{25,9},{2,18},{10... | collective-permute-start | bytes 307208 | tf_op jit(solution)/shard_map/ppermute | solution.py:216
  49.7 24.5 %collective-permute-start.21 = (bf16[400,128]{1,0:T(8,128)(2,1)}, bf16[400,128]{1,0:T(8,128)(2,1)S(1)}, u32[]{:S(2)}, u32[]{:S(2)}) collective-permute-start(bf16[400,128]{1,0:T(8,128)(2,1)} %copy-done.4), channel_id=1, source_target_pairs={{0,24},{8,16},{16,8},{24,0},{1,25},{9,17},{17,9},{25,1},{2,26},{10... | collective-permute-start | bytes 307208 | tf_op jit(solution)/shard_map/ppermute | solution.py:216
  70.6 21.7 %collective-permute-start.10 = (bf16[400,128]{1,0:T(8,128)(2,1)S(1)}, bf16[400,128]{1,0:T(8,128)(2,1)S(1)}, u32[]{:S(2)}, u32[]{:S(2)}) collective-permute-start(bf16[400,128]{1,0:T(8,128)(2,1)S(1)} %get-tuple-element.34), channel_id=1, source_target_pairs={{0,8},{8,0},{16,24},{24,16},{1,9},{9,1},{17,25},{25,17},{2,10},{10... | collective-permute-start | bytes 307208 | tf_op jit(solution)/shard_map/ppermute | solution.py:216
  72.1 21.7 %collective-permute-start.11 = (bf16[400,128]{1,0:T(8,128)(2,1)S(1)}, bf16[400,128]{1,0:T(8,128)(2,1)S(1)}, u32[]{:S(2)}, u32[]{:S(2)}) collective-permute-start(bf16[400,128]{1,0:T(8,128)(2,1)S(1)} %get-tuple-element.35), channel_id=1, source_target_pairs={{0,16},{8,24},{16,0},{24,8},{1,17},{9,25},{17,1},{25,9},{2,18},{10... | collective-permute-start | bytes 307208 | tf_op jit(solution)/shard_map/ppermute | solution.py:216
  72.8 21.0 %collective-permute-start.12 = (bf16[400,128]{1,0:T(8,128)(2,1)S(1)}, bf16[400,128]{1,0:T(8,128)(2,1)S(1)}, u32[]{:S(2)}, u32[]{:S(2)}) collective-permute-start(bf16[400,128]{1,0:T(8,128)(2,1)S(1)} %get-tuple-element.36), channel_id=1, source_target_pairs={{0,24},{8,16},{16,8},{24,0},{1,25},{9,17},{17,9},{25,1},{2,26},{10... | collective-permute-start | bytes 307208 | tf_op jit(solution)/shard_map/ppermute | solution.py:216
  90.2 14.4 %collective-permute-start.22 = (bf16[400,128]{1,0:T(8,128)(2,1)S(1)}, bf16[400,128]{1,0:T(8,128)(2,1)S(1)}, u32[]{:S(2)}, u32[]{:S(2)}) collective-permute-start(bf16[400,128]{1,0:T(8,128)(2,1)S(1)} %get-tuple-element.42), channel_id=1, source_target_pairs={{0,8},{8,0},{16,24},{24,16},{1,9},{9,1},{17,25},{25,17},{2,10},{10... | collective-permute-start | bytes 307208 | tf_op jit(solution)/shard_map/ppermute | solution.py:216
  91.6 12.9 %collective-permute-start.23 = (bf16[400,128]{1,0:T(8,128)(2,1)S(1)}, bf16[400,128]{1,0:T(8,128)(2,1)S(1)}, u32[]{:S(2)}, u32[]{:S(2)}) collective-permute-start(bf16[400,128]{1,0:T(8,128)(2,1)S(1)} %get-tuple-element.43), channel_id=1, source_target_pairs={{0,16},{8,24},{16,0},{24,8},{1,17},{9,25},{17,1},{25,9},{2,18},{10... | collective-permute-start | bytes 307208 | tf_op jit(solution)/shard_map/ppermute | solution.py:216
  103.9 23.0 %collective-permute-start.16 = (bf16[160,1280]{1,0:T(8,128)(2,1)S(1)}, bf16[160,1280]{1,0:T(8,128)(2,1)S(1)}, u32[]{:S(2)}, u32[]{:S(2)}) collective-permute-start(bf16[160,1280]{1,0:T(8,128)(2,1)S(1)} %get-tuple-element.48), channel_id=1, source_target_pairs={{3,2},{7,6},{11,10},{15,14},{19,18},{23,22},{27,26},{31,30}} | collective-permute-start | bytes 1228808 | tf_op jit(solution)/shard_map/ppermute | solution.py:194
  112.6 23.9 %collective-permute-start.28 = (bf16[160,1280]{1,0:T(8,128)(2,1)S(1)}, bf16[160,1280]{1,0:T(8,128)(2,1)S(1)}, u32[]{:S(2)}, u32[]{:S(2)}) collective-permute-start(bf16[160,1280]{1,0:T(8,128)(2,1)S(1)} %get-tuple-element.52), channel_id=1, source_target_pairs={{3,2},{7,6},{11,10},{15,14},{19,18},{23,22},{27,26},{31,30}} | collective-permute-start | bytes 1228808 | tf_op jit(solution)/shard_map/ppermute | solution.py:194
  113.3 17.9 %collective-permute-start.14 = (bf16[160,1280]{1,0:T(8,128)(2,1)S(1)}, bf16[160,1280]{1,0:T(8,128)(2,1)S(1)}, u32[]{:S(2)}, u32[]{:S(2)}) collective-permute-start(bf16[160,1280]{1,0:T(8,128)(2,1)S(1)} %bitcast_add_fusion.7), channel_id=1, source_target_pairs={{0,1},{1,2},{4,5},{5,6},{8,9},{9,10},{12,13},{13,14},{16,17},{17,1... | collective-permute-start | bytes 1228808 | tf_op jit(solution)/shard_map/ppermute | solution.py:193
  122.5 17.5 %collective-permute-start.26 = (bf16[160,1280]{1,0:T(8,128)(2,1)S(1)}, bf16[160,1280]{1,0:T(8,128)(2,1)S(1)}, u32[]{:S(2)}, u32[]{:S(2)}) collective-permute-start(bf16[160,1280]{1,0:T(8,128)(2,1)S(1)} %bitcast_add_fusion.2), channel_id=1, source_target_pairs={{0,1},{1,2},{4,5},{5,6},{8,9},{9,10},{12,13},{13,14},{16,17},{17,1... | collective-permute-start | bytes 1228808 | tf_op jit(solution)/shard_map/ppermute | solution.py:193
  131.3 17.4 %collective-permute-start.15 = (bf16[160,1280]{1,0:T(8,128)(2,1)S(1)}, bf16[160,1280]{1,0:T(8,128)(2,1)S(1)}, u32[]{:S(2)}, u32[]{:S(2)}) collective-permute-start(bf16[160,1280]{1,0:T(8,128)(2,1)S(1)} %get-tuple-element.45), channel_id=1, source_target_pairs={{0,1},{1,2},{2,3},{4,5},{5,6},{6,7},{8,9},{9,10},{10,11},{12,13},{... | collective-permute-start | bytes 1228808 | tf_op jit(solution)/shard_map/ppermute | solution.py:193
  140.1 21.4 %collective-permute-start.27 = (bf16[160,1280]{1,0:T(8,128)(2,1)S(1)}, bf16[160,1280]{1,0:T(8,128)(2,1)S(1)}, u32[]{:S(2)}, u32[]{:S(2)}) collective-permute-start(bf16[160,1280]{1,0:T(8,128)(2,1)S(1)} %get-tuple-element.49), channel_id=1, source_target_pairs={{0,1},{1,2},{2,3},{4,5},{5,6},{6,7},{8,9},{9,10},{10,11},{12,13},{... | collective-permute-start | bytes 1228808 | tf_op jit(solution)/shard_map/ppermute | solution.py:193
  145.3 16.2 %collective-permute-start.18 = (bf16[160,1280]{1,0:T(8,128)(2,1)S(1)}, bf16[160,1280]{1,0:T(8,128)(2,1)S(1)}, u32[]{:S(2)}, u32[]{:S(2)}) collective-permute-start(bf16[160,1280]{1,0:T(8,128)(2,1)S(1)} %bitcast_add_fusion.6), channel_id=1, source_target_pairs={{3,2},{2,1},{1,0},{7,6},{6,5},{5,4},{11,10},{10,9},{9,8},{15,14},{... | collective-permute-start | bytes 1228808 | tf_op jit(solution)/shard_map/ppermute | solution.py:194
  146.6 20.0 %collective-permute-start.30 = (bf16[160,1280]{1,0:T(8,128)(2,1)S(1)}, bf16[160,1280]{1,0:T(8,128)(2,1)S(1)}, u32[]{:S(2)}, u32[]{:S(2)}) collective-permute-start(bf16[160,1280]{1,0:T(8,128)(2,1)S(1)} %bitcast_add_fusion.1), channel_id=1, source_target_pairs={{3,2},{2,1},{1,0},{7,6},{6,5},{5,4},{11,10},{10,9},{9,8},{15,14},{... | collective-permute-start | bytes 1228808 | tf_op jit(solution)/shard_map/ppermute | solution.py:194
  (20 other events, 91.9 us)

commit v2 on v0

--- a/solution.py
+++ b/solution.py
@@ -3,13 +3,271 @@
 import jax
 import jax.numpy as jnp
 from jax import lax
+from jax.experimental import pallas as pl
+from jax.experimental.pallas import tpu as pltpu
 from jax.sharding import PartitionSpec as P
 
 HD = 128
 HALO = 4
-
-
 NEG_FILL = -1e30
+CHUNKS = 2
+VMEM = pltpu.CompilerParams(vmem_limit_bytes=32 * 1024 * 1024)
+
+
+def pack_kernel(t_ref, q_ref, k_ref, v_ref, first, *rest, partner, partners, full, share, row):
+    sems = rest[-1]
+    tokens = q_ref.shape[0]
+    part = tokens // CHUNKS
+    chip = t_ref[0] ^ partner
+    heads = [chip * full + i for i in range(full)] + [partners * full + chip // share]
+    lanes = [pl.ds(pl.multiple_of(h * HD, HD), HD) for h in heads]
+    moves = []
+    for kind, source in enumerate((k_ref, v_ref)):
+        for i, lane in enumerate(lanes):
+            place = pl.ds((kind * (full + 1) + i) * tokens, tokens)
+            moves.append((source.at[:, lane], first.at[place]))
+    for c in range(CHUNKS):
+        target, base = (first, 2 * (full + 1) * tokens) if c == 0 else (rest[c - 1], 0)
+        for i in range(full):
+            moves.append((q_ref.at[pl.ds(c * part, part), lanes[i]], target.at[pl.ds(base + i * part, part)]))
+        start = pl.multiple_of(c * part + (chip % share) * row, 16)
+        moves.append((q_ref.at[pl.ds(start, row), lanes[full]], target.at[pl.ds(base + full * part, row)]))
+    copies = [pltpu.make_async_copy(a, b, sems.at[n]) for n, (a, b) in enumerate(moves)]
+    for copy in copies:
+        copy.start()
+    for copy in copies:
+        copy.wait()
+
+
+def pack(t, q, k, v, partner, partners, full, share, row):
+    tokens = q.shape[0]
+    queries = full * (tokens // CHUNKS) + row
+    slabs = 2 * (full + 1) * tokens + queries
+    whole = pl.BlockSpec(memory_space=pltpu.VMEM)
+    anywhere = pl.BlockSpec(memory_space=pl.ANY)
+    shapes = [jax.ShapeDtypeStruct((slabs, HD), q.dtype)]
+    shapes += [jax.ShapeDtypeStruct((queries, HD), q.dtype)] * (CHUNKS - 1)
+
+    def kernel(*refs):
+        pack_kernel(*refs, partner=partner, partners=partners, full=full, share=share, row=row)
+
+    return pl.pallas_call(
+        kernel,
+        out_shape=shapes,
+        in_specs=[pl.BlockSpec(memory_space=pltpu.SMEM), anywhere, anywhere, anywhere],
+        out_specs=[whole] * len(shapes),
+        scratch_shapes=[pltpu.SemaphoreType.DMA(((full + 1) * (2 + CHUNKS),))],
+        compiler_params=VMEM,
+        name="pack",
+    )(t, q, k, v)
+
+
+def attend_kernel(
+    place_ref, window_ref, *refs, chunk, partners, full, share, row, rows_dev, total_rows, asked
+):
+    queries = refs[:partners]
+    near = refs[partners : 2 * partners]
+    far = refs[2 * partners : 3 * partners]
+    outs = refs[3 * partners :]
+    slots = full + 1
+    tokens = rows_dev * row
+    count = 2 * partners * tokens
+    t, s = place_ref[0], place_ref[1]
+    rows_part = rows_dev // CHUNKS
+    factor = math.log2(math.e) / math.sqrt(HD)
+
+    at = lax.broadcasted_iota(jnp.int32, (1, count), 1)
+    frame = at // (2 * tokens)
+    side = (at // tokens) % 2
+    key_row = (at % tokens) // row + rows_dev * jnp.where(side == 0, s, 1 - s)
+    widths = []
+    for m in range(partners):
+        wide = jnp.zeros_like(at)
+        for m2 in range(partners):
+            wide = jnp.where(frame == m2, window_ref[t ^ m, t ^ m2], wide)
+        widths.append(wide)
+
+    def bias(unit, m):
+        part_row = unit % rows_part if unit < full * rows_part else t % share
+        distance = jnp.abs(key_row - (rows_dev * s + rows_part * chunk + part_row))
+        return jnp.where(distance <= widths[m], 0.0, NEG_FILL).astype(jnp.float32)
+
+    def block(kind, slot):
+        base = (kind * slots + slot) * tokens
+        return jnp.concatenate([r[pl.ds(base, tokens)] for m in range(partners) for r in (near[m], far[m])], axis=0)
+
+    def score(tile):
+        unit, pair = tile
+        q = jnp.concatenate([queries[m][pl.ds(asked + unit * row, row)] for m in pair], axis=0)
+        return lax.dot_general(
+            q, block(0, unit // rows_part), (((1,), (1,)), ((), ())), preferred_element_type=jnp.float32
+        )
+
+    def weigh(tile, scores):
+        unit, pair = tile
+        scores = jnp.concatenate(
+            [scores[i * row : (i + 1) * row] + bias(unit, m) for i, m in enumerate(pair)], axis=0
+        )
+        top = jnp.max(scores, axis=-1, keepdims=True)
+        return jnp.exp2((scores - top) * factor).astype(jnp.bfloat16)
+
+    def gather(tile, weights):
+        unit, pair = tile
+        held = block(1, unit // rows_part)
+        held = jnp.concatenate([held, jnp.ones_like(held)], axis=1)
+        summed = jnp.dot(weights, held, preferred_element_type=jnp.float32)
+        out = (summed[:, :HD] / summed[:, HD:]).astype(jnp.bfloat16)
+        for i, m in enumerate(pair):
+            outs[m][pl.ds(unit * row, row)] = out[i * row : (i + 1) * row]
+
+    pairs = [tuple(range(m, m + 2)) for m in range(0, partners, 2)]
+    tiles = [(unit, pair) for unit in range(full * rows_part + 1) for pair in pairs]
+    scores, last = score(tiles[0]), None
+    for i, tile in enumerate(tiles):
+        following = score(tiles[i + 1]) if i + 1 < len(tiles) else None
+        if last is not None:
+            gather(*last)
+        last = (tile, weigh(tile, scores))
+        scores = following
+    gather(*last)
+
+
+def attend(place, window, queries, near, far, chunk, full, share, row, rows_dev):
+    partners = len(queries)
+    rows_out = full * (rows_dev // CHUNKS) * row + row
+    count = 2 * partners * rows_dev * row
+    whole = pl.BlockSpec(memory_space=pltpu.VMEM)
+    scalars = pl.BlockSpec(memory_space=pltpu.SMEM)
+
+    def kernel(*refs):
+        attend_kernel(
+            *refs,
+            chunk=chunk,
+            partners=partners,
+            full=full,
+            share=share,
+            row=row,
+            rows_dev=rows_dev,
+            total_rows=2 * rows_dev,
+            asked=queries[0].shape[0] - rows_out,
+        )
+
+    work = partners * rows_out * count
+    return pl.pallas_call(
+        kernel,
+        out_shape=[jax.ShapeDtypeStruct((rows_out, HD), jnp.bfloat16)] * partners,
+        in_specs=[scalars, scalars] + [whole] * (3 * partners),
+        out_specs=[whole] * partners,
+        compiler_params=VMEM,
+        cost_estimate=pl.CostEstimate(
+            flops=work * HD * 4, bytes_accessed=count * HD * 4 * (full + 1), transcendentals=work
+        ),
+        name="attend",
+    )(place, window, *queries, *near, *far)
+
+
+def project_kernel(t_ref, *refs, partners, full, share, row):
+    parts = refs[:partners]
+    weight, out, mixed = refs[partners:]
+    part = mixed.shape[0]
+    for m in range(partners):
+        chip = t_ref[0] ^ m
+        for i in range(full):
+            lane = pl.ds(pl.multiple_of((chip * full + i) * HD, HD), HD)
+            mixed[:, lane] = parts[m][pl.ds(i * part, part)]
+        lane = pl.ds(pl.multiple_of((partners * full + chip // share) * HD, HD), HD)
+        rows = pl.ds(pl.multiple_of((chip % share) * row, 16), row)
+        mixed[rows, lane] = parts[m][pl.ds(full * part, row)]
+    shares, _, block = out.shape
+    for d in range(shares):
+        product = jnp.dot(mixed[...], weight[:, d * block : (d + 1) * block], preferred_element_type=jnp.float32)
+        out[d] = product.astype(out.dtype)
+
+
+def project(t, parts, weight, shares, full, share, row):
+    partners = len(parts)
+    feats, width = weight.shape
+    part = (parts[0].shape[0] - row) // full
+    block = width // shares
+    whole = pl.BlockSpec(memory_space=pltpu.VMEM)
+
+    def kernel(*refs):
+        project_kernel(*refs, partners=partners, full=full, share=share, row=row)
+
+    return pl.pallas_call(
+        kernel,
+        out_shape=jax.ShapeDtypeStruct((shares, part, block), jnp.bfloat16),
+        in_specs=[pl.BlockSpec(memory_space=pltpu.SMEM)] + [whole] * (partners + 1),
+        out_specs=whole,
+        scratch_shapes=[pltpu.VMEM((part, feats), jnp.bfloat16)],
+        compiler_params=VMEM,
+        cost_estimate=pl.CostEstimate(
+            flops=2 * part * feats * width, bytes_accessed=2 * feats * width, transcendentals=0
+        ),
+        name="project",
+    )(t, *parts, weight)
+
+
+def scatter_sums(chunks, axis):
+    size = lax.axis_size(axis)
+    place = lax.axis_index(axis)
+
+    def share(mixed, d):
+        return lax.dynamic_index_in_dim(mixed, jnp.clip(d, 0, size - 1), 0, False)
+
+    held = [None] * len(chunks)
+    for step in range(1, size):
+        for c, mixed in enumerate(chunks):
+            right = share(mixed, place + size - step)
+            left = share(mixed, place - size + step)
+            if held[c] is not None:
+                right, left = right + held[c][0], left + held[c][1]
+            right, left = lax.optimization_barrier((right, left))
+            held[c] = (
+                lax.ppermute(right, axis, [(i, i + 1) for i in range(step)]),
+                lax.ppermute(left, axis, [(size - 1 - i, size - 2 - i) for i in range(step)]),
+            )
+    return [share(mixed, place) + right + left for mixed, (right, left) in zip(chunks, held)]
+
+
+def exchange_plan(query, key, value, window, out_weight):
+    frames_dev, rows_dev, width, feats = query.shape
+    partners = lax.axis_size("tm")
+    heads = feats // HD
+    full = heads // partners
+    share = partners // (heads - full * partners)
+    t = lax.axis_index("tm").astype(jnp.int32)
+    s = lax.axis_index("space").astype(jnp.int32)
+    place = jnp.stack([t, s])
+    tokens = rows_dev * width
+    flat = [a.reshape(tokens, feats) for a in (query, key, value)]
+
+    def swap(x, m):
+        return x if m == 0 else lax.ppermute(x, "tm", [(i, i ^ m) for i in range(partners)])
+
+    packed = [pack(place, *flat, m, partners, full, share, width) for m in range(partners)]
+    near = [swap(p[0], m) for m, p in enumerate(packed)]
+    far = [lax.ppermute(x, "space", [(0, 1), (1, 0)]) for x in near]
+
+    mixed = []
+    for c in range(CHUNKS):
+        queries = near if c == 0 else [swap(p[c], m) for m, p in enumerate(packed)]
+        done = attend(place, window, queries, near, far, c, full, share, width, rows_dev)
+        done = [swap(x, m) for m, x in enumerate(done)]
+        mixed.append(project(place, done, out_weight, lax.axis_size("head"), full, share, width))
+    outputs = scatter_sums(mixed, "head")
+    return jnp.concatenate(outputs, axis=0).reshape(frames_dev, rows_dev, width, -1)
+
+
+def can_exchange(mesh, query, key, value, window, out_weight):
+    partners, sides = mesh.shape["tm"], mesh.shape["space"]
+    frames, rows, width, feats = query.shape
+    heads = feats // HD // mesh.shape["head"]
+    rows_dev = rows // sides
+    rest = heads % partners
+    if partners & (partners - 1) or sides != 2 or frames != partners or rest == 0 or heads < partners:
+        return False
+    return partners % rest == 0 and rows_dev == CHUNKS * (partners // rest) and width % 16 == 0
 
 
 def padded_2(x, sides, width):
@@ -72,7 +330,7 @@
     )
 
 
-def body(query, key, value, window, out_weight):
+def gather_plan(query, key, value, window, out_weight):
     frames_dev, rows_dev, width, feats = query.shape
     heads_dev = feats // HD
     qcount = frames_dev * rows_dev * width
@@ -125,6 +383,11 @@
         P(),
         P("head", None),
     )
-    return jax.shard_map(
-        body, mesh=mesh, in_specs=placed, out_specs=P("tm", "space", None, "head"), check_vma=False
-    )
+
+    def run(*args):
+        body = exchange_plan if can_exchange(mesh, *args) else gather_plan
+        return jax.shard_map(
+            body, mesh=mesh, in_specs=placed, out_specs=P("tm", "space", None, "head"), check_vma=False
+        )(*args)
+
+    return run

time: 484 us -> 119 us (0.25)
  waiting for transfers between devices: 248 us -> 45.5 us
  matrix products: 94.2 us -> 0 us
  local copies, waits for them, and re-layouts: 66.9 us -> 3.57 us
  other arithmetic: 49.6 us -> 1.53 us
  starting transfers between devices: 3.8 us -> 44.2 us
  Pallas kernels: 0 us -> 23.2 us
  between operations: 13.5 us -> 0.27 us
  loops' own time: 7.59 us -> 0 us
    all_gather x1 -> x0, waiting for transfers between devices: 181 us -> none  [body(): piece = lax.all_gather(padded, 'tm', axis=1, tiled=True)]
    dot_general x9 -> x0, matrix products: 94.2 us -> none  [the longest x4 41.8 us: absorb(): jnp.einsum('qhd,khd->hqk', queries, keys, preferred_element_type=jnp.floa...]
    reduce_scatter x1 -> x0, waiting for transfers between devices: 62.4 us -> none  [body(): lax.psum_scatter(lax.dot_general(out_weight, attended, (((0,), (1,)), (()...]
    ppermute x2 -> x28, waiting for transfers between devices: 4.1 us -> 45.5 us  [the longest x12 23.2 us: swap(): lax.ppermute(x, 'tm', [(i, i ^ m) for i in range(partners)])]
    ppermute x2 -> x28, starting transfers between devices: 3.75 us -> 44.2 us  [the longest x6 23.3 us: scatter_sums(): lax.ppermute(right, axis, [(i, i + 1) for i in range(step)])]
    squeeze x8 -> x2, local copies, waits for them, and re-layouts: 37.5 us -> 0.13 us  [share(): return lax.dynamic_index_in_dim(mixed, jnp.clip(d, 0, size - 1), 0, False)]
    reduce_sum x4 -> x0, other arithmetic: 34.5 us -> none  [absorb(): new_sum = run_sum * factor + jnp.sum(weights, axis=-1)]
    pallas_call x0 -> x8, Pallas kernels: none -> 23.2 us  [the longest x2 14 us: attend(): pl.pallas_call(kernel, out_shape=[jax.ShapeDtypeStruct((rows_out, HD), jn...]
  transfers between devices with their start and end apart: 4 -> 28, of which waited for: 4 -> 11; matrix products, arithmetic and copies ran while one was open for 0% -> 0% of each run, Pallas kernels for 0% -> 19%
where the time goes in v2:
time: 119 us; the launch traced here: 118 us
  waiting for transfers between devices  45.5 us (38%)
  starting transfers between devices  44.2 us (37%)
  Pallas kernels  23.2 us (19%)
  local copies, waits for them, and re-layouts  3.57 us (3%)
  other arithmetic  1.53 us (1%)
    ppermute x6, starting transfers between devices, scatter_sums(): lax.ppermute(right, axis, [(i, i + 1) for i in range(step)])  23.3 us
    ppermute x12, waiting for transfers between devices, swap(): lax.ppermute(x, 'tm', [(i, i ^ m) for i in range(partners)])  23.2 us
    ppermute x6, waiting for transfers between devices, scatter_sums(): lax.ppermute(right, axis, [(i, i + 1) for i in range(step)])  21.1 us
    ppermute x12, starting transfers between devices, swap(): lax.ppermute(x, 'tm', [(i, i ^ m) for i in range(partners)])  15.3 us
    pallas_call x2, Pallas kernels, attend(): pl.pallas_call(kernel, out_shape=[jax.ShapeDtypeStruct((rows_out, HD), jn...  14 us
    pallas_call x2, Pallas kernels, project(): pl.pallas_call(kernel, out_shape=jax.ShapeDtypeStruct((shares, part, bloc...  6 us
    ppermute x6, starting transfers between devices, scatter_sums(): lax.ppermute(left, axis, [(size - 1 - i, size - 2 - i) for i in range(ste...  5.33 us
    unnamed x10, local copies, waits for them, and re-layouts  3.45 us
  transfers between devices with their start and end apart: 28, of which 11 were waited for; matrix products, arithmetic and copies ran while one was open for 0% of the time, Pallas kernels for 19%

profile of v2, /device:TPU:0, one launch (start us, length us, event | category | flops | bytes accessed | tf_op | source)
XLA Modules:
  0.0 118.3 jit_solution(4734460699483169245)
XLA Ops:
  4.3 4.0 %collective-permute-start.2 = (bf16[2320,128]{1,0:T(8,128)(2,1)S(1)}, bf16[2320,128]{1,0:T(8,128)(2,1)S(1)}, u32[]{:S(2)}, u32[]{:S(2)}) collective-permute-start(bf16[2320,128]{1,0:T(8,128)(2,1)S(1)} %get-tuple-element.36), channel_id=1, source_target_pairs={{0,24},{8,16},{16,8},{24,0},{1,25},{9,17},{17,9},{25,1},{2,26},{10... | collective-permute-start | bytes 1781768 | tf_op jit(solution)/shard_map/ppermute | solution.py:246
  11.6 11.0 %collective-permute-done.2.refs_5_.refs_9_ = bf16[2320,128]{1,0:T(8,128)(2,1)S(1)} collective-permute-done((bf16[2320,128]{1,0:T(8,128)(2,1)S(1)}, bf16[2320,128]{1,0:T(8,128)(2,1)S(1)}, u32[]{:S(2)}, u32[]{:S(2)}) %collective-permute-start.2) | collective-permute-done | bytes 593952 | tf_op jit(solution)/shard_map/ppermute | solution.py:246
  22.6 11.9 %collective-permute-done.1.refs_4_.refs_8_ = bf16[2320,128]{1,0:T(8,128)(2,1)S(1)} collective-permute-done((bf16[2320,128]{1,0:T(8,128)(2,1)S(1)}, bf16[2320,128]{1,0:T(8,128)(2,1)S(1)}, u32[]{:S(2)}, u32[]{:S(2)}) %collective-permute-start.1) | collective-permute-done | bytes 593952 | tf_op jit(solution)/shard_map/ppermute | solution.py:246
  34.9 2.6 %collective-permute-start.18 = (bf16[400,128]{1,0:T(8,128)(2,1)S(1)}, bf16[400,128]{1,0:T(8,128)(2,1)S(1)}, u32[]{:S(2)}, u32[]{:S(2)}) collective-permute-start(bf16[400,128]{1,0:T(8,128)(2,1)S(1)} %get-tuple-element.50), channel_id=1, source_target_pairs={{0,24},{8,16},{16,8},{24,0},{1,25},{9,17},{17,9},{25,1},{2,26},{10... | collective-permute-start | bytes 307208 | tf_op jit(solution)/shard_map/ppermute | solution.py:246
  38.5 7.0 %attend.2 = (bf16[400,128]{1,0:T(8,128)(2,1)S(1)}, bf16[400,128]{1,0:T(8,128)(2,1)S(1)}, bf16[400,128]{1,0:T(8,128)(2,1)S(1)}, bf16[400,128]{1,0:T(8,128)(2,1)S(1)}) custom-call(s32[2]{0:T(128)S(1)} %pad_add_fusion.refs_0_, s32[4,4]{1,0:T(4,128)S(1)} %copy-done.4, bf16[2320,128]{1,0:T(8,128)(2,1)S(1)} %get-tuple-element.33.refs_2_.refs_6_, ...), custom_call_target="tpu_custom_call" | custom-call | flops 2097152000 | bytes 3932160 | tf_op jit(solution)/shard_map/attend/pallas_call | solution.py:156
  45.4 1.7 %collective-permute-start.7 = (bf16[400,128]{1,0:T(8,128)(2,1)S(1)}, bf16[400,128]{1,0:T(8,128)(2,1)S(1)}, u32[]{:S(2)}, u32[]{:S(2)}) collective-permute-start(bf16[400,128]{1,0:T(8,128)(2,1)S(1)} %get-tuple-element.38), channel_id=1, source_target_pairs={{0,8},{8,0},{16,24},{24,16},{1,9},{9,1},{17,25},{25,17},{2,10},{10... | collective-permute-start | bytes 307208 | tf_op jit(solution)/shard_map/ppermute | solution.py:246
  47.2 1.5 %collective-permute-start.8 = (bf16[400,128]{1,0:T(8,128)(2,1)S(1)}, bf16[400,128]{1,0:T(8,128)(2,1)S(1)}, u32[]{:S(2)}, u32[]{:S(2)}) collective-permute-start(bf16[400,128]{1,0:T(8,128)(2,1)S(1)} %get-tuple-element.39), channel_id=1, source_target_pairs={{0,16},{8,24},{16,0},{24,8},{1,17},{9,25},{17,1},{25,9},{2,18},{10... | collective-permute-start | bytes 307208 | tf_op jit(solution)/shard_map/ppermute | solution.py:246
  49.0 7.0 %attend.3 = (bf16[400,128]{1,0:T(8,128)(2,1)S(1)}, bf16[400,128]{1,0:T(8,128)(2,1)S(1)}, bf16[400,128]{1,0:T(8,128)(2,1)S(1)}, bf16[400,128]{1,0:T(8,128)(2,1)S(1)}) custom-call(s32[2]{0:T(128)S(1)} %pad_add_fusion.refs_0_, s32[4,4]{1,0:T(4,128)S(1)} %copy-done.4, bf16[400,128]{1,0:T(8,128)(2,1)S(1)} %get-tuple-element.47.refs_2_, ...), custom_call_target="tpu_custom_call" | custom-call | flops 2097152000 | bytes 3932160 | tf_op jit(solution)/shard_map/attend/pallas_call | solution.py:156
  56.0 1.7 %collective-permute-start.19 = (bf16[400,128]{1,0:T(8,128)(2,1)S(1)}, bf16[400,128]{1,0:T(8,128)(2,1)S(1)}, u32[]{:S(2)}, u32[]{:S(2)}) collective-permute-start(bf16[400,128]{1,0:T(8,128)(2,1)S(1)} %get-tuple-element.52), channel_id=1, source_target_pairs={{0,8},{8,0},{16,24},{24,16},{1,9},{9,1},{17,25},{25,17},{2,10},{10... | collective-permute-start | bytes 307208 | tf_op jit(solution)/shard_map/ppermute | solution.py:246
  57.8 1.5 %collective-permute-start.20 = (bf16[400,128]{1,0:T(8,128)(2,1)S(1)}, bf16[400,128]{1,0:T(8,128)(2,1)S(1)}, u32[]{:S(2)}, u32[]{:S(2)}) collective-permute-start(bf16[400,128]{1,0:T(8,128)(2,1)S(1)} %get-tuple-element.53), channel_id=1, source_target_pairs={{0,16},{8,24},{16,0},{24,8},{1,17},{9,25},{17,1},{25,9},{2,18},{10... | collective-permute-start | bytes 307208 | tf_op jit(solution)/shard_map/ppermute | solution.py:246
  59.6 3.0 %project.2 = bf16[4,160,1280]{2,1,0:T(8,128)(2,1)S(1)} custom-call(s32[2]{0:T(128)S(1)} %pad_add_fusion.refs_0_, bf16[400,128]{1,0:T(8,128)(2,1)S(1)} %get-tuple-element.37.refs_1_, bf16[400,128]{1,0:T(8,128)(2,1)S(1)} %collective-permute-done.7.refs_2_, bf16[400,128]{1,0:T(8,128)(2,1)S(1)} %collective-permute-done.8.refs_3_, ...), custom_call_target="tpu_custom_call" | custom-call | flops 2097152000 | bytes 13107200 | tf_op jit(solution)/shard_map/project/pallas_call | solution.py:197
  62.7 3.7 %collective-permute-start.10 = (bf16[160,1280]{1,0:T(8,128)(2,1)S(1)}, bf16[160,1280]{1,0:T(8,128)(2,1)S(1)}, u32[]{:S(2)}, u32[]{:S(2)}) collective-permute-start(bf16[160,1280]{1,0:T(8,128)(2,1)S(1)} %get-tuple-element.41), channel_id=1, source_target_pairs={{0,1},{4,5},{8,9},{12,13},{16,17},{20,21},{24,25},{28,29}} | collective-permute-start | bytes 1228808 | tf_op jit(solution)/shard_map/ppermute | solution.py:227
  67.1 3.0 %project.3 = bf16[4,160,1280]{2,1,0:T(8,128)(2,1)S(1)} custom-call(s32[2]{0:T(128)S(1)} %pad_add_fusion.refs_0_, bf16[400,128]{1,0:T(8,128)(2,1)S(1)} %get-tuple-element.51.refs_1_, bf16[400,128]{1,0:T(8,128)(2,1)S(1)} %collective-permute-done.19.refs_2_, bf16[400,128]{1,0:T(8,128)(2,1)S(1)} %collective-permute-done.20.refs_3_, ...), custom_call_target="tpu_custom_call" | custom-call | flops 2097152000 | bytes 13107200 | tf_op jit(solution)/shard_map/project/pallas_call | solution.py:197
  70.1 1.3 %collective-permute-start.22 = (bf16[160,1280]{1,0:T(8,128)(2,1)S(1)}, bf16[160,1280]{1,0:T(8,128)(2,1)S(1)}, u32[]{:S(2)}, u32[]{:S(2)}) collective-permute-start(bf16[160,1280]{1,0:T(8,128)(2,1)S(1)} %get-tuple-element.55), channel_id=1, source_target_pairs={{0,1},{4,5},{8,9},{12,13},{16,17},{20,21},{24,25},{28,29}} | collective-permute-start | bytes 1228808 | tf_op jit(solution)/shard_map/ppermute | solution.py:227
  72.2 4.1 %collective-permute-done.10 = bf16[160,1280]{1,0:T(8,128)(2,1)S(1)} collective-permute-done((bf16[160,1280]{1,0:T(8,128)(2,1)S(1)}, bf16[160,1280]{1,0:T(8,128)(2,1)S(1)}, u32[]{:S(2)}, u32[]{:S(2)}) %collective-permute-start.10) | collective-permute-done | bytes 409632 | tf_op jit(solution)/shard_map/ppermute | solution.py:227
  76.3 4.4 %collective-permute-start.12 = (bf16[160,1280]{1,0:T(8,128)(2,1)S(1)}, bf16[160,1280]{1,0:T(8,128)(2,1)S(1)}, u32[]{:S(2)}, u32[]{:S(2)}) collective-permute-start(bf16[160,1280]{1,0:T(8,128)(2,1)S(1)} %get-tuple-element.43), channel_id=1, source_target_pairs={{0,1},{1,2},{4,5},{5,6},{8,9},{9,10},{12,13},{13,14},{16,17},{17,1... | collective-permute-start | bytes 1228808 | tf_op jit(solution)/shard_map/ppermute | solution.py:227
  81.4 3.6 %collective-permute-done.22 = bf16[160,1280]{1,0:T(8,128)(2,1)S(1)} collective-permute-done((bf16[160,1280]{1,0:T(8,128)(2,1)S(1)}, bf16[160,1280]{1,0:T(8,128)(2,1)S(1)}, u32[]{:S(2)}, u32[]{:S(2)}) %collective-permute-start.22) | collective-permute-done | bytes 409632 | tf_op jit(solution)/shard_map/ppermute | solution.py:227
  85.1 4.4 %collective-permute-start.24 = (bf16[160,1280]{1,0:T(8,128)(2,1)S(1)}, bf16[160,1280]{1,0:T(8,128)(2,1)S(1)}, u32[]{:S(2)}, u32[]{:S(2)}) collective-permute-start(bf16[160,1280]{1,0:T(8,128)(2,1)S(1)} %get-tuple-element.57), channel_id=1, source_target_pairs={{0,1},{1,2},{4,5},{5,6},{8,9},{9,10},{12,13},{13,14},{16,17},{17,1... | collective-permute-start | bytes 1228808 | tf_op jit(solution)/shard_map/ppermute | solution.py:227
  90.2 3.6 %collective-permute-done.12 = bf16[160,1280]{1,0:T(8,128)(2,1)S(1)} collective-permute-done((bf16[160,1280]{1,0:T(8,128)(2,1)S(1)}, bf16[160,1280]{1,0:T(8,128)(2,1)S(1)}, u32[]{:S(2)}, u32[]{:S(2)}) %collective-permute-start.12) | collective-permute-done | bytes 409632 | tf_op jit(solution)/shard_map/ppermute | solution.py:227
  93.9 4.7 %collective-permute-start.14 = (bf16[160,1280]{1,0:T(8,128)(2,1)S(1)}, bf16[160,1280]{1,0:T(8,128)(2,1)S(1)}, u32[]{:S(2)}, u32[]{:S(2)}) collective-permute-start(bf16[160,1280]{1,0:T(8,128)(2,1)S(1)} %get-tuple-element.45), channel_id=1, source_target_pairs={{0,1},{1,2},{2,3},{4,5},{5,6},{6,7},{8,9},{9,10},{10,11},{12,13},{... | collective-permute-start | bytes 1228808 | tf_op jit(solution)/shard_map/ppermute | solution.py:227
  99.9 2.7 %collective-permute-done.24 = bf16[160,1280]{1,0:T(8,128)(2,1)S(1)} collective-permute-done((bf16[160,1280]{1,0:T(8,128)(2,1)S(1)}, bf16[160,1280]{1,0:T(8,128)(2,1)S(1)}, u32[]{:S(2)}, u32[]{:S(2)}) %collective-permute-start.24) | collective-permute-done | bytes 409632 | tf_op jit(solution)/shard_map/ppermute | solution.py:227
  102.7 4.7 %collective-permute-start.26 = (bf16[160,1280]{1,0:T(8,128)(2,1)S(1)}, bf16[160,1280]{1,0:T(8,128)(2,1)S(1)}, u32[]{:S(2)}, u32[]{:S(2)}) collective-permute-start(bf16[160,1280]{1,0:T(8,128)(2,1)S(1)} %get-tuple-element.59), channel_id=1, source_target_pairs={{0,1},{1,2},{2,3},{4,5},{5,6},{6,7},{8,9},{9,10},{10,11},{12,13},{... | collective-permute-start | bytes 1228808 | tf_op jit(solution)/shard_map/ppermute | solution.py:227
  108.7 2.6 %collective-permute-done.14 = bf16[160,1280]{1,0:T(8,128)(2,1)S(1)} collective-permute-done((bf16[160,1280]{1,0:T(8,128)(2,1)S(1)}, bf16[160,1280]{1,0:T(8,128)(2,1)S(1)}, u32[]{:S(2)}, u32[]{:S(2)}) %collective-permute-start.14) | collective-permute-done | bytes 409632 | tf_op jit(solution)/shard_map/ppermute | solution.py:227
  112.0 4.7 %collective-permute-done.26 = bf16[160,1280]{1,0:T(8,128)(2,1)S(1)} collective-permute-done((bf16[160,1280]{1,0:T(8,128)(2,1)S(1)}, bf16[160,1280]{1,0:T(8,128)(2,1)S(1)}, u32[]{:S(2)}, u32[]{:S(2)}) %collective-permute-start.26) | collective-permute-done | bytes 409632 | tf_op jit(solution)/shard_map/ppermute | solution.py:227
  (60 shorter events, 17.6 us)
Async XLA Ops:
  4.3 18.2 %collective-permute-start.2 = (bf16[2320,128]{1,0:T(8,128)(2,1)S(1)}, bf16[2320,128]{1,0:T(8,128)(2,1)S(1)}, u32[]{:S(2)}, u32[]{:S(2)}) collective-permute-start(bf16[2320,128]{1,0:T(8,128)(2,1)S(1)} %get-tuple-element.36), channel_id=1, source_target_pairs={{0,24},{8,16},{16,8},{24,0},{1,25},{9,17},{17,9},{25,1},{2,26},{10... | collective-permute-start | bytes 1781768 | tf_op jit(solution)/shard_map/ppermute | solution.py:246
  9.1 25.3 %collective-permute-start.1 = (bf16[2320,128]{1,0:T(8,128)(2,1)S(1)}, bf16[2320,128]{1,0:T(8,128)(2,1)S(1)}, u32[]{:S(2)}, u32[]{:S(2)}) collective-permute-start(bf16[2320,128]{1,0:T(8,128)(2,1)S(1)} %get-tuple-element.35), channel_id=1, source_target_pairs={{0,16},{8,24},{16,0},{24,8},{1,17},{9,25},{17,1},{25,9},{2,18},{10... | collective-permute-start | bytes 1781768 | tf_op jit(solution)/shard_map/ppermute | solution.py:246
  10.5 24.2 %collective-permute-start = (bf16[2320,128]{1,0:T(8,128)(2,1)S(1)}, bf16[2320,128]{1,0:T(8,128)(2,1)S(1)}, u32[]{:S(2)}, u32[]{:S(2)}) collective-permute-start(bf16[2320,128]{1,0:T(8,128)(2,1)S(1)} %get-tuple-element.34), channel_id=1, source_target_pairs={{0,8},{8,0},{16,24},{24,16},{1,9},{9,1},{17,25},{25,17},{2,10},{10... | collective-permute-start | bytes 1781768 | tf_op jit(solution)/shard_map/ppermute | solution.py:246
  11.5 26.1 %collective-permute-start.3 = (bf16[2320,128]{1,0:T(8,128)(2,1)S(1)}, bf16[2320,128]{1,0:T(8,128)(2,1)S(1)}, u32[]{:S(2)}, u32[]{:S(2)}) collective-permute-start(bf16[2320,128]{1,0:T(8,128)(2,1)S(1)} %get-tuple-element.33.refs_2_.refs_6_), channel_id=1, source_target_pairs={{0,4},{4,0},{1,5},{5,1},{2,6},{6,2},{3,7},{7,3},{8,12},{12,8},{9,1... | collective-permute-start | bytes 1781768 | tf_op jit(solution)/shard_map/ppermute | solution.py:250
  22.6 15.5 %collective-permute-start.6 = (bf16[2320,128]{1,0:T(8,128)(2,1)S(1)}, bf16[2320,128]{1,0:T(8,128)(2,1)}, u32[]{:S(2)}, u32[]{:S(2)}) collective-permute-start(bf16[2320,128]{1,0:T(8,128)(2,1)S(1)} %collective-permute-done.2.refs_5_.refs_9_), channel_id=1, source_target_pairs={{0,4},{4,0},{1,5},{5,1},{2,6},{6,2},{3,7},{7,3},{8,12},{12,8},{9,1... | collective-permute-start | bytes 1781768 | tf_op jit(solution)/shard_map/ppermute | solution.py:250
  34.9 13.8 %collective-permute-start.18 = (bf16[400,128]{1,0:T(8,128)(2,1)S(1)}, bf16[400,128]{1,0:T(8,128)(2,1)S(1)}, u32[]{:S(2)}, u32[]{:S(2)}) collective-permute-start(bf16[400,128]{1,0:T(8,128)(2,1)S(1)} %get-tuple-element.50), channel_id=1, source_target_pairs={{0,24},{8,16},{16,8},{24,0},{1,25},{9,17},{17,9},{25,1},{2,26},{10... | collective-permute-start | bytes 307208 | tf_op jit(solution)/shard_map/ppermute | solution.py:246
  37.6 11.4 %collective-permute-start.17 = (bf16[400,128]{1,0:T(8,128)(2,1)S(1)}, bf16[400,128]{1,0:T(8,128)(2,1)S(1)}, u32[]{:S(2)}, u32[]{:S(2)}) collective-permute-start(bf16[400,128]{1,0:T(8,128)(2,1)S(1)} %get-tuple-element.49), channel_id=1, source_target_pairs={{0,16},{8,24},{16,0},{24,8},{1,17},{9,25},{17,1},{25,9},{2,18},{10... | collective-permute-start | bytes 307208 | tf_op jit(solution)/shard_map/ppermute | solution.py:246
  38.1 10.9 %collective-permute-start.16 = (bf16[400,128]{1,0:T(8,128)(2,1)S(1)}, bf16[400,128]{1,0:T(8,128)(2,1)S(1)}, u32[]{:S(2)}, u32[]{:S(2)}) collective-permute-start(bf16[400,128]{1,0:T(8,128)(2,1)S(1)} %get-tuple-element.48), channel_id=1, source_target_pairs={{0,8},{8,0},{16,24},{24,16},{1,9},{9,1},{17,25},{25,17},{2,10},{10... | collective-permute-start | bytes 307208 | tf_op jit(solution)/shard_map/ppermute | solution.py:246
  45.4 13.9 %collective-permute-start.7 = (bf16[400,128]{1,0:T(8,128)(2,1)S(1)}, bf16[400,128]{1,0:T(8,128)(2,1)S(1)}, u32[]{:S(2)}, u32[]{:S(2)}) collective-permute-start(bf16[400,128]{1,0:T(8,128)(2,1)S(1)} %get-tuple-element.38), channel_id=1, source_target_pairs={{0,8},{8,0},{16,24},{24,16},{1,9},{9,1},{17,25},{25,17},{2,10},{10... | collective-permute-start | bytes 307208 | tf_op jit(solution)/shard_map/ppermute | solution.py:246
  47.2 12.4 %collective-permute-start.8 = (bf16[400,128]{1,0:T(8,128)(2,1)S(1)}, bf16[400,128]{1,0:T(8,128)(2,1)S(1)}, u32[]{:S(2)}, u32[]{:S(2)}) collective-permute-start(bf16[400,128]{1,0:T(8,128)(2,1)S(1)} %get-tuple-element.39), channel_id=1, source_target_pairs={{0,16},{8,24},{16,0},{24,8},{1,17},{9,25},{17,1},{25,9},{2,18},{10... | collective-permute-start | bytes 307208 | tf_op jit(solution)/shard_map/ppermute | solution.py:246
  48.7 10.9 %collective-permute-start.9 = (bf16[400,128]{1,0:T(8,128)(2,1)S(1)}, bf16[400,128]{1,0:T(8,128)(2,1)S(1)}, u32[]{:S(2)}, u32[]{:S(2)}) collective-permute-start(bf16[400,128]{1,0:T(8,128)(2,1)S(1)} %get-tuple-element.40), channel_id=1, source_target_pairs={{0,24},{8,16},{16,8},{24,0},{1,25},{9,17},{17,9},{25,1},{2,26},{10... | collective-permute-start | bytes 307208 | tf_op jit(solution)/shard_map/ppermute | solution.py:246
  56.0 11.0 %collective-permute-start.19 = (bf16[400,128]{1,0:T(8,128)(2,1)S(1)}, bf16[400,128]{1,0:T(8,128)(2,1)S(1)}, u32[]{:S(2)}, u32[]{:S(2)}) collective-permute-start(bf16[400,128]{1,0:T(8,128)(2,1)S(1)} %get-tuple-element.52), channel_id=1, source_target_pairs={{0,8},{8,0},{16,24},{24,16},{1,9},{9,1},{17,25},{25,17},{2,10},{10... | collective-permute-start | bytes 307208 | tf_op jit(solution)/shard_map/ppermute | solution.py:246
  62.7 13.6 %collective-permute-start.10 = (bf16[160,1280]{1,0:T(8,128)(2,1)S(1)}, bf16[160,1280]{1,0:T(8,128)(2,1)S(1)}, u32[]{:S(2)}, u32[]{:S(2)}) collective-permute-start(bf16[160,1280]{1,0:T(8,128)(2,1)S(1)} %get-tuple-element.41), channel_id=1, source_target_pairs={{0,1},{4,5},{8,9},{12,13},{16,17},{20,21},{24,25},{28,29}} | collective-permute-start | bytes 1228808 | tf_op jit(solution)/shard_map/ppermute | solution.py:227
  66.3 9.9 %collective-permute-start.11 = (bf16[160,1280]{1,0:T(8,128)(2,1)S(1)}, bf16[160,1280]{1,0:T(8,128)(2,1)S(1)}, u32[]{:S(2)}, u32[]{:S(2)}) collective-permute-start(bf16[160,1280]{1,0:T(8,128)(2,1)S(1)} %get-tuple-element.42), channel_id=1, source_target_pairs={{3,2},{7,6},{11,10},{15,14},{19,18},{23,22},{27,26},{31,30}} | collective-permute-start | bytes 1228808 | tf_op jit(solution)/shard_map/ppermute | solution.py:228
  70.1 14.9 %collective-permute-start.22 = (bf16[160,1280]{1,0:T(8,128)(2,1)S(1)}, bf16[160,1280]{1,0:T(8,128)(2,1)S(1)}, u32[]{:S(2)}, u32[]{:S(2)}) collective-permute-start(bf16[160,1280]{1,0:T(8,128)(2,1)S(1)} %get-tuple-element.55), channel_id=1, source_target_pairs={{0,1},{4,5},{8,9},{12,13},{16,17},{20,21},{24,25},{28,29}} | collective-permute-start | bytes 1228808 | tf_op jit(solution)/shard_map/ppermute | solution.py:227
  71.5 13.5 %collective-permute-start.23 = (bf16[160,1280]{1,0:T(8,128)(2,1)S(1)}, bf16[160,1280]{1,0:T(8,128)(2,1)S(1)}, u32[]{:S(2)}, u32[]{:S(2)}) collective-permute-start(bf16[160,1280]{1,0:T(8,128)(2,1)S(1)} %get-tuple-element.56), channel_id=1, source_target_pairs={{3,2},{7,6},{11,10},{15,14},{19,18},{23,22},{27,26},{31,30}} | collective-permute-start | bytes 1228808 | tf_op jit(solution)/shard_map/ppermute | solution.py:228
  76.3 17.5 %collective-permute-start.12 = (bf16[160,1280]{1,0:T(8,128)(2,1)S(1)}, bf16[160,1280]{1,0:T(8,128)(2,1)S(1)}, u32[]{:S(2)}, u32[]{:S(2)}) collective-permute-start(bf16[160,1280]{1,0:T(8,128)(2,1)S(1)} %get-tuple-element.43), channel_id=1, source_target_pairs={{0,1},{1,2},{4,5},{5,6},{8,9},{9,10},{12,13},{13,14},{16,17},{17,1... | collective-permute-start | bytes 1228808 | tf_op jit(solution)/shard_map/ppermute | solution.py:227
  80.7 13.0 %collective-permute-start.13 = (bf16[160,1280]{1,0:T(8,128)(2,1)S(1)}, bf16[160,1280]{1,0:T(8,128)(2,1)S(1)}, u32[]{:S(2)}, u32[]{:S(2)}) collective-permute-start(bf16[160,1280]{1,0:T(8,128)(2,1)S(1)} %get-tuple-element.44), channel_id=1, source_target_pairs={{3,2},{2,1},{7,6},{6,5},{11,10},{10,9},{15,14},{14,13},{19,18},{18... | collective-permute-start | bytes 1228808 | tf_op jit(solution)/shard_map/ppermute | solution.py:228
  85.1 17.4 %collective-permute-start.24 = (bf16[160,1280]{1,0:T(8,128)(2,1)S(1)}, bf16[160,1280]{1,0:T(8,128)(2,1)S(1)}, u32[]{:S(2)}, u32[]{:S(2)}) collective-permute-start(bf16[160,1280]{1,0:T(8,128)(2,1)S(1)} %get-tuple-element.57), channel_id=1, source_target_pairs={{0,1},{1,2},{4,5},{5,6},{8,9},{9,10},{12,13},{13,14},{16,17},{17,1... | collective-permute-start | bytes 1228808 | tf_op jit(solution)/shard_map/ppermute | solution.py:227
  89.5 13.0 %collective-permute-start.25 = (bf16[160,1280]{1,0:T(8,128)(2,1)S(1)}, bf16[160,1280]{1,0:T(8,128)(2,1)S(1)}, u32[]{:S(2)}, u32[]{:S(2)}) collective-permute-start(bf16[160,1280]{1,0:T(8,128)(2,1)S(1)} %get-tuple-element.58), channel_id=1, source_target_pairs={{3,2},{2,1},{7,6},{6,5},{11,10},{10,9},{15,14},{14,13},{19,18},{18... | collective-permute-start | bytes 1228808 | tf_op jit(solution)/shard_map/ppermute | solution.py:228
  93.9 17.4 %collective-permute-start.14 = (bf16[160,1280]{1,0:T(8,128)(2,1)S(1)}, bf16[160,1280]{1,0:T(8,128)(2,1)S(1)}, u32[]{:S(2)}, u32[]{:S(2)}) collective-permute-start(bf16[160,1280]{1,0:T(8,128)(2,1)S(1)} %get-tuple-element.45), channel_id=1, source_target_pairs={{0,1},{1,2},{2,3},{4,5},{5,6},{6,7},{8,9},{9,10},{10,11},{12,13},{... | collective-permute-start | bytes 1228808 | tf_op jit(solution)/shard_map/ppermute | solution.py:227
  98.6 13.3 %collective-permute-start.15 = (bf16[160,1280]{1,0:T(8,128)(2,1)S(1)}, bf16[160,1280]{1,0:T(8,128)(2,1)S(1)}, u32[]{:S(2)}, u32[]{:S(2)}) collective-permute-start(bf16[160,1280]{1,0:T(8,128)(2,1)S(1)} %get-tuple-element.46), channel_id=1, source_target_pairs={{3,2},{2,1},{1,0},{7,6},{6,5},{5,4},{11,10},{10,9},{9,8},{15,14},{... | collective-permute-start | bytes 1228808 | tf_op jit(solution)/shard_map/ppermute | solution.py:228
  102.7 14.0 %collective-permute-start.26 = (bf16[160,1280]{1,0:T(8,128)(2,1)S(1)}, bf16[160,1280]{1,0:T(8,128)(2,1)S(1)}, u32[]{:S(2)}, u32[]{:S(2)}) collective-permute-start(bf16[160,1280]{1,0:T(8,128)(2,1)S(1)} %get-tuple-element.59), channel_id=1, source_target_pairs={{0,1},{1,2},{2,3},{4,5},{5,6},{6,7},{8,9},{9,10},{10,11},{12,13},{... | collective-permute-start | bytes 1228808 | tf_op jit(solution)/shard_map/ppermute | solution.py:227
  107.4 9.8 %collective-permute-start.27 = (bf16[160,1280]{1,0:T(8,128)(2,1)S(1)}, bf16[160,1280]{1,0:T(8,128)(2,1)S(1)}, u32[]{:S(2)}, u32[]{:S(2)}) collective-permute-start(bf16[160,1280]{1,0:T(8,128)(2,1)S(1)} %get-tuple-element.60), channel_id=1, source_target_pairs={{3,2},{2,1},{1,0},{7,6},{6,5},{5,4},{11,10},{10,9},{9,8},{15,14},{... | collective-permute-start | bytes 1228808 | tf_op jit(solution)/shard_map/ppermute | solution.py:228
  (9 other events, 77.3 us)

commit v3 on v2

--- a/solution.py
+++ b/solution.py
@@ -14,11 +14,11 @@
 VMEM = pltpu.CompilerParams(vmem_limit_bytes=32 * 1024 * 1024)
 
 
-def pack_kernel(t_ref, q_ref, k_ref, v_ref, first, *rest, partner, partners, full, share, row):
+def pack_kernel(q_ref, k_ref, v_ref, first, *rest, partner, partners, full, share, row):
     sems = rest[-1]
     tokens = q_ref.shape[0]
     part = tokens // CHUNKS
-    chip = t_ref[0] ^ partner
+    chip = lax.axis_index("tm") ^ partner
     heads = [chip * full + i for i in range(full)] + [partners * full + chip // share]
     lanes = [pl.ds(pl.multiple_of(h * HD, HD), HD) for h in heads]
     moves = []
@@ -39,7 +39,8 @@
         copy.wait()
 
 
-def pack(t, q, k, v, partner, partners, full, share, row):
+def pack(q, k, v, partner, partners, full, share, row):
+    direct = partner == partners - 1
     tokens = q.shape[0]
     queries = full * (tokens // CHUNKS) + row
     slabs = 2 * (full + 1) * tokens + queries
@@ -54,16 +55,16 @@
     return pl.pallas_call(
         kernel,
         out_shape=shapes,
-        in_specs=[pl.BlockSpec(memory_space=pltpu.SMEM), anywhere, anywhere, anywhere],
+        in_specs=[anywhere] * 3,
         out_specs=[whole] * len(shapes),
         scratch_shapes=[pltpu.SemaphoreType.DMA(((full + 1) * (2 + CHUNKS),))],
-        compiler_params=VMEM,
+        compiler_params=pltpu.CompilerParams(vmem_limit_bytes=(60 if direct else 32) * 1024 * 1024),
         name="pack",
-    )(t, q, k, v)
+    )(q, k, v)
 
 
 def attend_kernel(
-    place_ref, window_ref, *refs, chunk, partners, full, share, row, rows_dev, total_rows, asked
+    window_ref, *refs, chunk, partners, full, share, row, rows_dev, total_rows, asked
 ):
     queries = refs[:partners]
     near = refs[partners : 2 * partners]
@@ -72,7 +73,7 @@
     slots = full + 1
     tokens = rows_dev * row
     count = 2 * partners * tokens
-    t, s = place_ref[0], place_ref[1]
+    t, s = lax.axis_index("tm"), lax.axis_index("space")
     rows_part = rows_dev // CHUNKS
     factor = math.log2(math.e) / math.sqrt(HD)
 
@@ -132,7 +133,7 @@
     gather(*last)
 
 
-def attend(place, window, queries, near, far, chunk, full, share, row, rows_dev):
+def attend(window, queries, near, far, chunk, full, share, row, rows_dev):
     partners = len(queries)
     rows_out = full * (rows_dev // CHUNKS) * row + row
     count = 2 * partners * rows_dev * row
@@ -156,78 +157,98 @@
     return pl.pallas_call(
         kernel,
         out_shape=[jax.ShapeDtypeStruct((rows_out, HD), jnp.bfloat16)] * partners,
-        in_specs=[scalars, scalars] + [whole] * (3 * partners),
+        in_specs=[scalars] + [whole] * (3 * partners),
         out_specs=[whole] * partners,
         compiler_params=VMEM,
         cost_estimate=pl.CostEstimate(
             flops=work * HD * 4, bytes_accessed=count * HD * 4 * (full + 1), transcendentals=work
         ),
         name="attend",
-    )(place, window, *queries, *near, *far)
-
-
-def project_kernel(t_ref, *refs, partners, full, share, row):
-    parts = refs[:partners]
-    weight, out, mixed = refs[partners:]
-    part = mixed.shape[0]
+    )(window, *queries, *near, *far)
+
+
+def shares_sent(place, size):
+    wanted = []
+    for k in range(1, size):
+        right, left = place + size - k, place - size + k
+        if 2 * k <= size:
+            wanted.append(jnp.where(place < k, right, jnp.maximum(left, 0)))
+        else:
+            wanted += [jnp.minimum(right, size - 1), jnp.maximum(left, 0)]
+    return [*wanted, place]
+
+
+def project_kernel(*refs, after, partners, full, share, row, size):
+    parts, weight, outs, mixed = refs[:partners], refs[partners], refs[partners + 1 + after : -1], refs[-1]
+    part, block = outs[0].shape
+    wide = full * HD
+    t = lax.axis_index("tm")
+    firsts, lasts = [], []
     for m in range(partners):
-        chip = t_ref[0] ^ m
         for i in range(full):
-            lane = pl.ds(pl.multiple_of((chip * full + i) * HD, HD), HD)
-            mixed[:, lane] = parts[m][pl.ds(i * part, part)]
-        lane = pl.ds(pl.multiple_of((partners * full + chip // share) * HD, HD), HD)
-        rows = pl.ds(pl.multiple_of((chip % share) * row, 16), row)
-        mixed[rows, lane] = parts[m][pl.ds(full * part, row)]
-    shares, _, block = out.shape
-    for d in range(shares):
-        product = jnp.dot(mixed[...], weight[:, d * block : (d + 1) * block], preferred_element_type=jnp.float32)
-        out[d] = product.astype(out.dtype)
-
-
-def project(t, parts, weight, shares, full, share, row):
+            mixed[:, m * wide + i * HD : m * wide + (i + 1) * HD] = parts[m][pl.ds(i * part, part)]
+        firsts.append((t ^ m) * wide)
+        group, offset = divmod(m, share)
+        lane = partners * wide + group * HD
+        rows = pl.ds(pl.multiple_of((t ^ m) % share * row, 16), row)
+        mixed[rows, lane : lane + HD] = parts[m][pl.ds(full * part, row)]
+        if offset == 0:
+            lasts.append(partners * wide + (t ^ m) // share * HD)
+    starts = [(start, wide) for start in firsts] + [(start, HD) for start in lasts]
+    for d, out in zip(shares_sent(lax.axis_index("head"), size), outs):
+        columns = pl.ds(pl.multiple_of(d * block, HD), block)
+        rows = [weight[pl.ds(pl.multiple_of(start, HD), n), columns] for start, n in starts]
+        product = jnp.dot(mixed[...], jnp.concatenate(rows, axis=0), preferred_element_type=jnp.float32)
+        out[...] = product.astype(out.dtype)
+
+
+def project(parts, weight, size, full, share, row, after=()):
     partners = len(parts)
     feats, width = weight.shape
     part = (parts[0].shape[0] - row) // full
-    block = width // shares
+    count = len(shares_sent(0, size))
     whole = pl.BlockSpec(memory_space=pltpu.VMEM)
 
     def kernel(*refs):
-        project_kernel(*refs, partners=partners, full=full, share=share, row=row)
+        project_kernel(
+            *refs, after=len(after), partners=partners, full=full, share=share, row=row, size=size
+        )
 
     return pl.pallas_call(
         kernel,
-        out_shape=jax.ShapeDtypeStruct((shares, part, block), jnp.bfloat16),
-        in_specs=[pl.BlockSpec(memory_space=pltpu.SMEM)] + [whole] * (partners + 1),
-        out_specs=whole,
+        out_shape=[jax.ShapeDtypeStruct((part, width // size), jnp.bfloat16)] * count,
+        in_specs=[whole] * (partners + 1) + [pl.BlockSpec(memory_space=pl.ANY)] * len(after),
+        out_specs=[whole] * count,
         scratch_shapes=[pltpu.VMEM((part, feats), jnp.bfloat16)],
         compiler_params=VMEM,
         cost_estimate=pl.CostEstimate(
             flops=2 * part * feats * width, bytes_accessed=2 * feats * width, transcendentals=0
         ),
         name="project",
-    )(t, *parts, weight)
-
-
-def scatter_sums(chunks, axis):
+    )(*parts, weight, *after)
+
+
+def begin_sums(shares, axis):
     size = lax.axis_size(axis)
-    place = lax.axis_index(axis)
-
-    def share(mixed, d):
-        return lax.dynamic_index_in_dim(mixed, jnp.clip(d, 0, size - 1), 0, False)
-
-    held = [None] * len(chunks)
-    for step in range(1, size):
-        for c, mixed in enumerate(chunks):
-            right = share(mixed, place + size - step)
-            left = share(mixed, place - size + step)
-            if held[c] is not None:
-                right, left = right + held[c][0], left + held[c][1]
-            right, left = lax.optimization_barrier((right, left))
+    come = lax.ppermute(shares[0], axis, [(0, 1), (size - 1, size - 2)])
+    return shares[1] + come, list(shares[2:])
+
+
+def finish_sums(begun, axis):
+    size = lax.axis_size(axis)
+    held = [(sent, sent) for sent, _ in begun]
+    for step in range(2, size):
+        for c, (_, shares) in enumerate(begun):
+            right, left = held[c]
+            if step > 2:
+                send_right = shares.pop(0)
+                send_left = send_right if 2 * step <= size else shares.pop(0)
+                right, left = send_right + right, send_left + left
             held[c] = (
                 lax.ppermute(right, axis, [(i, i + 1) for i in range(step)]),
                 lax.ppermute(left, axis, [(size - 1 - i, size - 2 - i) for i in range(step)]),
             )
-    return [share(mixed, place) + right + left for mixed, (right, left) in zip(chunks, held)]
+    return [own + right + left for (_, (own,)), (right, left) in zip(begun, held)]
 
 
 def exchange_plan(query, key, value, window, out_weight):
@@ -236,26 +257,27 @@
     heads = feats // HD
     full = heads // partners
     share = partners // (heads - full * partners)
-    t = lax.axis_index("tm").astype(jnp.int32)
-    s = lax.axis_index("space").astype(jnp.int32)
-    place = jnp.stack([t, s])
     tokens = rows_dev * width
     flat = [a.reshape(tokens, feats) for a in (query, key, value)]
 
     def swap(x, m):
         return x if m == 0 else lax.ppermute(x, "tm", [(i, i ^ m) for i in range(partners)])
 
-    packed = [pack(place, *flat, m, partners, full, share, width) for m in range(partners)]
+    packed = [pack(*flat, m, partners, full, share, width) for m in range(partners)]
     near = [swap(p[0], m) for m, p in enumerate(packed)]
     far = [lax.ppermute(x, "space", [(0, 1), (1, 0)]) for x in near]
 
-    mixed = []
+    done = []
     for c in range(CHUNKS):
         queries = near if c == 0 else [swap(p[c], m) for m, p in enumerate(packed)]
-        done = attend(place, window, queries, near, far, c, full, share, width, rows_dev)
-        done = [swap(x, m) for m, x in enumerate(done)]
-        mixed.append(project(place, done, out_weight, lax.axis_size("head"), full, share, width))
-    outputs = scatter_sums(mixed, "head")
+        done.append(attend(window, queries, near, far, c, full, share, width, rows_dev))
+    begun = []
+    for c in range(CHUNKS):
+        parts = [swap(x, m) for m, x in enumerate(done[c])]
+        after = [x[0] for x in done[c + 1 :]]
+        shares = project(parts, out_weight, lax.axis_size("head"), full, share, width, after)
+        begun.append(begin_sums(shares, "head"))
+    outputs = finish_sums(begun, "head")
     return jnp.concatenate(outputs, axis=0).reshape(frames_dev, rows_dev, width, -1)
 
 
@@ -264,6 +286,8 @@
     frames, rows, width, feats = query.shape
     heads = feats // HD // mesh.shape["head"]
     rows_dev = rows // sides
+    if mesh.shape["head"] != 4:
+        return False
     rest = heads % partners
     if partners & (partners - 1) or sides != 2 or frames != partners or rest == 0 or heads < partners:
         return False

time: 119 us -> 114 us (0.958)
  waiting for transfers between devices: 45.5 us -> 50.1 us
  starting transfers between devices: 44.2 us -> 40.3 us
  local copies, waits for them, and re-layouts: 3.57 us -> 0.03 us
  Pallas kernels: 23.2 us -> 21.3 us
    ppermute x12, waiting for transfers between devices: 23.2 us -> 29.5 us  [swap(): lax.ppermute(x, 'tm', [(i, i ^ m) for i in range(partners)])]
    ppermute x12 -> x10, starting transfers between devices: 28.6 us -> 24.7 us  [the longest x4 15.7 us: finish_sums(): lax.ppermute(right, axis, [(i, i + 1) for i in range(step)])]
    unnamed x10 -> x12, local copies, waits for them, and re-layouts: 3.45 us -> 0.03 us
    ppermute x12 -> x10, waiting for transfers between devices: 22.3 us -> 20.6 us  [the longest x4 13.4 us: finish_sums(): lax.ppermute(right, axis, [(i, i + 1) for i in range(step)])]
    pallas_call x2, Pallas kernels: 14 us -> 12.3 us  [attend(): pl.pallas_call(kernel, out_shape=[jax.ShapeDtypeStruct((rows_out, HD), jn...]
  transfers between devices with their start and end apart: 28 -> 26, of which waited for: 11 -> 11; matrix products, arithmetic and copies ran while one was open for 0% -> 1% of each run, Pallas kernels for 19% -> 14%
where the time goes in v3:
time: 114 us
  waiting for transfers between devices  50.1 us (44%)
  starting transfers between devices  40.3 us (35%)
  Pallas kernels  21.3 us (19%)
  other arithmetic  1.66 us (1%)
    ppermute x12, waiting for transfers between devices, swap(): lax.ppermute(x, 'tm', [(i, i ^ m) for i in range(partners)])  29.5 us
    ppermute x4, starting transfers between devices, finish_sums(): lax.ppermute(right, axis, [(i, i + 1) for i in range(step)])  15.7 us
    ppermute x12, starting transfers between devices, swap(): lax.ppermute(x, 'tm', [(i, i ^ m) for i in range(partners)])  15.3 us
    ppermute x4, waiting for transfers between devices, finish_sums(): lax.ppermute(right, axis, [(i, i + 1) for i in range(step)])  13.4 us
    pallas_call x2, Pallas kernels, attend(): pl.pallas_call(kernel, out_shape=[jax.ShapeDtypeStruct((rows_out, HD), jn...  12.3 us
    ppermute x2, waiting for transfers between devices, begin_sums(): come = lax.ppermute(shares[0], axis, [(0, 1), (size - 1, size - 2)])  7.19 us
    pallas_call x2, Pallas kernels, project(): pl.pallas_call(kernel, out_shape=[jax.ShapeDtypeStruct((part, width // si...  6.03 us
    ppermute x2, starting transfers between devices, begin_sums(): come = lax.ppermute(shares[0], axis, [(0, 1), (size - 1, size - 2)])  5.02 us
  transfers between devices with their start and end apart: 26, of which 11 were waited for; matrix products, arithmetic and copies ran while one was open for 1% of the time, Pallas kernels for 14%

profile of v3, /device:TPU:0, one launch (start us, length us, event | category | flops | bytes accessed | tf_op | source)
XLA Modules:
  0.0 113.7 jit_solution(12084894235170283033)
XLA Ops:
  0.0 2.2 %pack.7 = (bf16[2320,128]{1,0:T(8,128)(2,1)}, bf16[400,128]{1,0:T(8,128)(2,1)}) custom-call(bf16[320,1280]{1,0:T(8,128)(2,1)} %bitcast.4, bf16[320,1280]{1,0:T(8,128)(2,1)} %bitcast.8, bf16[320,1280]{1,0:T(8,128)(2,1)} %bitcast.12), custom_call_target="tpu_custom_call" | custom-call | tf_op jit(solution)/shard_map/pack/pallas_call | solution.py:55
  2.2 4.0 %collective-permute-start.2 = (bf16[2320,128]{1,0:T(8,128)(2,1)}, bf16[2320,128]{1,0:T(8,128)(2,1)S(1)}, u32[]{:S(2)}, u32[]{:S(2)}) collective-permute-start(bf16[2320,128]{1,0:T(8,128)(2,1)} %get-tuple-element.34), channel_id=1, source_target_pairs={{0,24},{8,16},{16,8},{24,0},{1,25},{9,17},{17,9},{25,1},{2,26},{10... | collective-permute-start | bytes 1781768 | tf_op jit(solution)/shard_map/ppermute | solution.py:264
  7.9 12.8 %collective-permute-done.2.refs_4_.refs_8_ = bf16[2320,128]{1,0:T(8,128)(2,1)S(1)} collective-permute-done((bf16[2320,128]{1,0:T(8,128)(2,1)}, bf16[2320,128]{1,0:T(8,128)(2,1)S(1)}, u32[]{:S(2)}, u32[]{:S(2)}) %collective-permute-start.2) | collective-permute-done | bytes 593952 | tf_op jit(solution)/shard_map/ppermute | solution.py:264
  20.7 11.9 %collective-permute-done.1.refs_3_.refs_7_ = bf16[2320,128]{1,0:T(8,128)(2,1)S(1)} collective-permute-done((bf16[2320,128]{1,0:T(8,128)(2,1)S(1)}, bf16[2320,128]{1,0:T(8,128)(2,1)S(1)}, u32[]{:S(2)}, u32[]{:S(2)}) %collective-permute-start.1) | collective-permute-done | bytes 593952 | tf_op jit(solution)/shard_map/ppermute | solution.py:264
  33.1 1.9 %collective-permute-start.12 = (bf16[400,128]{1,0:T(8,128)(2,1)S(1)}, bf16[400,128]{1,0:T(8,128)(2,1)S(1)}, u32[]{:S(2)}, u32[]{:S(2)}) collective-permute-start(bf16[400,128]{1,0:T(8,128)(2,1)S(1)} %copy-done.5), channel_id=1, source_target_pairs={{0,24},{8,16},{16,8},{24,0},{1,25},{9,17},{17,9},{25,1},{2,26},{10... | collective-permute-start | bytes 307208 | tf_op jit(solution)/shard_map/ppermute | solution.py:264
  36.6 6.1 %attend.2 = (bf16[400,128]{1,0:T(8,128)(2,1)S(1)}, bf16[400,128]{1,0:T(8,128)(2,1)S(1)}, bf16[400,128]{1,0:T(8,128)(2,1)S(1)}, bf16[400,128]{1,0:T(8,128)(2,1)S(1)}) custom-call(s32[4,4]{1,0:T(4,128)S(1)} %copy-done.4, bf16[2320,128]{1,0:T(8,128)(2,1)S(1)} %get-tuple-element.31.refs_1_.refs_5_, bf16[2320,128]{1,0:T(8,128)(2,1)S(1)} %collective-permute-done.refs_2_.refs_6_, ...), custom_call_target="tpu_custom_call" | custom-call | flops 2097152000 | bytes 3932160 | tf_op jit(solution)/shard_map/attend/pallas_call | solution.py:157
  42.7 1.7 %collective-permute-start.7 = (bf16[400,128]{1,0:T(8,128)(2,1)S(1)}, bf16[400,128]{1,0:T(8,128)(2,1)S(1)}, u32[]{:S(2)}, u32[]{:S(2)}) collective-permute-start(bf16[400,128]{1,0:T(8,128)(2,1)S(1)} %get-tuple-element.36), channel_id=1, source_target_pairs={{0,8},{8,0},{16,24},{24,16},{1,9},{9,1},{17,25},{25,17},{2,10},{10... | collective-permute-start | bytes 307208 | tf_op jit(solution)/shard_map/ppermute | solution.py:264
  46.2 6.2 %attend.3 = (bf16[400,128]{1,0:T(8,128)(2,1)S(1)}, bf16[400,128]{1,0:T(8,128)(2,1)S(1)}, bf16[400,128]{1,0:T(8,128)(2,1)S(1)}, bf16[400,128]{1,0:T(8,128)(2,1)S(1)}) custom-call(s32[4,4]{1,0:T(4,128)S(1)} %copy-done.4, bf16[400,128]{1,0:T(8,128)(2,1)S(1)} %get-tuple-element.39.refs_1_, bf16[400,128]{1,0:T(8,128)(2,1)S(1)} %collective-permute-done.10.refs_2_, ...), custom_call_target="tpu_custom_call" | custom-call | flops 2097152000 | bytes 3932160 | tf_op jit(solution)/shard_map/attend/pallas_call | solution.py:157
  52.5 3.0 %project.2 = (bf16[160,1280]{1,0:T(8,128)(2,1)S(1)}, bf16[160,1280]{1,0:T(8,128)(2,1)S(1)}, bf16[160,1280]{1,0:T(8,128)(2,1)S(1)}, bf16[160,1280]{1,0:T(8,128)(2,1)S(1)}, bf16[160,1280]{1,0:T(8,128)(2,1)S(1)}) custom-call(bf16[400,128]{1,0:T(8,128)(2,1)S(1)} %get-tuple-element.35.refs_0_, bf16[400,128]{1,0:T(8,128)(2,1)S(1)} %collective-permute-done.7.refs_1_, ...), custom_call_target="tpu_custom_call" | custom-call | flops 2097152000 | bytes 13107200 | tf_op jit(solution)/shard_map/project/pallas_call | solution.py:217
  55.5 3.7 %collective-permute-start.13 = (bf16[160,1280]{1,0:T(8,128)(2,1)S(1)}, bf16[160,1280]{1,0:T(8,128)(2,1)S(1)}, u32[]{:S(2)}, u32[]{:S(2)}) collective-permute-start(bf16[160,1280]{1,0:T(8,128)(2,1)S(1)} %get-tuple-element.47), channel_id=1, source_target_pairs={{0,1},{3,2},{4,5},{7,6},{8,9},{11,10},{12,13},{15,14},{16,17},{19,... | collective-permute-start | bytes 1228808 | tf_op jit(solution)/shard_map/ppermute | solution.py:233
  59.2 1.5 %collective-permute-start.18 = (bf16[400,128]{1,0:T(8,128)(2,1)S(1)}, bf16[400,128]{1,0:T(8,128)(2,1)S(1)}, u32[]{:S(2)}, u32[]{:S(2)}) collective-permute-start(bf16[400,128]{1,0:T(8,128)(2,1)S(1)} %get-tuple-element.49), channel_id=1, source_target_pairs={{0,8},{8,0},{16,24},{24,16},{1,9},{9,1},{17,25},{25,17},{2,10},{10... | collective-permute-start | bytes 307208 | tf_op jit(solution)/shard_map/ppermute | solution.py:264
  62.8 1.8 %collective-permute-done.18.refs_1_ = bf16[400,128]{1,0:T(8,128)(2,1)S(1)} collective-permute-done((bf16[400,128]{1,0:T(8,128)(2,1)S(1)}, bf16[400,128]{1,0:T(8,128)(2,1)S(1)}, u32[]{:S(2)}, u32[]{:S(2)}) %collective-permute-start.18) | collective-permute-done | bytes 102432 | tf_op jit(solution)/shard_map/ppermute | solution.py:264
  65.4 1.9 %collective-permute-done.20.refs_3_ = bf16[400,128]{1,0:T(8,128)(2,1)S(1)} collective-permute-done((bf16[400,128]{1,0:T(8,128)(2,1)S(1)}, bf16[400,128]{1,0:T(8,128)(2,1)S(1)}, u32[]{:S(2)}, u32[]{:S(2)}) %collective-permute-start.20) | collective-permute-done | bytes 102432 | tf_op jit(solution)/shard_map/ppermute | solution.py:264
  67.3 3.0 %project.3 = (bf16[160,1280]{1,0:T(8,128)(2,1)S(1)}, bf16[160,1280]{1,0:T(8,128)(2,1)S(1)}, bf16[160,1280]{1,0:T(8,128)(2,1)S(1)}, bf16[160,1280]{1,0:T(8,128)(2,1)S(1)}, bf16[160,1280]{1,0:T(8,128)(2,1)S(1)}) custom-call(bf16[400,128]{1,0:T(8,128)(2,1)S(1)} %get-tuple-element.43.refs_5_.refs_0_, bf16[400,128]{1,0:T(8,128)(2,1)S(1)} %collective-permute-done.18.refs_1_, ...), custom_call_target="tpu_custom_call" | custom-call | flops 2097152000 | bytes 13107200 | tf_op jit(solution)/shard_map/project/pallas_call | solution.py:217
  70.3 1.3 %collective-permute-start.21 = (bf16[160,1280]{1,0:T(8,128)(2,1)S(1)}, bf16[160,1280]{1,0:T(8,128)(2,1)S(1)}, u32[]{:S(2)}, u32[]{:S(2)}) collective-permute-start(bf16[160,1280]{1,0:T(8,128)(2,1)S(1)} %get-tuple-element.55), channel_id=1, source_target_pairs={{0,1},{3,2},{4,5},{7,6},{8,9},{11,10},{12,13},{15,14},{16,17},{19,... | collective-permute-start | bytes 1228808 | tf_op jit(solution)/shard_map/ppermute | solution.py:233
  72.5 1.9 %collective-permute-start.14 = (bf16[160,1280]{1,0:T(8,128)(2,1)S(1)}, bf16[160,1280]{1,0:T(8,128)(2,1)S(1)}, u32[]{:S(2)}, u32[]{:S(2)}) collective-permute-start(bf16[160,1280]{1,0:T(8,128)(2,1)S(1)} %add.30), channel_id=1, source_target_pairs={{0,1},{1,2},{4,5},{5,6},{8,9},{9,10},{12,13},{13,14},{16,17},{17,1... | collective-permute-start | bytes 1228808 | tf_op jit(solution)/shard_map/ppermute | solution.py:248
  74.4 7.2 %collective-permute-done.21 = bf16[160,1280]{1,0:T(8,128)(2,1)S(1)} collective-permute-done((bf16[160,1280]{1,0:T(8,128)(2,1)S(1)}, bf16[160,1280]{1,0:T(8,128)(2,1)S(1)}, u32[]{:S(2)}, u32[]{:S(2)}) %collective-permute-start.21) | collective-permute-done | bytes 409632 | tf_op jit(solution)/shard_map/ppermute | solution.py:233
  82.3 5.0 %collective-permute-start.22 = (bf16[160,1280]{1,0:T(8,128)(2,1)S(1)}, bf16[160,1280]{1,0:T(8,128)(2,1)S(1)}, u32[]{:S(2)}, u32[]{:S(2)}) collective-permute-start(bf16[160,1280]{1,0:T(8,128)(2,1)S(1)} %add.35), channel_id=1, source_target_pairs={{0,1},{1,2},{4,5},{5,6},{8,9},{9,10},{12,13},{13,14},{16,17},{17,1... | collective-permute-start | bytes 1228808 | tf_op jit(solution)/shard_map/ppermute | solution.py:248
  88.8 1.5 %collective-permute-done.14 = bf16[160,1280]{1,0:T(8,128)(2,1)S(1)} collective-permute-done((bf16[160,1280]{1,0:T(8,128)(2,1)S(1)}, bf16[160,1280]{1,0:T(8,128)(2,1)S(1)}, u32[]{:S(2)}, u32[]{:S(2)}) %collective-permute-start.14) | collective-permute-done | bytes 409632 | tf_op jit(solution)/shard_map/ppermute | solution.py:248
  90.4 4.4 %collective-permute-start.15 = (bf16[160,1280]{1,0:T(8,128)(2,1)S(1)}, bf16[160,1280]{1,0:T(8,128)(2,1)S(1)}, u32[]{:S(2)}, u32[]{:S(2)}) collective-permute-start(bf16[160,1280]{1,0:T(8,128)(2,1)S(1)} %add.31), channel_id=1, source_target_pairs={{0,1},{1,2},{2,3},{4,5},{5,6},{6,7},{8,9},{9,10},{10,11},{12,13},{... | collective-permute-start | bytes 1228808 | tf_op jit(solution)/shard_map/ppermute | solution.py:248
  96.3 2.8 %collective-permute-done.22 = bf16[160,1280]{1,0:T(8,128)(2,1)S(1)} collective-permute-done((bf16[160,1280]{1,0:T(8,128)(2,1)S(1)}, bf16[160,1280]{1,0:T(8,128)(2,1)S(1)}, u32[]{:S(2)}, u32[]{:S(2)}) %collective-permute-start.22) | collective-permute-done | bytes 409632 | tf_op jit(solution)/shard_map/ppermute | solution.py:248
  99.2 4.4 %collective-permute-start.23 = (bf16[160,1280]{1,0:T(8,128)(2,1)S(1)}, bf16[160,1280]{1,0:T(8,128)(2,1)S(1)}, u32[]{:S(2)}, u32[]{:S(2)}) collective-permute-start(bf16[160,1280]{1,0:T(8,128)(2,1)S(1)} %add.36), channel_id=1, source_target_pairs={{0,1},{1,2},{2,3},{4,5},{5,6},{6,7},{8,9},{9,10},{10,11},{12,13},{... | collective-permute-start | bytes 1228808 | tf_op jit(solution)/shard_map/ppermute | solution.py:248
  103.6 4.2 %collective-permute-done.15 = bf16[160,1280]{1,0:T(8,128)(2,1)S(1)} collective-permute-done((bf16[160,1280]{1,0:T(8,128)(2,1)S(1)}, bf16[160,1280]{1,0:T(8,128)(2,1)S(1)}, u32[]{:S(2)}, u32[]{:S(2)}) %collective-permute-start.15) | collective-permute-done | bytes 409632 | tf_op jit(solution)/shard_map/ppermute | solution.py:248
  108.0 4.7 %collective-permute-done.23 = bf16[160,1280]{1,0:T(8,128)(2,1)S(1)} collective-permute-done((bf16[160,1280]{1,0:T(8,128)(2,1)S(1)}, bf16[160,1280]{1,0:T(8,128)(2,1)S(1)}, u32[]{:S(2)}, u32[]{:S(2)}) %collective-permute-start.23) | collective-permute-done | bytes 409632 | tf_op jit(solution)/shard_map/ppermute | solution.py:248
  (57 shorter events, 14.0 us)
Async XLA Ops:
  2.2 18.5 %collective-permute-start.2 = (bf16[2320,128]{1,0:T(8,128)(2,1)}, bf16[2320,128]{1,0:T(8,128)(2,1)S(1)}, u32[]{:S(2)}, u32[]{:S(2)}) collective-permute-start(bf16[2320,128]{1,0:T(8,128)(2,1)} %get-tuple-element.34), channel_id=1, source_target_pairs={{0,24},{8,16},{16,8},{24,0},{1,25},{9,17},{17,9},{25,1},{2,26},{10... | collective-permute-start | bytes 1781768 | tf_op jit(solution)/shard_map/ppermute | solution.py:264
  6.5 26.1 %collective-permute-start.1 = (bf16[2320,128]{1,0:T(8,128)(2,1)S(1)}, bf16[2320,128]{1,0:T(8,128)(2,1)S(1)}, u32[]{:S(2)}, u32[]{:S(2)}) collective-permute-start(bf16[2320,128]{1,0:T(8,128)(2,1)S(1)} %get-tuple-element.33), channel_id=1, source_target_pairs={{0,16},{8,24},{16,0},{24,8},{1,17},{9,25},{17,1},{25,9},{2,18},{10... | collective-permute-start | bytes 1781768 | tf_op jit(solution)/shard_map/ppermute | solution.py:264
  7.4 25.5 %collective-permute-start = (bf16[2320,128]{1,0:T(8,128)(2,1)S(1)}, bf16[2320,128]{1,0:T(8,128)(2,1)S(1)}, u32[]{:S(2)}, u32[]{:S(2)}) collective-permute-start(bf16[2320,128]{1,0:T(8,128)(2,1)S(1)} %get-tuple-element.32), channel_id=1, source_target_pairs={{0,8},{8,0},{16,24},{24,16},{1,9},{9,1},{17,25},{25,17},{2,10},{10... | collective-permute-start | bytes 1781768 | tf_op jit(solution)/shard_map/ppermute | solution.py:264
  7.8 27.2 %collective-permute-start.3 = (bf16[2320,128]{1,0:T(8,128)(2,1)S(1)}, bf16[2320,128]{1,0:T(8,128)(2,1)S(1)}, u32[]{:S(2)}, u32[]{:S(2)}) collective-permute-start(bf16[2320,128]{1,0:T(8,128)(2,1)S(1)} %get-tuple-element.31.refs_1_.refs_5_), channel_id=1, source_target_pairs={{0,4},{4,0},{1,5},{5,1},{2,6},{6,2},{3,7},{7,3},{8,12},{12,8},{9,1... | collective-permute-start | bytes 1781768 | tf_op jit(solution)/shard_map/ppermute | solution.py:268
  20.7 15.5 %collective-permute-start.6 = (bf16[2320,128]{1,0:T(8,128)(2,1)S(1)}, bf16[2320,128]{1,0:T(8,128)(2,1)S(1)}, u32[]{:S(2)}, u32[]{:S(2)}) collective-permute-start(bf16[2320,128]{1,0:T(8,128)(2,1)S(1)} %collective-permute-done.2.refs_4_.refs_8_), channel_id=1, source_target_pairs={{0,4},{4,0},{1,5},{5,1},{2,6},{6,2},{3,7},{7,3},{8,12},{12,8},{9,1... | collective-permute-start | bytes 1781768 | tf_op jit(solution)/shard_map/ppermute | solution.py:268
  33.1 12.2 %collective-permute-start.12 = (bf16[400,128]{1,0:T(8,128)(2,1)S(1)}, bf16[400,128]{1,0:T(8,128)(2,1)S(1)}, u32[]{:S(2)}, u32[]{:S(2)}) collective-permute-start(bf16[400,128]{1,0:T(8,128)(2,1)S(1)} %copy-done.5), channel_id=1, source_target_pairs={{0,24},{8,16},{16,8},{24,0},{1,25},{9,17},{17,9},{25,1},{2,26},{10... | collective-permute-start | bytes 307208 | tf_op jit(solution)/shard_map/ppermute | solution.py:264
  35.0 11.2 %collective-permute-start.11 = (bf16[400,128]{1,0:T(8,128)(2,1)S(1)}, bf16[400,128]{1,0:T(8,128)(2,1)S(1)}, u32[]{:S(2)}, u32[]{:S(2)}) collective-permute-start(bf16[400,128]{1,0:T(8,128)(2,1)S(1)} %get-tuple-element.41), channel_id=1, source_target_pairs={{0,16},{8,24},{16,0},{24,8},{1,17},{9,25},{17,1},{25,9},{2,18},{10... | collective-permute-start | bytes 307208 | tf_op jit(solution)/shard_map/ppermute | solution.py:264
  36.2 10.0 %collective-permute-start.10 = (bf16[400,128]{1,0:T(8,128)(2,1)S(1)}, bf16[400,128]{1,0:T(8,128)(2,1)S(1)}, u32[]{:S(2)}, u32[]{:S(2)}) collective-permute-start(bf16[400,128]{1,0:T(8,128)(2,1)S(1)} %get-tuple-element.40), channel_id=1, source_target_pairs={{0,8},{8,0},{16,24},{24,16},{1,9},{9,1},{17,25},{25,17},{2,10},{10... | collective-permute-start | bytes 307208 | tf_op jit(solution)/shard_map/ppermute | solution.py:264
  42.7 9.8 %collective-permute-start.7 = (bf16[400,128]{1,0:T(8,128)(2,1)S(1)}, bf16[400,128]{1,0:T(8,128)(2,1)S(1)}, u32[]{:S(2)}, u32[]{:S(2)}) collective-permute-start(bf16[400,128]{1,0:T(8,128)(2,1)S(1)} %get-tuple-element.36), channel_id=1, source_target_pairs={{0,8},{8,0},{16,24},{24,16},{1,9},{9,1},{17,25},{25,17},{2,10},{10... | collective-permute-start | bytes 307208 | tf_op jit(solution)/shard_map/ppermute | solution.py:264
  44.4 8.1 %collective-permute-start.8 = (bf16[400,128]{1,0:T(8,128)(2,1)S(1)}, bf16[400,128]{1,0:T(8,128)(2,1)S(1)}, u32[]{:S(2)}, u32[]{:S(2)}) collective-permute-start(bf16[400,128]{1,0:T(8,128)(2,1)S(1)} %get-tuple-element.37), channel_id=1, source_target_pairs={{0,16},{8,24},{16,0},{24,8},{1,17},{9,25},{17,1},{25,9},{2,18},{10... | collective-permute-start | bytes 307208 | tf_op jit(solution)/shard_map/ppermute | solution.py:264
  45.2 7.2 %collective-permute-start.9 = (bf16[400,128]{1,0:T(8,128)(2,1)S(1)}, bf16[400,128]{1,0:T(8,128)(2,1)S(1)}, u32[]{:S(2)}, u32[]{:S(2)}) collective-permute-start(bf16[400,128]{1,0:T(8,128)(2,1)S(1)} %get-tuple-element.38), channel_id=1, source_target_pairs={{0,24},{8,16},{16,8},{24,0},{1,25},{9,17},{17,9},{25,1},{2,26},{10... | collective-permute-start | bytes 307208 | tf_op jit(solution)/shard_map/ppermute | solution.py:264
  55.5 16.1 %collective-permute-start.13 = (bf16[160,1280]{1,0:T(8,128)(2,1)S(1)}, bf16[160,1280]{1,0:T(8,128)(2,1)S(1)}, u32[]{:S(2)}, u32[]{:S(2)}) collective-permute-start(bf16[160,1280]{1,0:T(8,128)(2,1)S(1)} %get-tuple-element.47), channel_id=1, source_target_pairs={{0,1},{3,2},{4,5},{7,6},{8,9},{11,10},{12,13},{15,14},{16,17},{19,... | collective-permute-start | bytes 1228808 | tf_op jit(solution)/shard_map/ppermute | solution.py:233
  59.2 5.4 %collective-permute-start.18 = (bf16[400,128]{1,0:T(8,128)(2,1)S(1)}, bf16[400,128]{1,0:T(8,128)(2,1)S(1)}, u32[]{:S(2)}, u32[]{:S(2)}) collective-permute-start(bf16[400,128]{1,0:T(8,128)(2,1)S(1)} %get-tuple-element.49), channel_id=1, source_target_pairs={{0,8},{8,0},{16,24},{24,16},{1,9},{9,1},{17,25},{25,17},{2,10},{10... | collective-permute-start | bytes 307208 | tf_op jit(solution)/shard_map/ppermute | solution.py:264
  60.8 4.7 %collective-permute-start.19 = (bf16[400,128]{1,0:T(8,128)(2,1)S(1)}, bf16[400,128]{1,0:T(8,128)(2,1)S(1)}, u32[]{:S(2)}, u32[]{:S(2)}) collective-permute-start(bf16[400,128]{1,0:T(8,128)(2,1)S(1)} %get-tuple-element.50), channel_id=1, source_target_pairs={{0,16},{8,24},{16,0},{24,8},{1,17},{9,25},{17,1},{25,9},{2,18},{10... | collective-permute-start | bytes 307208 | tf_op jit(solution)/shard_map/ppermute | solution.py:264
  61.8 5.6 %collective-permute-start.20 = (bf16[400,128]{1,0:T(8,128)(2,1)S(1)}, bf16[400,128]{1,0:T(8,128)(2,1)S(1)}, u32[]{:S(2)}, u32[]{:S(2)}) collective-permute-start(bf16[400,128]{1,0:T(8,128)(2,1)S(1)} %get-tuple-element.51), channel_id=1, source_target_pairs={{0,24},{8,16},{16,8},{24,0},{1,25},{9,17},{17,9},{25,1},{2,26},{10... | collective-permute-start | bytes 307208 | tf_op jit(solution)/shard_map/ppermute | solution.py:264
  70.3 11.2 %collective-permute-start.21 = (bf16[160,1280]{1,0:T(8,128)(2,1)S(1)}, bf16[160,1280]{1,0:T(8,128)(2,1)S(1)}, u32[]{:S(2)}, u32[]{:S(2)}) collective-permute-start(bf16[160,1280]{1,0:T(8,128)(2,1)S(1)} %get-tuple-element.55), channel_id=1, source_target_pairs={{0,1},{3,2},{4,5},{7,6},{8,9},{11,10},{12,13},{15,14},{16,17},{19,... | collective-permute-start | bytes 1228808 | tf_op jit(solution)/shard_map/ppermute | solution.py:233
  71.8 15.6 %collective-permute-start.16 = (bf16[160,1280]{1,0:T(8,128)(2,1)S(1)}, bf16[160,1280]{1,0:T(8,128)(2,1)S(1)}, u32[]{:S(2)}, u32[]{:S(2)}) collective-permute-start(bf16[160,1280]{1,0:T(8,128)(2,1)S(1)} %add.30), channel_id=1, source_target_pairs={{3,2},{2,1},{7,6},{6,5},{11,10},{10,9},{15,14},{14,13},{19,18},{18... | collective-permute-start | bytes 1228808 | tf_op jit(solution)/shard_map/ppermute | solution.py:249
  72.5 17.8 %collective-permute-start.14 = (bf16[160,1280]{1,0:T(8,128)(2,1)S(1)}, bf16[160,1280]{1,0:T(8,128)(2,1)S(1)}, u32[]{:S(2)}, u32[]{:S(2)}) collective-permute-start(bf16[160,1280]{1,0:T(8,128)(2,1)S(1)} %add.30), channel_id=1, source_target_pairs={{0,1},{1,2},{4,5},{5,6},{8,9},{9,10},{12,13},{13,14},{16,17},{17,1... | collective-permute-start | bytes 1228808 | tf_op jit(solution)/shard_map/ppermute | solution.py:248
  81.6 13.2 %collective-permute-start.24 = (bf16[160,1280]{1,0:T(8,128)(2,1)S(1)}, bf16[160,1280]{1,0:T(8,128)(2,1)S(1)}, u32[]{:S(2)}, u32[]{:S(2)}) collective-permute-start(bf16[160,1280]{1,0:T(8,128)(2,1)S(1)} %add.35), channel_id=1, source_target_pairs={{3,2},{2,1},{7,6},{6,5},{11,10},{10,9},{15,14},{14,13},{19,18},{18... | collective-permute-start | bytes 1228808 | tf_op jit(solution)/shard_map/ppermute | solution.py:249
  82.3 16.8 %collective-permute-start.22 = (bf16[160,1280]{1,0:T(8,128)(2,1)S(1)}, bf16[160,1280]{1,0:T(8,128)(2,1)S(1)}, u32[]{:S(2)}, u32[]{:S(2)}) collective-permute-start(bf16[160,1280]{1,0:T(8,128)(2,1)S(1)} %add.35), channel_id=1, source_target_pairs={{0,1},{1,2},{4,5},{5,6},{8,9},{9,10},{12,13},{13,14},{16,17},{17,1... | collective-permute-start | bytes 1228808 | tf_op jit(solution)/shard_map/ppermute | solution.py:248
  87.5 16.1 %collective-permute-start.17 = (bf16[160,1280]{1,0:T(8,128)(2,1)S(1)}, bf16[160,1280]{1,0:T(8,128)(2,1)S(1)}, u32[]{:S(2)}, u32[]{:S(2)}) collective-permute-start(bf16[160,1280]{1,0:T(8,128)(2,1)S(1)} %add.33), channel_id=1, source_target_pairs={{3,2},{2,1},{1,0},{7,6},{6,5},{5,4},{11,10},{10,9},{9,8},{15,14},{... | collective-permute-start | bytes 1228808 | tf_op jit(solution)/shard_map/ppermute | solution.py:249
  90.4 17.5 %collective-permute-start.15 = (bf16[160,1280]{1,0:T(8,128)(2,1)S(1)}, bf16[160,1280]{1,0:T(8,128)(2,1)S(1)}, u32[]{:S(2)}, u32[]{:S(2)}) collective-permute-start(bf16[160,1280]{1,0:T(8,128)(2,1)S(1)} %add.31), channel_id=1, source_target_pairs={{0,1},{1,2},{2,3},{4,5},{5,6},{6,7},{8,9},{9,10},{10,11},{12,13},{... | collective-permute-start | bytes 1228808 | tf_op jit(solution)/shard_map/ppermute | solution.py:248
  95.0 13.0 %collective-permute-start.25 = (bf16[160,1280]{1,0:T(8,128)(2,1)S(1)}, bf16[160,1280]{1,0:T(8,128)(2,1)S(1)}, u32[]{:S(2)}, u32[]{:S(2)}) collective-permute-start(bf16[160,1280]{1,0:T(8,128)(2,1)S(1)} %add.38), channel_id=1, source_target_pairs={{3,2},{2,1},{1,0},{7,6},{6,5},{5,4},{11,10},{10,9},{9,8},{15,14},{... | collective-permute-start | bytes 1228808 | tf_op jit(solution)/shard_map/ppermute | solution.py:249
  99.2 13.5 %collective-permute-start.23 = (bf16[160,1280]{1,0:T(8,128)(2,1)S(1)}, bf16[160,1280]{1,0:T(8,128)(2,1)S(1)}, u32[]{:S(2)}, u32[]{:S(2)}) collective-permute-start(bf16[160,1280]{1,0:T(8,128)(2,1)S(1)} %add.36), channel_id=1, source_target_pairs={{0,1},{1,2},{2,3},{4,5},{5,6},{6,7},{8,9},{9,10},{10,11},{12,13},{... | collective-permute-start | bytes 1228808 | tf_op jit(solution)/shard_map/ppermute | solution.py:248
  (8 other events, 97.2 us)

commit v4 on v3

--- a/solution.py
+++ b/solution.py
@@ -178,7 +178,7 @@
     return [*wanted, place]
 
 
-def project_kernel(*refs, after, partners, full, share, row, size):
+def project_kernel(*refs, after, partners, full, share, row, size, chosen):
     parts, weight, outs, mixed = refs[:partners], refs[partners], refs[partners + 1 + after : -1], refs[-1]
     part, block = outs[0].shape
     wide = full * HD
@@ -195,23 +195,30 @@
         if offset == 0:
             lasts.append(partners * wide + (t ^ m) // share * HD)
     starts = [(start, wide) for start in firsts] + [(start, HD) for start in lasts]
-    for d, out in zip(shares_sent(lax.axis_index("head"), size), outs):
+    for d, out in zip(shares_sent(lax.axis_index("head"), size)[chosen], outs):
         columns = pl.ds(pl.multiple_of(d * block, HD), block)
         rows = [weight[pl.ds(pl.multiple_of(start, HD), n), columns] for start, n in starts]
         product = jnp.dot(mixed[...], jnp.concatenate(rows, axis=0), preferred_element_type=jnp.float32)
         out[...] = product.astype(out.dtype)
 
 
-def project(parts, weight, size, full, share, row, after=()):
+def project(parts, weight, size, full, share, row, chosen, after=()):
     partners = len(parts)
     feats, width = weight.shape
     part = (parts[0].shape[0] - row) // full
-    count = len(shares_sent(0, size))
+    count = len(shares_sent(0, size)[chosen])
     whole = pl.BlockSpec(memory_space=pltpu.VMEM)
 
     def kernel(*refs):
         project_kernel(
-            *refs, after=len(after), partners=partners, full=full, share=share, row=row, size=size
+            *refs,
+            after=len(after),
+            partners=partners,
+            full=full,
+            share=share,
+            row=row,
+            size=size,
+            chosen=chosen,
         )
 
     return pl.pallas_call(
@@ -271,12 +278,19 @@
     for c in range(CHUNKS):
         queries = near if c == 0 else [swap(p[c], m) for m, p in enumerate(packed)]
         done.append(attend(window, queries, near, far, c, full, share, width, rows_dev))
-    begun = []
+    begun, shares = [], ()
     for c in range(CHUNKS):
         parts = [swap(x, m) for m, x in enumerate(done[c])]
-        after = [x[0] for x in done[c + 1 :]]
-        shares = project(parts, out_weight, lax.axis_size("head"), full, share, width, after)
+        common = (parts, out_weight, lax.axis_size("head"), full, share, width)
+        if c == 0:
+            shares = project(*common, slice(1), [x[0] for x in done[1:]])
+            shares += project(*common, slice(1, None))
+        else:
+            shares = project(*common, slice(1), shares[-1:])
+            shares += project(*common, slice(1, None))
         begun.append(begin_sums(shares, "head"))
+        if c == 0:
+            first, *done[1] = lax.optimization_barrier((shares[0], *done[1]))
     outputs = finish_sums(begun, "head")
     return jnp.concatenate(outputs, axis=0).reshape(frames_dev, rows_dev, width, -1)
 

time: 114 us -> 109 us (0.956)
  waiting for transfers between devices: 50.1 us -> 45.1 us
    ppermute x2, waiting for transfers between devices: 7.19 us -> 4.6 us  [begin_sums(): come = lax.ppermute(shares[0], axis, [(0, 1), (size - 1, size - 2)])]
    ppermute x12, waiting for transfers between devices: 29.5 us -> 27.1 us  [swap(): lax.ppermute(x, 'tm', [(i, i ^ m) for i in range(partners)])]
    pallas_call x2 -> x4, Pallas kernels: 6.03 us -> 6.38 us  [project(): pl.pallas_call(kernel, out_shape=[jax.ShapeDtypeStruct((part, width // si...]
  transfers between devices with their start and end apart: 26 -> 26, of which waited for: 11 -> 10; matrix products, arithmetic and copies ran while one was open for 1% -> 1% of each run, Pallas kernels for 14% -> 17%
where the time goes in v4:
time: 109 us
  waiting for transfers between devices  45.1 us (41%)
  starting transfers between devices  40.5 us (37%)
  Pallas kernels  21.5 us (20%)
  other arithmetic  1.65 us (2%)
    ppermute x12, waiting for transfers between devices, swap(): lax.ppermute(x, 'tm', [(i, i ^ m) for i in range(partners)])  27.1 us
    ppermute x4, starting transfers between devices, finish_sums(): lax.ppermute(right, axis, [(i, i + 1) for i in range(step)])  15.9 us
    ppermute x12, starting transfers between devices, swap(): lax.ppermute(x, 'tm', [(i, i ^ m) for i in range(partners)])  15.3 us
    ppermute x4, waiting for transfers between devices, finish_sums(): lax.ppermute(right, axis, [(i, i + 1) for i in range(step)])  13.3 us
    pallas_call x2, Pallas kernels, attend(): pl.pallas_call(kernel, out_shape=[jax.ShapeDtypeStruct((rows_out, HD), jn...  12.1 us
    pallas_call x4, Pallas kernels, project(): pl.pallas_call(kernel, out_shape=[jax.ShapeDtypeStruct((part, width // si...  6.38 us
    ppermute x2, starting transfers between devices, begin_sums(): come = lax.ppermute(shares[0], axis, [(0, 1), (size - 1, size - 2)])  4.99 us
    ppermute x2, waiting for transfers between devices, begin_sums(): come = lax.ppermute(shares[0], axis, [(0, 1), (size - 1, size - 2)])  4.6 us
  transfers between devices with their start and end apart: 26, of which 10 were waited for; matrix products, arithmetic and copies ran while one was open for 1% of the time, Pallas kernels for 17%

profile of v4, /device:TPU:0, one launch (start us, length us, event | category | flops | bytes accessed | tf_op | source)
XLA Modules:
  0.0 109.0 jit_solution(4153337384888205596)
XLA Ops:
  0.0 2.2 %pack.7 = (bf16[2320,128]{1,0:T(8,128)(2,1)}, bf16[400,128]{1,0:T(8,128)(2,1)}) custom-call(bf16[320,1280]{1,0:T(8,128)(2,1)} %bitcast.4, bf16[320,1280]{1,0:T(8,128)(2,1)} %bitcast.8, bf16[320,1280]{1,0:T(8,128)(2,1)} %bitcast.12), custom_call_target="tpu_custom_call" | custom-call | tf_op jit(solution)/shard_map/pack/pallas_call | solution.py:55
  2.2 4.0 %collective-permute-start.2 = (bf16[2320,128]{1,0:T(8,128)(2,1)}, bf16[2320,128]{1,0:T(8,128)(2,1)S(1)}, u32[]{:S(2)}, u32[]{:S(2)}) collective-permute-start(bf16[2320,128]{1,0:T(8,128)(2,1)} %get-tuple-element.36), channel_id=1, source_target_pairs={{0,24},{8,16},{16,8},{24,0},{1,25},{9,17},{17,9},{25,1},{2,26},{10... | collective-permute-start | bytes 1781768 | tf_op jit(solution)/shard_map/ppermute | solution.py:271
  7.9 12.8 %collective-permute-done.2.refs_4_.refs_8_ = bf16[2320,128]{1,0:T(8,128)(2,1)S(1)} collective-permute-done((bf16[2320,128]{1,0:T(8,128)(2,1)}, bf16[2320,128]{1,0:T(8,128)(2,1)S(1)}, u32[]{:S(2)}, u32[]{:S(2)}) %collective-permute-start.2) | collective-permute-done | bytes 593952 | tf_op jit(solution)/shard_map/ppermute | solution.py:271
  20.7 11.9 %collective-permute-done.1.refs_3_.refs_7_ = bf16[2320,128]{1,0:T(8,128)(2,1)S(1)} collective-permute-done((bf16[2320,128]{1,0:T(8,128)(2,1)S(1)}, bf16[2320,128]{1,0:T(8,128)(2,1)S(1)}, u32[]{:S(2)}, u32[]{:S(2)}) %collective-permute-start.1) | collective-permute-done | bytes 593952 | tf_op jit(solution)/shard_map/ppermute | solution.py:271
  33.1 1.9 %collective-permute-start.12 = (bf16[400,128]{1,0:T(8,128)(2,1)S(1)}, bf16[400,128]{1,0:T(8,128)(2,1)S(1)}, u32[]{:S(2)}, u32[]{:S(2)}) collective-permute-start(bf16[400,128]{1,0:T(8,128)(2,1)S(1)} %copy-done.5), channel_id=1, source_target_pairs={{0,24},{8,16},{16,8},{24,0},{1,25},{9,17},{17,9},{25,1},{2,26},{10... | collective-permute-start | bytes 307208 | tf_op jit(solution)/shard_map/ppermute | solution.py:271
  36.6 6.0 %attend.2 = (bf16[400,128]{1,0:T(8,128)(2,1)S(1)}, bf16[400,128]{1,0:T(8,128)(2,1)S(1)}, bf16[400,128]{1,0:T(8,128)(2,1)S(1)}, bf16[400,128]{1,0:T(8,128)(2,1)S(1)}) custom-call(s32[4,4]{1,0:T(4,128)S(1)} %copy-done.4, bf16[2320,128]{1,0:T(8,128)(2,1)S(1)} %get-tuple-element.33.refs_1_.refs_5_, bf16[2320,128]{1,0:T(8,128)(2,1)S(1)} %collective-permute-done.refs_2_.refs_6_, ...), custom_call_target="tpu_custom_call" | custom-call | flops 2097152000 | bytes 3932160 | tf_op jit(solution)/shard_map/attend/pallas_call | solution.py:157
  42.6 1.7 %collective-permute-start.7 = (bf16[400,128]{1,0:T(8,128)(2,1)S(1)}, bf16[400,128]{1,0:T(8,128)(2,1)S(1)}, u32[]{:S(2)}, u32[]{:S(2)}) collective-permute-start(bf16[400,128]{1,0:T(8,128)(2,1)S(1)} %get-tuple-element.38), channel_id=1, source_target_pairs={{0,8},{8,0},{16,24},{24,16},{1,9},{9,1},{17,25},{25,17},{2,10},{10... | collective-permute-start | bytes 307208 | tf_op jit(solution)/shard_map/ppermute | solution.py:271
  46.1 6.2 %attend.3 = (bf16[400,128]{1,0:T(8,128)(2,1)S(1)}, bf16[400,128]{1,0:T(8,128)(2,1)S(1)}, bf16[400,128]{1,0:T(8,128)(2,1)S(1)}, bf16[400,128]{1,0:T(8,128)(2,1)S(1)}) custom-call(s32[4,4]{1,0:T(4,128)S(1)} %copy-done.4, bf16[400,128]{1,0:T(8,128)(2,1)S(1)} %get-tuple-element.44.refs_1_, bf16[400,128]{1,0:T(8,128)(2,1)S(1)} %collective-permute-done.10.refs_2_, ...), custom_call_target="tpu_custom_call" | custom-call | flops 2097152000 | bytes 3932160 | tf_op jit(solution)/shard_map/attend/pallas_call | solution.py:157
  53.1 3.7 %collective-permute-start.13 = (bf16[160,1280]{1,0:T(8,128)(2,1)S(1)}, bf16[160,1280]{1,0:T(8,128)(2,1)S(1)}, u32[]{:S(2)}, u32[]{:S(2)}) collective-permute-start(bf16[160,1280]{1,0:T(8,128)(2,1)S(1)} %project.5), channel_id=1, source_target_pairs={{0,1},{3,2},{4,5},{7,6},{8,9},{11,10},{12,13},{15,14},{16,17},{19,... | collective-permute-start | bytes 1228808 | tf_op jit(solution)/shard_map/ppermute | solution.py:240
  56.8 1.6 %collective-permute-start.18 = (bf16[400,128]{1,0:T(8,128)(2,1)S(1)}, bf16[400,128]{1,0:T(8,128)(2,1)S(1)}, u32[]{:S(2)}, u32[]{:S(2)}) collective-permute-start(bf16[400,128]{1,0:T(8,128)(2,1)S(1)} %get-tuple-element.54), channel_id=1, source_target_pairs={{0,8},{8,0},{16,24},{24,16},{1,9},{9,1},{17,25},{25,17},{2,10},{10... | collective-permute-start | bytes 307208 | tf_op jit(solution)/shard_map/ppermute | solution.py:271
  60.4 2.4 %project.4 = (bf16[160,1280]{1,0:T(8,128)(2,1)S(1)}, bf16[160,1280]{1,0:T(8,128)(2,1)S(1)}, bf16[160,1280]{1,0:T(8,128)(2,1)S(1)}, bf16[160,1280]{1,0:T(8,128)(2,1)S(1)}) custom-call(bf16[400,128]{1,0:T(8,128)(2,1)S(1)} %get-tuple-element.37.refs_0_, bf16[400,128]{1,0:T(8,128)(2,1)S(1)} %collective-permute-done.7.refs_1_, ...), custom_call_target="tpu_custom_call" | custom-call | flops 2097152000 | bytes 13107200 | tf_op jit(solution)/shard_map/project/pallas_call | solution.py:224
  63.0 1.9 %collective-permute-done.20.refs_3_ = bf16[400,128]{1,0:T(8,128)(2,1)S(1)} collective-permute-done((bf16[400,128]{1,0:T(8,128)(2,1)S(1)}, bf16[400,128]{1,0:T(8,128)(2,1)S(1)}, u32[]{:S(2)}, u32[]{:S(2)}) %collective-permute-start.20) | collective-permute-done | bytes 102432 | tf_op jit(solution)/shard_map/ppermute | solution.py:271
  65.7 1.3 %collective-permute-start.21 = (bf16[160,1280]{1,0:T(8,128)(2,1)S(1)}, bf16[160,1280]{1,0:T(8,128)(2,1)S(1)}, u32[]{:S(2)}, u32[]{:S(2)}) collective-permute-start(bf16[160,1280]{1,0:T(8,128)(2,1)S(1)} %project.7), channel_id=1, source_target_pairs={{0,1},{3,2},{4,5},{7,6},{8,9},{11,10},{12,13},{15,14},{16,17},{19,... | collective-permute-start | bytes 1228808 | tf_op jit(solution)/shard_map/ppermute | solution.py:240
  67.8 2.0 %collective-permute-start.14 = (bf16[160,1280]{1,0:T(8,128)(2,1)S(1)}, bf16[160,1280]{1,0:T(8,128)(2,1)S(1)}, u32[]{:S(2)}, u32[]{:S(2)}) collective-permute-start(bf16[160,1280]{1,0:T(8,128)(2,1)S(1)} %add.30), channel_id=1, source_target_pairs={{0,1},{1,2},{4,5},{5,6},{8,9},{9,10},{12,13},{13,14},{16,17},{17,1... | collective-permute-start | bytes 1228808 | tf_op jit(solution)/shard_map/ppermute | solution.py:255
  69.9 2.4 %project.6 = (bf16[160,1280]{1,0:T(8,128)(2,1)S(1)}, bf16[160,1280]{1,0:T(8,128)(2,1)S(1)}, bf16[160,1280]{1,0:T(8,128)(2,1)S(1)}, bf16[160,1280]{1,0:T(8,128)(2,1)S(1)}) custom-call(bf16[400,128]{1,0:T(8,128)(2,1)S(1)} %get-tuple-element.53.refs_5_.refs_0_, bf16[400,128]{1,0:T(8,128)(2,1)S(1)} %collective-permute-done.18.refs_1_, ...), custom_call_target="tpu_custom_call" | custom-call | flops 2097152000 | bytes 13107200 | tf_op jit(solution)/shard_map/project/pallas_call | solution.py:224
  72.3 4.6 %collective-permute-done.21 = bf16[160,1280]{1,0:T(8,128)(2,1)S(1)} collective-permute-done((bf16[160,1280]{1,0:T(8,128)(2,1)S(1)}, bf16[160,1280]{1,0:T(8,128)(2,1)S(1)}, u32[]{:S(2)}, u32[]{:S(2)}) %collective-permute-start.21) | collective-permute-done | bytes 409632 | tf_op jit(solution)/shard_map/ppermute | solution.py:240
  77.7 5.0 %collective-permute-start.22 = (bf16[160,1280]{1,0:T(8,128)(2,1)S(1)}, bf16[160,1280]{1,0:T(8,128)(2,1)S(1)}, u32[]{:S(2)}, u32[]{:S(2)}) collective-permute-start(bf16[160,1280]{1,0:T(8,128)(2,1)S(1)} %add.35), channel_id=1, source_target_pairs={{0,1},{1,2},{4,5},{5,6},{8,9},{9,10},{12,13},{13,14},{16,17},{17,1... | collective-permute-start | bytes 1228808 | tf_op jit(solution)/shard_map/ppermute | solution.py:255
  84.2 1.5 %collective-permute-done.14 = bf16[160,1280]{1,0:T(8,128)(2,1)S(1)} collective-permute-done((bf16[160,1280]{1,0:T(8,128)(2,1)S(1)}, bf16[160,1280]{1,0:T(8,128)(2,1)S(1)}, u32[]{:S(2)}, u32[]{:S(2)}) %collective-permute-start.14) | collective-permute-done | bytes 409632 | tf_op jit(solution)/shard_map/ppermute | solution.py:255
  85.8 4.4 %collective-permute-start.15 = (bf16[160,1280]{1,0:T(8,128)(2,1)S(1)}, bf16[160,1280]{1,0:T(8,128)(2,1)S(1)}, u32[]{:S(2)}, u32[]{:S(2)}) collective-permute-start(bf16[160,1280]{1,0:T(8,128)(2,1)S(1)} %add.31), channel_id=1, source_target_pairs={{0,1},{1,2},{2,3},{4,5},{5,6},{6,7},{8,9},{9,10},{10,11},{12,13},{... | collective-permute-start | bytes 1228808 | tf_op jit(solution)/shard_map/ppermute | solution.py:255
  90.3 1.3 %collective-permute-start.25 = (bf16[160,1280]{1,0:T(8,128)(2,1)S(1)}, bf16[160,1280]{1,0:T(8,128)(2,1)S(1)}, u32[]{:S(2)}, u32[]{:S(2)}) collective-permute-start(bf16[160,1280]{1,0:T(8,128)(2,1)S(1)} %add.38), channel_id=1, source_target_pairs={{3,2},{2,1},{1,0},{7,6},{6,5},{5,4},{11,10},{10,9},{9,8},{15,14},{... | collective-permute-start | bytes 1228808 | tf_op jit(solution)/shard_map/ppermute | solution.py:256
  91.6 2.8 %collective-permute-done.22 = bf16[160,1280]{1,0:T(8,128)(2,1)S(1)} collective-permute-done((bf16[160,1280]{1,0:T(8,128)(2,1)S(1)}, bf16[160,1280]{1,0:T(8,128)(2,1)S(1)}, u32[]{:S(2)}, u32[]{:S(2)}) %collective-permute-start.22) | collective-permute-done | bytes 409632 | tf_op jit(solution)/shard_map/ppermute | solution.py:255
  94.6 4.4 %collective-permute-start.23 = (bf16[160,1280]{1,0:T(8,128)(2,1)S(1)}, bf16[160,1280]{1,0:T(8,128)(2,1)S(1)}, u32[]{:S(2)}, u32[]{:S(2)}) collective-permute-start(bf16[160,1280]{1,0:T(8,128)(2,1)S(1)} %add.36), channel_id=1, source_target_pairs={{0,1},{1,2},{2,3},{4,5},{5,6},{6,7},{8,9},{9,10},{10,11},{12,13},{... | collective-permute-start | bytes 1228808 | tf_op jit(solution)/shard_map/ppermute | solution.py:255
  99.0 4.2 %collective-permute-done.15 = bf16[160,1280]{1,0:T(8,128)(2,1)S(1)} collective-permute-done((bf16[160,1280]{1,0:T(8,128)(2,1)S(1)}, bf16[160,1280]{1,0:T(8,128)(2,1)S(1)}, u32[]{:S(2)}, u32[]{:S(2)}) %collective-permute-start.15) | collective-permute-done | bytes 409632 | tf_op jit(solution)/shard_map/ppermute | solution.py:255
  103.3 4.7 %collective-permute-done.23 = bf16[160,1280]{1,0:T(8,128)(2,1)S(1)} collective-permute-done((bf16[160,1280]{1,0:T(8,128)(2,1)S(1)}, bf16[160,1280]{1,0:T(8,128)(2,1)S(1)}, u32[]{:S(2)}, u32[]{:S(2)}) %collective-permute-start.23) | collective-permute-done | bytes 409632 | tf_op jit(solution)/shard_map/ppermute | solution.py:255
  (59 shorter events, 13.7 us)
Async XLA Ops:
  2.2 18.5 %collective-permute-start.2 = (bf16[2320,128]{1,0:T(8,128)(2,1)}, bf16[2320,128]{1,0:T(8,128)(2,1)S(1)}, u32[]{:S(2)}, u32[]{:S(2)}) collective-permute-start(bf16[2320,128]{1,0:T(8,128)(2,1)} %get-tuple-element.36), channel_id=1, source_target_pairs={{0,24},{8,16},{16,8},{24,0},{1,25},{9,17},{17,9},{25,1},{2,26},{10... | collective-permute-start | bytes 1781768 | tf_op jit(solution)/shard_map/ppermute | solution.py:271
  6.5 26.1 %collective-permute-start.1 = (bf16[2320,128]{1,0:T(8,128)(2,1)S(1)}, bf16[2320,128]{1,0:T(8,128)(2,1)S(1)}, u32[]{:S(2)}, u32[]{:S(2)}) collective-permute-start(bf16[2320,128]{1,0:T(8,128)(2,1)S(1)} %get-tuple-element.35), channel_id=1, source_target_pairs={{0,16},{8,24},{16,0},{24,8},{1,17},{9,25},{17,1},{25,9},{2,18},{10... | collective-permute-start | bytes 1781768 | tf_op jit(solution)/shard_map/ppermute | solution.py:271
  7.4 25.5 %collective-permute-start = (bf16[2320,128]{1,0:T(8,128)(2,1)S(1)}, bf16[2320,128]{1,0:T(8,128)(2,1)S(1)}, u32[]{:S(2)}, u32[]{:S(2)}) collective-permute-start(bf16[2320,128]{1,0:T(8,128)(2,1)S(1)} %get-tuple-element.34), channel_id=1, source_target_pairs={{0,8},{8,0},{16,24},{24,16},{1,9},{9,1},{17,25},{25,17},{2,10},{10... | collective-permute-start | bytes 1781768 | tf_op jit(solution)/shard_map/ppermute | solution.py:271
  7.8 27.2 %collective-permute-start.3 = (bf16[2320,128]{1,0:T(8,128)(2,1)S(1)}, bf16[2320,128]{1,0:T(8,128)(2,1)S(1)}, u32[]{:S(2)}, u32[]{:S(2)}) collective-permute-start(bf16[2320,128]{1,0:T(8,128)(2,1)S(1)} %get-tuple-element.33.refs_1_.refs_5_), channel_id=1, source_target_pairs={{0,4},{4,0},{1,5},{5,1},{2,6},{6,2},{3,7},{7,3},{8,12},{12,8},{9,1... | collective-permute-start | bytes 1781768 | tf_op jit(solution)/shard_map/ppermute | solution.py:275
  20.7 15.5 %collective-permute-start.6 = (bf16[2320,128]{1,0:T(8,128)(2,1)S(1)}, bf16[2320,128]{1,0:T(8,128)(2,1)S(1)}, u32[]{:S(2)}, u32[]{:S(2)}) collective-permute-start(bf16[2320,128]{1,0:T(8,128)(2,1)S(1)} %collective-permute-done.2.refs_4_.refs_8_), channel_id=1, source_target_pairs={{0,4},{4,0},{1,5},{5,1},{2,6},{6,2},{3,7},{7,3},{8,12},{12,8},{9,1... | collective-permute-start | bytes 1781768 | tf_op jit(solution)/shard_map/ppermute | solution.py:275
  33.1 12.1 %collective-permute-start.12 = (bf16[400,128]{1,0:T(8,128)(2,1)S(1)}, bf16[400,128]{1,0:T(8,128)(2,1)S(1)}, u32[]{:S(2)}, u32[]{:S(2)}) collective-permute-start(bf16[400,128]{1,0:T(8,128)(2,1)S(1)} %copy-done.5), channel_id=1, source_target_pairs={{0,24},{8,16},{16,8},{24,0},{1,25},{9,17},{17,9},{25,1},{2,26},{10... | collective-permute-start | bytes 307208 | tf_op jit(solution)/shard_map/ppermute | solution.py:271
  35.0 11.1 %collective-permute-start.11 = (bf16[400,128]{1,0:T(8,128)(2,1)S(1)}, bf16[400,128]{1,0:T(8,128)(2,1)S(1)}, u32[]{:S(2)}, u32[]{:S(2)}) collective-permute-start(bf16[400,128]{1,0:T(8,128)(2,1)S(1)} %get-tuple-element.46), channel_id=1, source_target_pairs={{0,16},{8,24},{16,0},{24,8},{1,17},{9,25},{17,1},{25,9},{2,18},{10... | collective-permute-start | bytes 307208 | tf_op jit(solution)/shard_map/ppermute | solution.py:271
  36.2 9.9 %collective-permute-start.10 = (bf16[400,128]{1,0:T(8,128)(2,1)S(1)}, bf16[400,128]{1,0:T(8,128)(2,1)S(1)}, u32[]{:S(2)}, u32[]{:S(2)}) collective-permute-start(bf16[400,128]{1,0:T(8,128)(2,1)S(1)} %get-tuple-element.45), channel_id=1, source_target_pairs={{0,8},{8,0},{16,24},{24,16},{1,9},{9,1},{17,25},{25,17},{2,10},{10... | collective-permute-start | bytes 307208 | tf_op jit(solution)/shard_map/ppermute | solution.py:271
  42.6 9.7 %collective-permute-start.7 = (bf16[400,128]{1,0:T(8,128)(2,1)S(1)}, bf16[400,128]{1,0:T(8,128)(2,1)S(1)}, u32[]{:S(2)}, u32[]{:S(2)}) collective-permute-start(bf16[400,128]{1,0:T(8,128)(2,1)S(1)} %get-tuple-element.38), channel_id=1, source_target_pairs={{0,8},{8,0},{16,24},{24,16},{1,9},{9,1},{17,25},{25,17},{2,10},{10... | collective-permute-start | bytes 307208 | tf_op jit(solution)/shard_map/ppermute | solution.py:271
  44.3 8.0 %collective-permute-start.8 = (bf16[400,128]{1,0:T(8,128)(2,1)S(1)}, bf16[400,128]{1,0:T(8,128)(2,1)S(1)}, u32[]{:S(2)}, u32[]{:S(2)}) collective-permute-start(bf16[400,128]{1,0:T(8,128)(2,1)S(1)} %get-tuple-element.39), channel_id=1, source_target_pairs={{0,16},{8,24},{16,0},{24,8},{1,17},{9,25},{17,1},{25,9},{2,18},{10... | collective-permute-start | bytes 307208 | tf_op jit(solution)/shard_map/ppermute | solution.py:271
  45.1 7.2 %collective-permute-start.9 = (bf16[400,128]{1,0:T(8,128)(2,1)S(1)}, bf16[400,128]{1,0:T(8,128)(2,1)S(1)}, u32[]{:S(2)}, u32[]{:S(2)}) collective-permute-start(bf16[400,128]{1,0:T(8,128)(2,1)S(1)} %get-tuple-element.40), channel_id=1, source_target_pairs={{0,24},{8,16},{16,8},{24,0},{1,25},{9,17},{17,9},{25,1},{2,26},{10... | collective-permute-start | bytes 307208 | tf_op jit(solution)/shard_map/ppermute | solution.py:271
  53.1 13.9 %collective-permute-start.13 = (bf16[160,1280]{1,0:T(8,128)(2,1)S(1)}, bf16[160,1280]{1,0:T(8,128)(2,1)S(1)}, u32[]{:S(2)}, u32[]{:S(2)}) collective-permute-start(bf16[160,1280]{1,0:T(8,128)(2,1)S(1)} %project.5), channel_id=1, source_target_pairs={{0,1},{3,2},{4,5},{7,6},{8,9},{11,10},{12,13},{15,14},{16,17},{19,... | collective-permute-start | bytes 1228808 | tf_op jit(solution)/shard_map/ppermute | solution.py:240
  56.8 6.0 %collective-permute-start.18 = (bf16[400,128]{1,0:T(8,128)(2,1)S(1)}, bf16[400,128]{1,0:T(8,128)(2,1)S(1)}, u32[]{:S(2)}, u32[]{:S(2)}) collective-permute-start(bf16[400,128]{1,0:T(8,128)(2,1)S(1)} %get-tuple-element.54), channel_id=1, source_target_pairs={{0,8},{8,0},{16,24},{24,16},{1,9},{9,1},{17,25},{25,17},{2,10},{10... | collective-permute-start | bytes 307208 | tf_op jit(solution)/shard_map/ppermute | solution.py:271
  58.4 4.7 %collective-permute-start.19 = (bf16[400,128]{1,0:T(8,128)(2,1)S(1)}, bf16[400,128]{1,0:T(8,128)(2,1)S(1)}, u32[]{:S(2)}, u32[]{:S(2)}) collective-permute-start(bf16[400,128]{1,0:T(8,128)(2,1)S(1)} %get-tuple-element.55), channel_id=1, source_target_pairs={{0,16},{8,24},{16,0},{24,8},{1,17},{9,25},{17,1},{25,9},{2,18},{10... | collective-permute-start | bytes 307208 | tf_op jit(solution)/shard_map/ppermute | solution.py:271
  59.4 5.6 %collective-permute-start.20 = (bf16[400,128]{1,0:T(8,128)(2,1)S(1)}, bf16[400,128]{1,0:T(8,128)(2,1)S(1)}, u32[]{:S(2)}, u32[]{:S(2)}) collective-permute-start(bf16[400,128]{1,0:T(8,128)(2,1)S(1)} %get-tuple-element.56), channel_id=1, source_target_pairs={{0,24},{8,16},{16,8},{24,0},{1,25},{9,17},{17,9},{25,1},{2,26},{10... | collective-permute-start | bytes 307208 | tf_op jit(solution)/shard_map/ppermute | solution.py:271
  65.7 11.2 %collective-permute-start.21 = (bf16[160,1280]{1,0:T(8,128)(2,1)S(1)}, bf16[160,1280]{1,0:T(8,128)(2,1)S(1)}, u32[]{:S(2)}, u32[]{:S(2)}) collective-permute-start(bf16[160,1280]{1,0:T(8,128)(2,1)S(1)} %project.7), channel_id=1, source_target_pairs={{0,1},{3,2},{4,5},{7,6},{8,9},{11,10},{12,13},{15,14},{16,17},{19,... | collective-permute-start | bytes 1228808 | tf_op jit(solution)/shard_map/ppermute | solution.py:240
  67.2 15.6 %collective-permute-start.16 = (bf16[160,1280]{1,0:T(8,128)(2,1)S(1)}, bf16[160,1280]{1,0:T(8,128)(2,1)S(1)}, u32[]{:S(2)}, u32[]{:S(2)}) collective-permute-start(bf16[160,1280]{1,0:T(8,128)(2,1)S(1)} %add.30), channel_id=1, source_target_pairs={{3,2},{2,1},{7,6},{6,5},{11,10},{10,9},{15,14},{14,13},{19,18},{18... | collective-permute-start | bytes 1228808 | tf_op jit(solution)/shard_map/ppermute | solution.py:256
  67.8 17.8 %collective-permute-start.14 = (bf16[160,1280]{1,0:T(8,128)(2,1)S(1)}, bf16[160,1280]{1,0:T(8,128)(2,1)S(1)}, u32[]{:S(2)}, u32[]{:S(2)}) collective-permute-start(bf16[160,1280]{1,0:T(8,128)(2,1)S(1)} %add.30), channel_id=1, source_target_pairs={{0,1},{1,2},{4,5},{5,6},{8,9},{9,10},{12,13},{13,14},{16,17},{17,1... | collective-permute-start | bytes 1228808 | tf_op jit(solution)/shard_map/ppermute | solution.py:255
  77.0 13.2 %collective-permute-start.24 = (bf16[160,1280]{1,0:T(8,128)(2,1)S(1)}, bf16[160,1280]{1,0:T(8,128)(2,1)S(1)}, u32[]{:S(2)}, u32[]{:S(2)}) collective-permute-start(bf16[160,1280]{1,0:T(8,128)(2,1)S(1)} %add.35), channel_id=1, source_target_pairs={{3,2},{2,1},{7,6},{6,5},{11,10},{10,9},{15,14},{14,13},{19,18},{18... | collective-permute-start | bytes 1228808 | tf_op jit(solution)/shard_map/ppermute | solution.py:256
  77.7 16.8 %collective-permute-start.22 = (bf16[160,1280]{1,0:T(8,128)(2,1)S(1)}, bf16[160,1280]{1,0:T(8,128)(2,1)S(1)}, u32[]{:S(2)}, u32[]{:S(2)}) collective-permute-start(bf16[160,1280]{1,0:T(8,128)(2,1)S(1)} %add.35), channel_id=1, source_target_pairs={{0,1},{1,2},{4,5},{5,6},{8,9},{9,10},{12,13},{13,14},{16,17},{17,1... | collective-permute-start | bytes 1228808 | tf_op jit(solution)/shard_map/ppermute | solution.py:255
  82.9 16.1 %collective-permute-start.17 = (bf16[160,1280]{1,0:T(8,128)(2,1)S(1)}, bf16[160,1280]{1,0:T(8,128)(2,1)S(1)}, u32[]{:S(2)}, u32[]{:S(2)}) collective-permute-start(bf16[160,1280]{1,0:T(8,128)(2,1)S(1)} %add.33), channel_id=1, source_target_pairs={{3,2},{2,1},{1,0},{7,6},{6,5},{5,4},{11,10},{10,9},{9,8},{15,14},{... | collective-permute-start | bytes 1228808 | tf_op jit(solution)/shard_map/ppermute | solution.py:256
  85.8 17.5 %collective-permute-start.15 = (bf16[160,1280]{1,0:T(8,128)(2,1)S(1)}, bf16[160,1280]{1,0:T(8,128)(2,1)S(1)}, u32[]{:S(2)}, u32[]{:S(2)}) collective-permute-start(bf16[160,1280]{1,0:T(8,128)(2,1)S(1)} %add.31), channel_id=1, source_target_pairs={{0,1},{1,2},{2,3},{4,5},{5,6},{6,7},{8,9},{9,10},{10,11},{12,13},{... | collective-permute-start | bytes 1228808 | tf_op jit(solution)/shard_map/ppermute | solution.py:255
  90.3 13.0 %collective-permute-start.25 = (bf16[160,1280]{1,0:T(8,128)(2,1)S(1)}, bf16[160,1280]{1,0:T(8,128)(2,1)S(1)}, u32[]{:S(2)}, u32[]{:S(2)}) collective-permute-start(bf16[160,1280]{1,0:T(8,128)(2,1)S(1)} %add.38), channel_id=1, source_target_pairs={{3,2},{2,1},{1,0},{7,6},{6,5},{5,4},{11,10},{10,9},{9,8},{15,14},{... | collective-permute-start | bytes 1228808 | tf_op jit(solution)/shard_map/ppermute | solution.py:256
  94.6 13.5 %collective-permute-start.23 = (bf16[160,1280]{1,0:T(8,128)(2,1)S(1)}, bf16[160,1280]{1,0:T(8,128)(2,1)S(1)}, u32[]{:S(2)}, u32[]{:S(2)}) collective-permute-start(bf16[160,1280]{1,0:T(8,128)(2,1)S(1)} %add.36), channel_id=1, source_target_pairs={{0,1},{1,2},{2,3},{4,5},{5,6},{6,7},{8,9},{9,10},{10,11},{12,13},{... | collective-permute-start | bytes 1228808 | tf_op jit(solution)/shard_map/ppermute | solution.py:255
  (8 other events, 97.1 us)

commit v5 on v4

--- a/solution.py
+++ b/solution.py
@@ -125,9 +125,9 @@
     tiles = [(unit, pair) for unit in range(full * rows_part + 1) for pair in pairs]
     scores, last = score(tiles[0]), None
     for i, tile in enumerate(tiles):
-        following = score(tiles[i + 1]) if i + 1 < len(tiles) else None
         if last is not None:
             gather(*last)
+        following = score(tiles[i + 1]) if i + 1 < len(tiles) else None
         last = (tile, weigh(tile, scores))
         scores = following
     gather(*last)

time: 109 us -> 109 us (level)
  no operation moved by 1% of the time
where the time goes in v5:
time: 109 us
  waiting for transfers between devices  45 us (41%)
  starting transfers between devices  40.5 us (37%)
  Pallas kernels  21.2 us (19%)
  other arithmetic  1.65 us (2%)
    ppermute x12, waiting for transfers between devices, swap(): lax.ppermute(x, 'tm', [(i, i ^ m) for i in range(partners)])  27.1 us
    ppermute x4, starting transfers between devices, finish_sums(): lax.ppermute(right, axis, [(i, i + 1) for i in range(step)])  15.9 us
    ppermute x12, starting transfers between devices, swap(): lax.ppermute(x, 'tm', [(i, i ^ m) for i in range(partners)])  15.3 us
    ppermute x4, waiting for transfers between devices, finish_sums(): lax.ppermute(right, axis, [(i, i + 1) for i in range(step)])  13.3 us
    pallas_call x2, Pallas kernels, attend(): pl.pallas_call(kernel, out_shape=[jax.ShapeDtypeStruct((rows_out, HD), jn...  11.6 us
    pallas_call x4, Pallas kernels, project(): pl.pallas_call(kernel, out_shape=[jax.ShapeDtypeStruct((part, width // si...  6.56 us
    ppermute x2, starting transfers between devices, begin_sums(): come = lax.ppermute(shares[0], axis, [(0, 1), (size - 1, size - 2)])  4.99 us
    ppermute x2, waiting for transfers between devices, begin_sums(): come = lax.ppermute(shares[0], axis, [(0, 1), (size - 1, size - 2)])  4.58 us
  transfers between devices with their start and end apart: 26, of which 10 were waited for; matrix products, arithmetic and copies ran while one was open for 1% of the time, Pallas kernels for 17%

profile of v5, /device:TPU:0, one launch (start us, length us, event | category | flops | bytes accessed | tf_op | source)
XLA Modules:
  0.0 108.7 jit_solution(514782419447954692)
XLA Ops:
  0.0 2.2 %pack.7 = (bf16[2320,128]{1,0:T(8,128)(2,1)}, bf16[400,128]{1,0:T(8,128)(2,1)}) custom-call(bf16[320,1280]{1,0:T(8,128)(2,1)} %bitcast.4, bf16[320,1280]{1,0:T(8,128)(2,1)} %bitcast.8, bf16[320,1280]{1,0:T(8,128)(2,1)} %bitcast.12), custom_call_target="tpu_custom_call" | custom-call | tf_op jit(solution)/shard_map/pack/pallas_call | solution.py:55
  2.2 4.0 %collective-permute-start.2 = (bf16[2320,128]{1,0:T(8,128)(2,1)}, bf16[2320,128]{1,0:T(8,128)(2,1)S(1)}, u32[]{:S(2)}, u32[]{:S(2)}) collective-permute-start(bf16[2320,128]{1,0:T(8,128)(2,1)} %get-tuple-element.36), channel_id=1, source_target_pairs={{0,24},{8,16},{16,8},{24,0},{1,25},{9,17},{17,9},{25,1},{2,26},{10... | collective-permute-start | bytes 1781768 | tf_op jit(solution)/shard_map/ppermute | solution.py:271
  7.9 12.8 %collective-permute-done.2.refs_4_.refs_8_ = bf16[2320,128]{1,0:T(8,128)(2,1)S(1)} collective-permute-done((bf16[2320,128]{1,0:T(8,128)(2,1)}, bf16[2320,128]{1,0:T(8,128)(2,1)S(1)}, u32[]{:S(2)}, u32[]{:S(2)}) %collective-permute-start.2) | collective-permute-done | bytes 593952 | tf_op jit(solution)/shard_map/ppermute | solution.py:271
  20.7 11.9 %collective-permute-done.1.refs_3_.refs_7_ = bf16[2320,128]{1,0:T(8,128)(2,1)S(1)} collective-permute-done((bf16[2320,128]{1,0:T(8,128)(2,1)S(1)}, bf16[2320,128]{1,0:T(8,128)(2,1)S(1)}, u32[]{:S(2)}, u32[]{:S(2)}) %collective-permute-start.1) | collective-permute-done | bytes 593952 | tf_op jit(solution)/shard_map/ppermute | solution.py:271
  33.1 1.9 %collective-permute-start.12 = (bf16[400,128]{1,0:T(8,128)(2,1)S(1)}, bf16[400,128]{1,0:T(8,128)(2,1)S(1)}, u32[]{:S(2)}, u32[]{:S(2)}) collective-permute-start(bf16[400,128]{1,0:T(8,128)(2,1)S(1)} %copy-done.5), channel_id=1, source_target_pairs={{0,24},{8,16},{16,8},{24,0},{1,25},{9,17},{17,9},{25,1},{2,26},{10... | collective-permute-start | bytes 307208 | tf_op jit(solution)/shard_map/ppermute | solution.py:271
  36.6 5.8 %attend.2 = (bf16[400,128]{1,0:T(8,128)(2,1)S(1)}, bf16[400,128]{1,0:T(8,128)(2,1)S(1)}, bf16[400,128]{1,0:T(8,128)(2,1)S(1)}, bf16[400,128]{1,0:T(8,128)(2,1)S(1)}) custom-call(s32[4,4]{1,0:T(4,128)S(1)} %copy-done.4, bf16[2320,128]{1,0:T(8,128)(2,1)S(1)} %get-tuple-element.33.refs_1_.refs_5_, bf16[2320,128]{1,0:T(8,128)(2,1)S(1)} %collective-permute-done.refs_2_.refs_6_, ...), custom_call_target="tpu_custom_call" | custom-call | flops 2097152000 | bytes 3932160 | tf_op jit(solution)/shard_map/attend/pallas_call | solution.py:157
  42.4 1.7 %collective-permute-start.7 = (bf16[400,128]{1,0:T(8,128)(2,1)S(1)}, bf16[400,128]{1,0:T(8,128)(2,1)S(1)}, u32[]{:S(2)}, u32[]{:S(2)}) collective-permute-start(bf16[400,128]{1,0:T(8,128)(2,1)S(1)} %get-tuple-element.38), channel_id=1, source_target_pairs={{0,8},{8,0},{16,24},{24,16},{1,9},{9,1},{17,25},{25,17},{2,10},{10... | collective-permute-start | bytes 307208 | tf_op jit(solution)/shard_map/ppermute | solution.py:271
  46.0 5.8 %attend.3 = (bf16[400,128]{1,0:T(8,128)(2,1)S(1)}, bf16[400,128]{1,0:T(8,128)(2,1)S(1)}, bf16[400,128]{1,0:T(8,128)(2,1)S(1)}, bf16[400,128]{1,0:T(8,128)(2,1)S(1)}) custom-call(s32[4,4]{1,0:T(4,128)S(1)} %copy-done.4, bf16[400,128]{1,0:T(8,128)(2,1)S(1)} %get-tuple-element.44.refs_1_, bf16[400,128]{1,0:T(8,128)(2,1)S(1)} %collective-permute-done.10.refs_2_, ...), custom_call_target="tpu_custom_call" | custom-call | flops 2097152000 | bytes 3932160 | tf_op jit(solution)/shard_map/attend/pallas_call | solution.py:157
  52.8 3.7 %collective-permute-start.13 = (bf16[160,1280]{1,0:T(8,128)(2,1)S(1)}, bf16[160,1280]{1,0:T(8,128)(2,1)S(1)}, u32[]{:S(2)}, u32[]{:S(2)}) collective-permute-start(bf16[160,1280]{1,0:T(8,128)(2,1)S(1)} %project.5), channel_id=1, source_target_pairs={{0,1},{3,2},{4,5},{7,6},{8,9},{11,10},{12,13},{15,14},{16,17},{19,... | collective-permute-start | bytes 1228808 | tf_op jit(solution)/shard_map/ppermute | solution.py:240
  56.5 1.6 %collective-permute-start.18 = (bf16[400,128]{1,0:T(8,128)(2,1)S(1)}, bf16[400,128]{1,0:T(8,128)(2,1)S(1)}, u32[]{:S(2)}, u32[]{:S(2)}) collective-permute-start(bf16[400,128]{1,0:T(8,128)(2,1)S(1)} %get-tuple-element.54), channel_id=1, source_target_pairs={{0,8},{8,0},{16,24},{24,16},{1,9},{9,1},{17,25},{25,17},{2,10},{10... | collective-permute-start | bytes 307208 | tf_op jit(solution)/shard_map/ppermute | solution.py:271
  60.0 2.4 %project.4 = (bf16[160,1280]{1,0:T(8,128)(2,1)S(1)}, bf16[160,1280]{1,0:T(8,128)(2,1)S(1)}, bf16[160,1280]{1,0:T(8,128)(2,1)S(1)}, bf16[160,1280]{1,0:T(8,128)(2,1)S(1)}) custom-call(bf16[400,128]{1,0:T(8,128)(2,1)S(1)} %get-tuple-element.37.refs_0_, bf16[400,128]{1,0:T(8,128)(2,1)S(1)} %collective-permute-done.7.refs_1_, ...), custom_call_target="tpu_custom_call" | custom-call | flops 2097152000 | bytes 13107200 | tf_op jit(solution)/shard_map/project/pallas_call | solution.py:224
  62.7 1.9 %collective-permute-done.20.refs_3_ = bf16[400,128]{1,0:T(8,128)(2,1)S(1)} collective-permute-done((bf16[400,128]{1,0:T(8,128)(2,1)S(1)}, bf16[400,128]{1,0:T(8,128)(2,1)S(1)}, u32[]{:S(2)}, u32[]{:S(2)}) %collective-permute-start.20) | collective-permute-done | bytes 102432 | tf_op jit(solution)/shard_map/ppermute | solution.py:271
  65.4 1.3 %collective-permute-start.21 = (bf16[160,1280]{1,0:T(8,128)(2,1)S(1)}, bf16[160,1280]{1,0:T(8,128)(2,1)S(1)}, u32[]{:S(2)}, u32[]{:S(2)}) collective-permute-start(bf16[160,1280]{1,0:T(8,128)(2,1)S(1)} %project.7), channel_id=1, source_target_pairs={{0,1},{3,2},{4,5},{7,6},{8,9},{11,10},{12,13},{15,14},{16,17},{19,... | collective-permute-start | bytes 1228808 | tf_op jit(solution)/shard_map/ppermute | solution.py:240
  67.5 2.1 %collective-permute-start.14 = (bf16[160,1280]{1,0:T(8,128)(2,1)S(1)}, bf16[160,1280]{1,0:T(8,128)(2,1)S(1)}, u32[]{:S(2)}, u32[]{:S(2)}) collective-permute-start(bf16[160,1280]{1,0:T(8,128)(2,1)S(1)} %add.30), channel_id=1, source_target_pairs={{0,1},{1,2},{4,5},{5,6},{8,9},{9,10},{12,13},{13,14},{16,17},{17,1... | collective-permute-start | bytes 1228808 | tf_op jit(solution)/shard_map/ppermute | solution.py:255
  69.6 2.4 %project.6 = (bf16[160,1280]{1,0:T(8,128)(2,1)S(1)}, bf16[160,1280]{1,0:T(8,128)(2,1)S(1)}, bf16[160,1280]{1,0:T(8,128)(2,1)S(1)}, bf16[160,1280]{1,0:T(8,128)(2,1)S(1)}) custom-call(bf16[400,128]{1,0:T(8,128)(2,1)S(1)} %get-tuple-element.53.refs_5_.refs_0_, bf16[400,128]{1,0:T(8,128)(2,1)S(1)} %collective-permute-done.18.refs_1_, ...), custom_call_target="tpu_custom_call" | custom-call | flops 2097152000 | bytes 13107200 | tf_op jit(solution)/shard_map/project/pallas_call | solution.py:224
  72.0 4.6 %collective-permute-done.21 = bf16[160,1280]{1,0:T(8,128)(2,1)S(1)} collective-permute-done((bf16[160,1280]{1,0:T(8,128)(2,1)S(1)}, bf16[160,1280]{1,0:T(8,128)(2,1)S(1)}, u32[]{:S(2)}, u32[]{:S(2)}) %collective-permute-start.21) | collective-permute-done | bytes 409632 | tf_op jit(solution)/shard_map/ppermute | solution.py:240
  77.4 5.0 %collective-permute-start.22 = (bf16[160,1280]{1,0:T(8,128)(2,1)S(1)}, bf16[160,1280]{1,0:T(8,128)(2,1)S(1)}, u32[]{:S(2)}, u32[]{:S(2)}) collective-permute-start(bf16[160,1280]{1,0:T(8,128)(2,1)S(1)} %add.35), channel_id=1, source_target_pairs={{0,1},{1,2},{4,5},{5,6},{8,9},{9,10},{12,13},{13,14},{16,17},{17,1... | collective-permute-start | bytes 1228808 | tf_op jit(solution)/shard_map/ppermute | solution.py:255
  82.5 1.3 %collective-permute-start.17 = (bf16[160,1280]{1,0:T(8,128)(2,1)S(1)}, bf16[160,1280]{1,0:T(8,128)(2,1)S(1)}, u32[]{:S(2)}, u32[]{:S(2)}) collective-permute-start(bf16[160,1280]{1,0:T(8,128)(2,1)S(1)} %add.33), channel_id=1, source_target_pairs={{3,2},{2,1},{1,0},{7,6},{6,5},{5,4},{11,10},{10,9},{9,8},{15,14},{... | collective-permute-start | bytes 1228808 | tf_op jit(solution)/shard_map/ppermute | solution.py:256
  83.8 1.5 %collective-permute-done.14 = bf16[160,1280]{1,0:T(8,128)(2,1)S(1)} collective-permute-done((bf16[160,1280]{1,0:T(8,128)(2,1)S(1)}, bf16[160,1280]{1,0:T(8,128)(2,1)S(1)}, u32[]{:S(2)}, u32[]{:S(2)}) %collective-permute-start.14) | collective-permute-done | bytes 409632 | tf_op jit(solution)/shard_map/ppermute | solution.py:255
  85.4 4.4 %collective-permute-start.15 = (bf16[160,1280]{1,0:T(8,128)(2,1)S(1)}, bf16[160,1280]{1,0:T(8,128)(2,1)S(1)}, u32[]{:S(2)}, u32[]{:S(2)}) collective-permute-start(bf16[160,1280]{1,0:T(8,128)(2,1)S(1)} %add.31), channel_id=1, source_target_pairs={{0,1},{1,2},{2,3},{4,5},{5,6},{6,7},{8,9},{9,10},{10,11},{12,13},{... | collective-permute-start | bytes 1228808 | tf_op jit(solution)/shard_map/ppermute | solution.py:255
  91.3 2.8 %collective-permute-done.22 = bf16[160,1280]{1,0:T(8,128)(2,1)S(1)} collective-permute-done((bf16[160,1280]{1,0:T(8,128)(2,1)S(1)}, bf16[160,1280]{1,0:T(8,128)(2,1)S(1)}, u32[]{:S(2)}, u32[]{:S(2)}) %collective-permute-start.22) | collective-permute-done | bytes 409632 | tf_op jit(solution)/shard_map/ppermute | solution.py:255
  94.2 4.4 %collective-permute-start.23 = (bf16[160,1280]{1,0:T(8,128)(2,1)S(1)}, bf16[160,1280]{1,0:T(8,128)(2,1)S(1)}, u32[]{:S(2)}, u32[]{:S(2)}) collective-permute-start(bf16[160,1280]{1,0:T(8,128)(2,1)S(1)} %add.36), channel_id=1, source_target_pairs={{0,1},{1,2},{2,3},{4,5},{5,6},{6,7},{8,9},{9,10},{10,11},{12,13},{... | collective-permute-start | bytes 1228808 | tf_op jit(solution)/shard_map/ppermute | solution.py:255
  98.7 4.2 %collective-permute-done.15 = bf16[160,1280]{1,0:T(8,128)(2,1)S(1)} collective-permute-done((bf16[160,1280]{1,0:T(8,128)(2,1)S(1)}, bf16[160,1280]{1,0:T(8,128)(2,1)S(1)}, u32[]{:S(2)}, u32[]{:S(2)}) %collective-permute-start.15) | collective-permute-done | bytes 409632 | tf_op jit(solution)/shard_map/ppermute | solution.py:255
  103.0 4.7 %collective-permute-done.23 = bf16[160,1280]{1,0:T(8,128)(2,1)S(1)} collective-permute-done((bf16[160,1280]{1,0:T(8,128)(2,1)S(1)}, bf16[160,1280]{1,0:T(8,128)(2,1)S(1)}, u32[]{:S(2)}, u32[]{:S(2)}) %collective-permute-start.23) | collective-permute-done | bytes 409632 | tf_op jit(solution)/shard_map/ppermute | solution.py:255
  (59 shorter events, 13.9 us)
Async XLA Ops:
  2.2 18.5 %collective-permute-start.2 = (bf16[2320,128]{1,0:T(8,128)(2,1)}, bf16[2320,128]{1,0:T(8,128)(2,1)S(1)}, u32[]{:S(2)}, u32[]{:S(2)}) collective-permute-start(bf16[2320,128]{1,0:T(8,128)(2,1)} %get-tuple-element.36), channel_id=1, source_target_pairs={{0,24},{8,16},{16,8},{24,0},{1,25},{9,17},{17,9},{25,1},{2,26},{10... | collective-permute-start | bytes 1781768 | tf_op jit(solution)/shard_map/ppermute | solution.py:271
  6.5 26.1 %collective-permute-start.1 = (bf16[2320,128]{1,0:T(8,128)(2,1)S(1)}, bf16[2320,128]{1,0:T(8,128)(2,1)S(1)}, u32[]{:S(2)}, u32[]{:S(2)}) collective-permute-start(bf16[2320,128]{1,0:T(8,128)(2,1)S(1)} %get-tuple-element.35), channel_id=1, source_target_pairs={{0,16},{8,24},{16,0},{24,8},{1,17},{9,25},{17,1},{25,9},{2,18},{10... | collective-permute-start | bytes 1781768 | tf_op jit(solution)/shard_map/ppermute | solution.py:271
  7.4 25.5 %collective-permute-start = (bf16[2320,128]{1,0:T(8,128)(2,1)S(1)}, bf16[2320,128]{1,0:T(8,128)(2,1)S(1)}, u32[]{:S(2)}, u32[]{:S(2)}) collective-permute-start(bf16[2320,128]{1,0:T(8,128)(2,1)S(1)} %get-tuple-element.34), channel_id=1, source_target_pairs={{0,8},{8,0},{16,24},{24,16},{1,9},{9,1},{17,25},{25,17},{2,10},{10... | collective-permute-start | bytes 1781768 | tf_op jit(solution)/shard_map/ppermute | solution.py:271
  7.8 27.2 %collective-permute-start.3 = (bf16[2320,128]{1,0:T(8,128)(2,1)S(1)}, bf16[2320,128]{1,0:T(8,128)(2,1)S(1)}, u32[]{:S(2)}, u32[]{:S(2)}) collective-permute-start(bf16[2320,128]{1,0:T(8,128)(2,1)S(1)} %get-tuple-element.33.refs_1_.refs_5_), channel_id=1, source_target_pairs={{0,4},{4,0},{1,5},{5,1},{2,6},{6,2},{3,7},{7,3},{8,12},{12,8},{9,1... | collective-permute-start | bytes 1781768 | tf_op jit(solution)/shard_map/ppermute | solution.py:275
  20.7 15.5 %collective-permute-start.6 = (bf16[2320,128]{1,0:T(8,128)(2,1)S(1)}, bf16[2320,128]{1,0:T(8,128)(2,1)S(1)}, u32[]{:S(2)}, u32[]{:S(2)}) collective-permute-start(bf16[2320,128]{1,0:T(8,128)(2,1)S(1)} %collective-permute-done.2.refs_4_.refs_8_), channel_id=1, source_target_pairs={{0,4},{4,0},{1,5},{5,1},{2,6},{6,2},{3,7},{7,3},{8,12},{12,8},{9,1... | collective-permute-start | bytes 1781768 | tf_op jit(solution)/shard_map/ppermute | solution.py:275
  33.1 11.9 %collective-permute-start.12 = (bf16[400,128]{1,0:T(8,128)(2,1)S(1)}, bf16[400,128]{1,0:T(8,128)(2,1)S(1)}, u32[]{:S(2)}, u32[]{:S(2)}) collective-permute-start(bf16[400,128]{1,0:T(8,128)(2,1)S(1)} %copy-done.5), channel_id=1, source_target_pairs={{0,24},{8,16},{16,8},{24,0},{1,25},{9,17},{17,9},{25,1},{2,26},{10... | collective-permute-start | bytes 307208 | tf_op jit(solution)/shard_map/ppermute | solution.py:271
  35.0 11.0 %collective-permute-start.11 = (bf16[400,128]{1,0:T(8,128)(2,1)S(1)}, bf16[400,128]{1,0:T(8,128)(2,1)S(1)}, u32[]{:S(2)}, u32[]{:S(2)}) collective-permute-start(bf16[400,128]{1,0:T(8,128)(2,1)S(1)} %get-tuple-element.46), channel_id=1, source_target_pairs={{0,16},{8,24},{16,0},{24,8},{1,17},{9,25},{17,1},{25,9},{2,18},{10... | collective-permute-start | bytes 307208 | tf_op jit(solution)/shard_map/ppermute | solution.py:271
  36.2 9.8 %collective-permute-start.10 = (bf16[400,128]{1,0:T(8,128)(2,1)S(1)}, bf16[400,128]{1,0:T(8,128)(2,1)S(1)}, u32[]{:S(2)}, u32[]{:S(2)}) collective-permute-start(bf16[400,128]{1,0:T(8,128)(2,1)S(1)} %get-tuple-element.45), channel_id=1, source_target_pairs={{0,8},{8,0},{16,24},{24,16},{1,9},{9,1},{17,25},{25,17},{2,10},{10... | collective-permute-start | bytes 307208 | tf_op jit(solution)/shard_map/ppermute | solution.py:271
  42.4 9.4 %collective-permute-start.7 = (bf16[400,128]{1,0:T(8,128)(2,1)S(1)}, bf16[400,128]{1,0:T(8,128)(2,1)S(1)}, u32[]{:S(2)}, u32[]{:S(2)}) collective-permute-start(bf16[400,128]{1,0:T(8,128)(2,1)S(1)} %get-tuple-element.38), channel_id=1, source_target_pairs={{0,8},{8,0},{16,24},{24,16},{1,9},{9,1},{17,25},{25,17},{2,10},{10... | collective-permute-start | bytes 307208 | tf_op jit(solution)/shard_map/ppermute | solution.py:271
  44.2 7.6 %collective-permute-start.8 = (bf16[400,128]{1,0:T(8,128)(2,1)S(1)}, bf16[400,128]{1,0:T(8,128)(2,1)S(1)}, u32[]{:S(2)}, u32[]{:S(2)}) collective-permute-start(bf16[400,128]{1,0:T(8,128)(2,1)S(1)} %get-tuple-element.39), channel_id=1, source_target_pairs={{0,16},{8,24},{16,0},{24,8},{1,17},{9,25},{17,1},{25,9},{2,18},{10... | collective-permute-start | bytes 307208 | tf_op jit(solution)/shard_map/ppermute | solution.py:271
  45.0 6.8 %collective-permute-start.9 = (bf16[400,128]{1,0:T(8,128)(2,1)S(1)}, bf16[400,128]{1,0:T(8,128)(2,1)S(1)}, u32[]{:S(2)}, u32[]{:S(2)}) collective-permute-start(bf16[400,128]{1,0:T(8,128)(2,1)S(1)} %get-tuple-element.40), channel_id=1, source_target_pairs={{0,24},{8,16},{16,8},{24,0},{1,25},{9,17},{17,9},{25,1},{2,26},{10... | collective-permute-start | bytes 307208 | tf_op jit(solution)/shard_map/ppermute | solution.py:271
  52.8 13.9 %collective-permute-start.13 = (bf16[160,1280]{1,0:T(8,128)(2,1)S(1)}, bf16[160,1280]{1,0:T(8,128)(2,1)S(1)}, u32[]{:S(2)}, u32[]{:S(2)}) collective-permute-start(bf16[160,1280]{1,0:T(8,128)(2,1)S(1)} %project.5), channel_id=1, source_target_pairs={{0,1},{3,2},{4,5},{7,6},{8,9},{11,10},{12,13},{15,14},{16,17},{19,... | collective-permute-start | bytes 1228808 | tf_op jit(solution)/shard_map/ppermute | solution.py:240
  56.5 6.0 %collective-permute-start.18 = (bf16[400,128]{1,0:T(8,128)(2,1)S(1)}, bf16[400,128]{1,0:T(8,128)(2,1)S(1)}, u32[]{:S(2)}, u32[]{:S(2)}) collective-permute-start(bf16[400,128]{1,0:T(8,128)(2,1)S(1)} %get-tuple-element.54), channel_id=1, source_target_pairs={{0,8},{8,0},{16,24},{24,16},{1,9},{9,1},{17,25},{25,17},{2,10},{10... | collective-permute-start | bytes 307208 | tf_op jit(solution)/shard_map/ppermute | solution.py:271
  58.1 4.7 %collective-permute-start.19 = (bf16[400,128]{1,0:T(8,128)(2,1)S(1)}, bf16[400,128]{1,0:T(8,128)(2,1)S(1)}, u32[]{:S(2)}, u32[]{:S(2)}) collective-permute-start(bf16[400,128]{1,0:T(8,128)(2,1)S(1)} %get-tuple-element.55), channel_id=1, source_target_pairs={{0,16},{8,24},{16,0},{24,8},{1,17},{9,25},{17,1},{25,9},{2,18},{10... | collective-permute-start | bytes 307208 | tf_op jit(solution)/shard_map/ppermute | solution.py:271
  59.0 5.6 %collective-permute-start.20 = (bf16[400,128]{1,0:T(8,128)(2,1)S(1)}, bf16[400,128]{1,0:T(8,128)(2,1)S(1)}, u32[]{:S(2)}, u32[]{:S(2)}) collective-permute-start(bf16[400,128]{1,0:T(8,128)(2,1)S(1)} %get-tuple-element.56), channel_id=1, source_target_pairs={{0,24},{8,16},{16,8},{24,0},{1,25},{9,17},{17,9},{25,1},{2,26},{10... | collective-permute-start | bytes 307208 | tf_op jit(solution)/shard_map/ppermute | solution.py:271
  65.4 11.2 %collective-permute-start.21 = (bf16[160,1280]{1,0:T(8,128)(2,1)S(1)}, bf16[160,1280]{1,0:T(8,128)(2,1)S(1)}, u32[]{:S(2)}, u32[]{:S(2)}) collective-permute-start(bf16[160,1280]{1,0:T(8,128)(2,1)S(1)} %project.7), channel_id=1, source_target_pairs={{0,1},{3,2},{4,5},{7,6},{8,9},{11,10},{12,13},{15,14},{16,17},{19,... | collective-permute-start | bytes 1228808 | tf_op jit(solution)/shard_map/ppermute | solution.py:240
  66.8 15.6 %collective-permute-start.16 = (bf16[160,1280]{1,0:T(8,128)(2,1)S(1)}, bf16[160,1280]{1,0:T(8,128)(2,1)S(1)}, u32[]{:S(2)}, u32[]{:S(2)}) collective-permute-start(bf16[160,1280]{1,0:T(8,128)(2,1)S(1)} %add.30), channel_id=1, source_target_pairs={{3,2},{2,1},{7,6},{6,5},{11,10},{10,9},{15,14},{14,13},{19,18},{18... | collective-permute-start | bytes 1228808 | tf_op jit(solution)/shard_map/ppermute | solution.py:256
  67.5 17.8 %collective-permute-start.14 = (bf16[160,1280]{1,0:T(8,128)(2,1)S(1)}, bf16[160,1280]{1,0:T(8,128)(2,1)S(1)}, u32[]{:S(2)}, u32[]{:S(2)}) collective-permute-start(bf16[160,1280]{1,0:T(8,128)(2,1)S(1)} %add.30), channel_id=1, source_target_pairs={{0,1},{1,2},{4,5},{5,6},{8,9},{9,10},{12,13},{13,14},{16,17},{17,1... | collective-permute-start | bytes 1228808 | tf_op jit(solution)/shard_map/ppermute | solution.py:255
  76.7 13.2 %collective-permute-start.24 = (bf16[160,1280]{1,0:T(8,128)(2,1)S(1)}, bf16[160,1280]{1,0:T(8,128)(2,1)S(1)}, u32[]{:S(2)}, u32[]{:S(2)}) collective-permute-start(bf16[160,1280]{1,0:T(8,128)(2,1)S(1)} %add.35), channel_id=1, source_target_pairs={{3,2},{2,1},{7,6},{6,5},{11,10},{10,9},{15,14},{14,13},{19,18},{18... | collective-permute-start | bytes 1228808 | tf_op jit(solution)/shard_map/ppermute | solution.py:256
  77.4 16.8 %collective-permute-start.22 = (bf16[160,1280]{1,0:T(8,128)(2,1)S(1)}, bf16[160,1280]{1,0:T(8,128)(2,1)S(1)}, u32[]{:S(2)}, u32[]{:S(2)}) collective-permute-start(bf16[160,1280]{1,0:T(8,128)(2,1)S(1)} %add.35), channel_id=1, source_target_pairs={{0,1},{1,2},{4,5},{5,6},{8,9},{9,10},{12,13},{13,14},{16,17},{17,1... | collective-permute-start | bytes 1228808 | tf_op jit(solution)/shard_map/ppermute | solution.py:255
  82.5 16.1 %collective-permute-start.17 = (bf16[160,1280]{1,0:T(8,128)(2,1)S(1)}, bf16[160,1280]{1,0:T(8,128)(2,1)S(1)}, u32[]{:S(2)}, u32[]{:S(2)}) collective-permute-start(bf16[160,1280]{1,0:T(8,128)(2,1)S(1)} %add.33), channel_id=1, source_target_pairs={{3,2},{2,1},{1,0},{7,6},{6,5},{5,4},{11,10},{10,9},{9,8},{15,14},{... | collective-permute-start | bytes 1228808 | tf_op jit(solution)/shard_map/ppermute | solution.py:256
  85.4 17.5 %collective-permute-start.15 = (bf16[160,1280]{1,0:T(8,128)(2,1)S(1)}, bf16[160,1280]{1,0:T(8,128)(2,1)S(1)}, u32[]{:S(2)}, u32[]{:S(2)}) collective-permute-start(bf16[160,1280]{1,0:T(8,128)(2,1)S(1)} %add.31), channel_id=1, source_target_pairs={{0,1},{1,2},{2,3},{4,5},{5,6},{6,7},{8,9},{9,10},{10,11},{12,13},{... | collective-permute-start | bytes 1228808 | tf_op jit(solution)/shard_map/ppermute | solution.py:255
  90.0 13.0 %collective-permute-start.25 = (bf16[160,1280]{1,0:T(8,128)(2,1)S(1)}, bf16[160,1280]{1,0:T(8,128)(2,1)S(1)}, u32[]{:S(2)}, u32[]{:S(2)}) collective-permute-start(bf16[160,1280]{1,0:T(8,128)(2,1)S(1)} %add.38), channel_id=1, source_target_pairs={{3,2},{2,1},{1,0},{7,6},{6,5},{5,4},{11,10},{10,9},{9,8},{15,14},{... | collective-permute-start | bytes 1228808 | tf_op jit(solution)/shard_map/ppermute | solution.py:256
  94.2 13.5 %collective-permute-start.23 = (bf16[160,1280]{1,0:T(8,128)(2,1)S(1)}, bf16[160,1280]{1,0:T(8,128)(2,1)S(1)}, u32[]{:S(2)}, u32[]{:S(2)}) collective-permute-start(bf16[160,1280]{1,0:T(8,128)(2,1)S(1)} %add.36), channel_id=1, source_target_pairs={{0,1},{1,2},{2,3},{4,5},{5,6},{6,7},{8,9},{9,10},{10,11},{12,13},{... | collective-permute-start | bytes 1228808 | tf_op jit(solution)/shard_map/ppermute | solution.py:255
  (8 other events, 96.6 us)

commit v6 on v5

--- a/solution.py
+++ b/solution.py
@@ -290,7 +290,8 @@
             shares += project(*common, slice(1, None))
         begun.append(begin_sums(shares, "head"))
         if c == 0:
-            first, *done[1] = lax.optimization_barrier((shares[0], *done[1]))
+            first, *tied = lax.optimization_barrier((shares[0], *done[1][:-1]))
+            done[1] = [*tied, done[1][-1]]
     outputs = finish_sums(begun, "head")
     return jnp.concatenate(outputs, axis=0).reshape(frames_dev, rows_dev, width, -1)
 

time: 109 us -> 109 us (level)
  no operation moved by 1% of the time
where the time goes in v6:
time: 109 us
  waiting for transfers between devices  44.2 us (41%)
  starting transfers between devices  41.2 us (38%)
  Pallas kernels  21.2 us (19%)
  other arithmetic  1.65 us (2%)
    ppermute x12, waiting for transfers between devices, swap(): lax.ppermute(x, 'tm', [(i, i ^ m) for i in range(partners)])  26.7 us
    ppermute x4, starting transfers between devices, finish_sums(): lax.ppermute(right, axis, [(i, i + 1) for i in range(step)])  16.6 us
    ppermute x12, starting transfers between devices, swap(): lax.ppermute(x, 'tm', [(i, i ^ m) for i in range(partners)])  15.3 us
    ppermute x4, waiting for transfers between devices, finish_sums(): lax.ppermute(right, axis, [(i, i + 1) for i in range(step)])  13.7 us
    pallas_call x2, Pallas kernels, attend(): pl.pallas_call(kernel, out_shape=[jax.ShapeDtypeStruct((rows_out, HD), jn...  11.6 us
    pallas_call x4, Pallas kernels, project(): pl.pallas_call(kernel, out_shape=[jax.ShapeDtypeStruct((part, width // si...  6.58 us
    ppermute x2, starting transfers between devices, begin_sums(): come = lax.ppermute(shares[0], axis, [(0, 1), (size - 1, size - 2)])  4.99 us
    ppermute x4, starting transfers between devices, finish_sums(): lax.ppermute(left, axis, [(size - 1 - i, size - 2 - i) for i in range(ste...  3.96 us
  transfers between devices with their start and end apart: 26, of which 10 were waited for; matrix products, arithmetic and copies ran while one was open for 1% of the time, Pallas kernels for 17%

profile of v6, /device:TPU:0, one launch (start us, length us, event | category | flops | bytes accessed | tf_op | source)
XLA Modules:
  0.0 108.7 jit_solution(5812003344133131921)
XLA Ops:
  0.0 2.2 %pack.7 = (bf16[2320,128]{1,0:T(8,128)(2,1)}, bf16[400,128]{1,0:T(8,128)(2,1)}) custom-call(bf16[320,1280]{1,0:T(8,128)(2,1)} %bitcast.4, bf16[320,1280]{1,0:T(8,128)(2,1)} %bitcast.8, bf16[320,1280]{1,0:T(8,128)(2,1)} %bitcast.12), custom_call_target="tpu_custom_call" | custom-call | tf_op jit(solution)/shard_map/pack/pallas_call | solution.py:55
  2.2 4.0 %collective-permute-start.2 = (bf16[2320,128]{1,0:T(8,128)(2,1)}, bf16[2320,128]{1,0:T(8,128)(2,1)S(1)}, u32[]{:S(2)}, u32[]{:S(2)}) collective-permute-start(bf16[2320,128]{1,0:T(8,128)(2,1)} %get-tuple-element.35), channel_id=1, source_target_pairs={{0,24},{8,16},{16,8},{24,0},{1,25},{9,17},{17,9},{25,1},{2,26},{10... | collective-permute-start | bytes 1781768 | tf_op jit(solution)/shard_map/ppermute | solution.py:271
  7.9 12.8 %collective-permute-done.2.refs_4_.refs_8_ = bf16[2320,128]{1,0:T(8,128)(2,1)S(1)} collective-permute-done((bf16[2320,128]{1,0:T(8,128)(2,1)}, bf16[2320,128]{1,0:T(8,128)(2,1)S(1)}, u32[]{:S(2)}, u32[]{:S(2)}) %collective-permute-start.2) | collective-permute-done | bytes 593952 | tf_op jit(solution)/shard_map/ppermute | solution.py:271
  20.7 11.9 %collective-permute-done.1.refs_3_.refs_7_ = bf16[2320,128]{1,0:T(8,128)(2,1)S(1)} collective-permute-done((bf16[2320,128]{1,0:T(8,128)(2,1)S(1)}, bf16[2320,128]{1,0:T(8,128)(2,1)S(1)}, u32[]{:S(2)}, u32[]{:S(2)}) %collective-permute-start.1) | collective-permute-done | bytes 593952 | tf_op jit(solution)/shard_map/ppermute | solution.py:271
  33.1 1.9 %collective-permute-start.12 = (bf16[400,128]{1,0:T(8,128)(2,1)S(1)}, bf16[400,128]{1,0:T(8,128)(2,1)S(1)}, u32[]{:S(2)}, u32[]{:S(2)}) collective-permute-start(bf16[400,128]{1,0:T(8,128)(2,1)S(1)} %copy-done.5), channel_id=1, source_target_pairs={{0,24},{8,16},{16,8},{24,0},{1,25},{9,17},{17,9},{25,1},{2,26},{10... | collective-permute-start | bytes 307208 | tf_op jit(solution)/shard_map/ppermute | solution.py:271
  36.6 5.8 %attend.2 = (bf16[400,128]{1,0:T(8,128)(2,1)S(1)}, bf16[400,128]{1,0:T(8,128)(2,1)S(1)}, bf16[400,128]{1,0:T(8,128)(2,1)S(1)}, bf16[400,128]{1,0:T(8,128)(2,1)S(1)}) custom-call(s32[4,4]{1,0:T(4,128)S(1)} %copy-done.4, bf16[2320,128]{1,0:T(8,128)(2,1)S(1)} %get-tuple-element.32.refs_1_.refs_5_, bf16[2320,128]{1,0:T(8,128)(2,1)S(1)} %collective-permute-done.refs_2_.refs_6_, ...), custom_call_target="tpu_custom_call" | custom-call | flops 2097152000 | bytes 3932160 | tf_op jit(solution)/shard_map/attend/pallas_call | solution.py:157
  42.4 1.7 %collective-permute-start.7 = (bf16[400,128]{1,0:T(8,128)(2,1)S(1)}, bf16[400,128]{1,0:T(8,128)(2,1)S(1)}, u32[]{:S(2)}, u32[]{:S(2)}) collective-permute-start(bf16[400,128]{1,0:T(8,128)(2,1)S(1)} %get-tuple-element.37), channel_id=1, source_target_pairs={{0,8},{8,0},{16,24},{24,16},{1,9},{9,1},{17,25},{25,17},{2,10},{10... | collective-permute-start | bytes 307208 | tf_op jit(solution)/shard_map/ppermute | solution.py:271
  46.0 5.8 %attend.3 = (bf16[400,128]{1,0:T(8,128)(2,1)S(1)}, bf16[400,128]{1,0:T(8,128)(2,1)S(1)}, bf16[400,128]{1,0:T(8,128)(2,1)S(1)}, bf16[400,128]{1,0:T(8,128)(2,1)S(1)}) custom-call(s32[4,4]{1,0:T(4,128)S(1)} %copy-done.4, bf16[400,128]{1,0:T(8,128)(2,1)S(1)} %get-tuple-element.43.refs_1_, bf16[400,128]{1,0:T(8,128)(2,1)S(1)} %collective-permute-done.10.refs_2_, ...), custom_call_target="tpu_custom_call" | custom-call | flops 2097152000 | bytes 3932160 | tf_op jit(solution)/shard_map/attend/pallas_call | solution.py:157
  52.8 3.7 %collective-permute-start.13 = (bf16[160,1280]{1,0:T(8,128)(2,1)S(1)}, bf16[160,1280]{1,0:T(8,128)(2,1)S(1)}, u32[]{:S(2)}, u32[]{:S(2)}) collective-permute-start(bf16[160,1280]{1,0:T(8,128)(2,1)S(1)} %project.5), channel_id=1, source_target_pairs={{0,1},{3,2},{4,5},{7,6},{8,9},{11,10},{12,13},{15,14},{16,17},{19,... | collective-permute-start | bytes 1228808 | tf_op jit(solution)/shard_map/ppermute | solution.py:240
  56.5 2.0 %collective-permute-start.20 = (bf16[400,128]{1,0:T(8,128)(2,1)S(1)}, bf16[400,128]{1,0:T(8,128)(2,1)S(1)}, u32[]{:S(2)}, u32[]{:S(2)}) collective-permute-start(bf16[400,128]{1,0:T(8,128)(2,1)S(1)} %get-tuple-element.54), channel_id=1, source_target_pairs={{0,24},{8,16},{16,8},{24,0},{1,25},{9,17},{17,9},{25,1},{2,26},{10... | collective-permute-start | bytes 307208 | tf_op jit(solution)/shard_map/ppermute | solution.py:271
  60.0 2.4 %project.4 = (bf16[160,1280]{1,0:T(8,128)(2,1)S(1)}, bf16[160,1280]{1,0:T(8,128)(2,1)S(1)}, bf16[160,1280]{1,0:T(8,128)(2,1)S(1)}, bf16[160,1280]{1,0:T(8,128)(2,1)S(1)}) custom-call(bf16[400,128]{1,0:T(8,128)(2,1)S(1)} %get-tuple-element.36.refs_0_, bf16[400,128]{1,0:T(8,128)(2,1)S(1)} %collective-permute-done.7.refs_1_, ...), custom_call_target="tpu_custom_call" | custom-call | flops 2097152000 | bytes 13107200 | tf_op jit(solution)/shard_map/project/pallas_call | solution.py:224
  65.0 1.3 %collective-permute-start.21 = (bf16[160,1280]{1,0:T(8,128)(2,1)S(1)}, bf16[160,1280]{1,0:T(8,128)(2,1)S(1)}, u32[]{:S(2)}, u32[]{:S(2)}) collective-permute-start(bf16[160,1280]{1,0:T(8,128)(2,1)S(1)} %project.7), channel_id=1, source_target_pairs={{0,1},{3,2},{4,5},{7,6},{8,9},{11,10},{12,13},{15,14},{16,17},{19,... | collective-permute-start | bytes 1228808 | tf_op jit(solution)/shard_map/ppermute | solution.py:240
  67.1 2.8 %collective-permute-start.14 = (bf16[160,1280]{1,0:T(8,128)(2,1)S(1)}, bf16[160,1280]{1,0:T(8,128)(2,1)S(1)}, u32[]{:S(2)}, u32[]{:S(2)}) collective-permute-start(bf16[160,1280]{1,0:T(8,128)(2,1)S(1)} %add.30), channel_id=1, source_target_pairs={{0,1},{1,2},{4,5},{5,6},{8,9},{9,10},{12,13},{13,14},{16,17},{17,1... | collective-permute-start | bytes 1228808 | tf_op jit(solution)/shard_map/ppermute | solution.py:255
  69.9 2.4 %project.6 = (bf16[160,1280]{1,0:T(8,128)(2,1)S(1)}, bf16[160,1280]{1,0:T(8,128)(2,1)S(1)}, bf16[160,1280]{1,0:T(8,128)(2,1)S(1)}, bf16[160,1280]{1,0:T(8,128)(2,1)S(1)}) custom-call(bf16[400,128]{1,0:T(8,128)(2,1)S(1)} %get-tuple-element.51.refs_5_.refs_0_, bf16[400,128]{1,0:T(8,128)(2,1)S(1)} %collective-permute-done.18.refs_1_, ...), custom_call_target="tpu_custom_call" | custom-call | flops 2097152000 | bytes 13107200 | tf_op jit(solution)/shard_map/project/pallas_call | solution.py:224
  72.4 3.8 %collective-permute-done.21 = bf16[160,1280]{1,0:T(8,128)(2,1)S(1)} collective-permute-done((bf16[160,1280]{1,0:T(8,128)(2,1)S(1)}, bf16[160,1280]{1,0:T(8,128)(2,1)S(1)}, u32[]{:S(2)}, u32[]{:S(2)}) %collective-permute-start.21) | collective-permute-done | bytes 409632 | tf_op jit(solution)/shard_map/ppermute | solution.py:240
  77.0 5.0 %collective-permute-start.22 = (bf16[160,1280]{1,0:T(8,128)(2,1)S(1)}, bf16[160,1280]{1,0:T(8,128)(2,1)S(1)}, u32[]{:S(2)}, u32[]{:S(2)}) collective-permute-start(bf16[160,1280]{1,0:T(8,128)(2,1)S(1)} %add.35), channel_id=1, source_target_pairs={{0,1},{1,2},{4,5},{5,6},{8,9},{9,10},{12,13},{13,14},{16,17},{17,1... | collective-permute-start | bytes 1228808 | tf_op jit(solution)/shard_map/ppermute | solution.py:255
  82.1 1.3 %collective-permute-start.17 = (bf16[160,1280]{1,0:T(8,128)(2,1)S(1)}, bf16[160,1280]{1,0:T(8,128)(2,1)S(1)}, u32[]{:S(2)}, u32[]{:S(2)}) collective-permute-start(bf16[160,1280]{1,0:T(8,128)(2,1)S(1)} %add.33), channel_id=1, source_target_pairs={{3,2},{2,1},{1,0},{7,6},{6,5},{5,4},{11,10},{10,9},{9,8},{15,14},{... | collective-permute-start | bytes 1228808 | tf_op jit(solution)/shard_map/ppermute | solution.py:256
  83.4 1.5 %collective-permute-done.14 = bf16[160,1280]{1,0:T(8,128)(2,1)S(1)} collective-permute-done((bf16[160,1280]{1,0:T(8,128)(2,1)S(1)}, bf16[160,1280]{1,0:T(8,128)(2,1)S(1)}, u32[]{:S(2)}, u32[]{:S(2)}) %collective-permute-start.14) | collective-permute-done | bytes 409632 | tf_op jit(solution)/shard_map/ppermute | solution.py:255
  85.1 4.4 %collective-permute-start.15 = (bf16[160,1280]{1,0:T(8,128)(2,1)S(1)}, bf16[160,1280]{1,0:T(8,128)(2,1)S(1)}, u32[]{:S(2)}, u32[]{:S(2)}) collective-permute-start(bf16[160,1280]{1,0:T(8,128)(2,1)S(1)} %add.31), channel_id=1, source_target_pairs={{0,1},{1,2},{2,3},{4,5},{5,6},{6,7},{8,9},{9,10},{10,11},{12,13},{... | collective-permute-start | bytes 1228808 | tf_op jit(solution)/shard_map/ppermute | solution.py:255
  89.6 1.3 %collective-permute-start.25 = (bf16[160,1280]{1,0:T(8,128)(2,1)S(1)}, bf16[160,1280]{1,0:T(8,128)(2,1)S(1)}, u32[]{:S(2)}, u32[]{:S(2)}) collective-permute-start(bf16[160,1280]{1,0:T(8,128)(2,1)S(1)} %add.38), channel_id=1, source_target_pairs={{3,2},{2,1},{1,0},{7,6},{6,5},{5,4},{11,10},{10,9},{9,8},{15,14},{... | collective-permute-start | bytes 1228808 | tf_op jit(solution)/shard_map/ppermute | solution.py:256
  90.9 2.8 %collective-permute-done.22 = bf16[160,1280]{1,0:T(8,128)(2,1)S(1)} collective-permute-done((bf16[160,1280]{1,0:T(8,128)(2,1)S(1)}, bf16[160,1280]{1,0:T(8,128)(2,1)S(1)}, u32[]{:S(2)}, u32[]{:S(2)}) %collective-permute-start.22) | collective-permute-done | bytes 409632 | tf_op jit(solution)/shard_map/ppermute | solution.py:255
  93.9 4.4 %collective-permute-start.23 = (bf16[160,1280]{1,0:T(8,128)(2,1)S(1)}, bf16[160,1280]{1,0:T(8,128)(2,1)S(1)}, u32[]{:S(2)}, u32[]{:S(2)}) collective-permute-start(bf16[160,1280]{1,0:T(8,128)(2,1)S(1)} %add.36), channel_id=1, source_target_pairs={{0,1},{1,2},{2,3},{4,5},{5,6},{6,7},{8,9},{9,10},{10,11},{12,13},{... | collective-permute-start | bytes 1228808 | tf_op jit(solution)/shard_map/ppermute | solution.py:255
  98.3 4.2 %collective-permute-done.15 = bf16[160,1280]{1,0:T(8,128)(2,1)S(1)} collective-permute-done((bf16[160,1280]{1,0:T(8,128)(2,1)S(1)}, bf16[160,1280]{1,0:T(8,128)(2,1)S(1)}, u32[]{:S(2)}, u32[]{:S(2)}) %collective-permute-start.15) | collective-permute-done | bytes 409632 | tf_op jit(solution)/shard_map/ppermute | solution.py:255
  102.6 5.0 %collective-permute-done.23 = bf16[160,1280]{1,0:T(8,128)(2,1)S(1)} collective-permute-done((bf16[160,1280]{1,0:T(8,128)(2,1)S(1)}, bf16[160,1280]{1,0:T(8,128)(2,1)S(1)}, u32[]{:S(2)}, u32[]{:S(2)}) %collective-permute-start.23) | collective-permute-done | bytes 409632 | tf_op jit(solution)/shard_map/ppermute | solution.py:255
  (59 shorter events, 13.6 us)
Async XLA Ops:
  2.2 18.5 %collective-permute-start.2 = (bf16[2320,128]{1,0:T(8,128)(2,1)}, bf16[2320,128]{1,0:T(8,128)(2,1)S(1)}, u32[]{:S(2)}, u32[]{:S(2)}) collective-permute-start(bf16[2320,128]{1,0:T(8,128)(2,1)} %get-tuple-element.35), channel_id=1, source_target_pairs={{0,24},{8,16},{16,8},{24,0},{1,25},{9,17},{17,9},{25,1},{2,26},{10... | collective-permute-start | bytes 1781768 | tf_op jit(solution)/shard_map/ppermute | solution.py:271
  6.5 26.1 %collective-permute-start.1 = (bf16[2320,128]{1,0:T(8,128)(2,1)S(1)}, bf16[2320,128]{1,0:T(8,128)(2,1)S(1)}, u32[]{:S(2)}, u32[]{:S(2)}) collective-permute-start(bf16[2320,128]{1,0:T(8,128)(2,1)S(1)} %get-tuple-element.34), channel_id=1, source_target_pairs={{0,16},{8,24},{16,0},{24,8},{1,17},{9,25},{17,1},{25,9},{2,18},{10... | collective-permute-start | bytes 1781768 | tf_op jit(solution)/shard_map/ppermute | solution.py:271
  7.4 25.5 %collective-permute-start = (bf16[2320,128]{1,0:T(8,128)(2,1)S(1)}, bf16[2320,128]{1,0:T(8,128)(2,1)S(1)}, u32[]{:S(2)}, u32[]{:S(2)}) collective-permute-start(bf16[2320,128]{1,0:T(8,128)(2,1)S(1)} %get-tuple-element.33), channel_id=1, source_target_pairs={{0,8},{8,0},{16,24},{24,16},{1,9},{9,1},{17,25},{25,17},{2,10},{10... | collective-permute-start | bytes 1781768 | tf_op jit(solution)/shard_map/ppermute | solution.py:271
  7.8 27.2 %collective-permute-start.3 = (bf16[2320,128]{1,0:T(8,128)(2,1)S(1)}, bf16[2320,128]{1,0:T(8,128)(2,1)S(1)}, u32[]{:S(2)}, u32[]{:S(2)}) collective-permute-start(bf16[2320,128]{1,0:T(8,128)(2,1)S(1)} %get-tuple-element.32.refs_1_.refs_5_), channel_id=1, source_target_pairs={{0,4},{4,0},{1,5},{5,1},{2,6},{6,2},{3,7},{7,3},{8,12},{12,8},{9,1... | collective-permute-start | bytes 1781768 | tf_op jit(solution)/shard_map/ppermute | solution.py:275
  20.7 15.5 %collective-permute-start.6 = (bf16[2320,128]{1,0:T(8,128)(2,1)S(1)}, bf16[2320,128]{1,0:T(8,128)(2,1)S(1)}, u32[]{:S(2)}, u32[]{:S(2)}) collective-permute-start(bf16[2320,128]{1,0:T(8,128)(2,1)S(1)} %collective-permute-done.2.refs_4_.refs_8_), channel_id=1, source_target_pairs={{0,4},{4,0},{1,5},{5,1},{2,6},{6,2},{3,7},{7,3},{8,12},{12,8},{9,1... | collective-permute-start | bytes 1781768 | tf_op jit(solution)/shard_map/ppermute | solution.py:275
  33.1 11.9 %collective-permute-start.12 = (bf16[400,128]{1,0:T(8,128)(2,1)S(1)}, bf16[400,128]{1,0:T(8,128)(2,1)S(1)}, u32[]{:S(2)}, u32[]{:S(2)}) collective-permute-start(bf16[400,128]{1,0:T(8,128)(2,1)S(1)} %copy-done.5), channel_id=1, source_target_pairs={{0,24},{8,16},{16,8},{24,0},{1,25},{9,17},{17,9},{25,1},{2,26},{10... | collective-permute-start | bytes 307208 | tf_op jit(solution)/shard_map/ppermute | solution.py:271
  35.0 11.0 %collective-permute-start.11 = (bf16[400,128]{1,0:T(8,128)(2,1)S(1)}, bf16[400,128]{1,0:T(8,128)(2,1)S(1)}, u32[]{:S(2)}, u32[]{:S(2)}) collective-permute-start(bf16[400,128]{1,0:T(8,128)(2,1)S(1)} %get-tuple-element.45), channel_id=1, source_target_pairs={{0,16},{8,24},{16,0},{24,8},{1,17},{9,25},{17,1},{25,9},{2,18},{10... | collective-permute-start | bytes 307208 | tf_op jit(solution)/shard_map/ppermute | solution.py:271
  36.2 9.8 %collective-permute-start.10 = (bf16[400,128]{1,0:T(8,128)(2,1)S(1)}, bf16[400,128]{1,0:T(8,128)(2,1)S(1)}, u32[]{:S(2)}, u32[]{:S(2)}) collective-permute-start(bf16[400,128]{1,0:T(8,128)(2,1)S(1)} %get-tuple-element.44), channel_id=1, source_target_pairs={{0,8},{8,0},{16,24},{24,16},{1,9},{9,1},{17,25},{25,17},{2,10},{10... | collective-permute-start | bytes 307208 | tf_op jit(solution)/shard_map/ppermute | solution.py:271
  42.4 9.4 %collective-permute-start.7 = (bf16[400,128]{1,0:T(8,128)(2,1)S(1)}, bf16[400,128]{1,0:T(8,128)(2,1)S(1)}, u32[]{:S(2)}, u32[]{:S(2)}) collective-permute-start(bf16[400,128]{1,0:T(8,128)(2,1)S(1)} %get-tuple-element.37), channel_id=1, source_target_pairs={{0,8},{8,0},{16,24},{24,16},{1,9},{9,1},{17,25},{25,17},{2,10},{10... | collective-permute-start | bytes 307208 | tf_op jit(solution)/shard_map/ppermute | solution.py:271
  44.2 7.6 %collective-permute-start.8 = (bf16[400,128]{1,0:T(8,128)(2,1)S(1)}, bf16[400,128]{1,0:T(8,128)(2,1)S(1)}, u32[]{:S(2)}, u32[]{:S(2)}) collective-permute-start(bf16[400,128]{1,0:T(8,128)(2,1)S(1)} %get-tuple-element.38), channel_id=1, source_target_pairs={{0,16},{8,24},{16,0},{24,8},{1,17},{9,25},{17,1},{25,9},{2,18},{10... | collective-permute-start | bytes 307208 | tf_op jit(solution)/shard_map/ppermute | solution.py:271
  45.0 6.8 %collective-permute-start.9 = (bf16[400,128]{1,0:T(8,128)(2,1)S(1)}, bf16[400,128]{1,0:T(8,128)(2,1)S(1)}, u32[]{:S(2)}, u32[]{:S(2)}) collective-permute-start(bf16[400,128]{1,0:T(8,128)(2,1)S(1)} %get-tuple-element.39), channel_id=1, source_target_pairs={{0,24},{8,16},{16,8},{24,0},{1,25},{9,17},{17,9},{25,1},{2,26},{10... | collective-permute-start | bytes 307208 | tf_op jit(solution)/shard_map/ppermute | solution.py:271
  52.8 13.5 %collective-permute-start.13 = (bf16[160,1280]{1,0:T(8,128)(2,1)S(1)}, bf16[160,1280]{1,0:T(8,128)(2,1)S(1)}, u32[]{:S(2)}, u32[]{:S(2)}) collective-permute-start(bf16[160,1280]{1,0:T(8,128)(2,1)S(1)} %project.5), channel_id=1, source_target_pairs={{0,1},{3,2},{4,5},{7,6},{8,9},{11,10},{12,13},{15,14},{16,17},{19,... | collective-permute-start | bytes 1228808 | tf_op jit(solution)/shard_map/ppermute | solution.py:240
  56.5 6.0 %collective-permute-start.20 = (bf16[400,128]{1,0:T(8,128)(2,1)S(1)}, bf16[400,128]{1,0:T(8,128)(2,1)S(1)}, u32[]{:S(2)}, u32[]{:S(2)}) collective-permute-start(bf16[400,128]{1,0:T(8,128)(2,1)S(1)} %get-tuple-element.54), channel_id=1, source_target_pairs={{0,24},{8,16},{16,8},{24,0},{1,25},{9,17},{17,9},{25,1},{2,26},{10... | collective-permute-start | bytes 307208 | tf_op jit(solution)/shard_map/ppermute | solution.py:271
  58.5 4.8 %collective-permute-start.18 = (bf16[400,128]{1,0:T(8,128)(2,1)S(1)}, bf16[400,128]{1,0:T(8,128)(2,1)S(1)}, u32[]{:S(2)}, u32[]{:S(2)}) collective-permute-start(bf16[400,128]{1,0:T(8,128)(2,1)S(1)} %get-tuple-element.52), channel_id=1, source_target_pairs={{0,8},{8,0},{16,24},{24,16},{1,9},{9,1},{17,25},{25,17},{2,10},{10... | collective-permute-start | bytes 307208 | tf_op jit(solution)/shard_map/ppermute | solution.py:271
  59.5 4.7 %collective-permute-start.19 = (bf16[400,128]{1,0:T(8,128)(2,1)S(1)}, bf16[400,128]{1,0:T(8,128)(2,1)S(1)}, u32[]{:S(2)}, u32[]{:S(2)}) collective-permute-start(bf16[400,128]{1,0:T(8,128)(2,1)S(1)} %get-tuple-element.53), channel_id=1, source_target_pairs={{0,16},{8,24},{16,0},{24,8},{1,17},{9,25},{17,1},{25,9},{2,18},{10... | collective-permute-start | bytes 307208 | tf_op jit(solution)/shard_map/ppermute | solution.py:271
  65.0 11.2 %collective-permute-start.21 = (bf16[160,1280]{1,0:T(8,128)(2,1)S(1)}, bf16[160,1280]{1,0:T(8,128)(2,1)S(1)}, u32[]{:S(2)}, u32[]{:S(2)}) collective-permute-start(bf16[160,1280]{1,0:T(8,128)(2,1)S(1)} %project.7), channel_id=1, source_target_pairs={{0,1},{3,2},{4,5},{7,6},{8,9},{11,10},{12,13},{15,14},{16,17},{19,... | collective-permute-start | bytes 1228808 | tf_op jit(solution)/shard_map/ppermute | solution.py:240
  66.4 15.6 %collective-permute-start.16 = (bf16[160,1280]{1,0:T(8,128)(2,1)S(1)}, bf16[160,1280]{1,0:T(8,128)(2,1)S(1)}, u32[]{:S(2)}, u32[]{:S(2)}) collective-permute-start(bf16[160,1280]{1,0:T(8,128)(2,1)S(1)} %add.30), channel_id=1, source_target_pairs={{3,2},{2,1},{7,6},{6,5},{11,10},{10,9},{15,14},{14,13},{19,18},{18... | collective-permute-start | bytes 1228808 | tf_op jit(solution)/shard_map/ppermute | solution.py:256
  67.1 17.8 %collective-permute-start.14 = (bf16[160,1280]{1,0:T(8,128)(2,1)S(1)}, bf16[160,1280]{1,0:T(8,128)(2,1)S(1)}, u32[]{:S(2)}, u32[]{:S(2)}) collective-permute-start(bf16[160,1280]{1,0:T(8,128)(2,1)S(1)} %add.30), channel_id=1, source_target_pairs={{0,1},{1,2},{4,5},{5,6},{8,9},{9,10},{12,13},{13,14},{16,17},{17,1... | collective-permute-start | bytes 1228808 | tf_op jit(solution)/shard_map/ppermute | solution.py:255
  76.3 13.2 %collective-permute-start.24 = (bf16[160,1280]{1,0:T(8,128)(2,1)S(1)}, bf16[160,1280]{1,0:T(8,128)(2,1)S(1)}, u32[]{:S(2)}, u32[]{:S(2)}) collective-permute-start(bf16[160,1280]{1,0:T(8,128)(2,1)S(1)} %add.35), channel_id=1, source_target_pairs={{3,2},{2,1},{7,6},{6,5},{11,10},{10,9},{15,14},{14,13},{19,18},{18... | collective-permute-start | bytes 1228808 | tf_op jit(solution)/shard_map/ppermute | solution.py:256
  77.0 16.8 %collective-permute-start.22 = (bf16[160,1280]{1,0:T(8,128)(2,1)S(1)}, bf16[160,1280]{1,0:T(8,128)(2,1)S(1)}, u32[]{:S(2)}, u32[]{:S(2)}) collective-permute-start(bf16[160,1280]{1,0:T(8,128)(2,1)S(1)} %add.35), channel_id=1, source_target_pairs={{0,1},{1,2},{4,5},{5,6},{8,9},{9,10},{12,13},{13,14},{16,17},{17,1... | collective-permute-start | bytes 1228808 | tf_op jit(solution)/shard_map/ppermute | solution.py:255
  82.1 16.1 %collective-permute-start.17 = (bf16[160,1280]{1,0:T(8,128)(2,1)S(1)}, bf16[160,1280]{1,0:T(8,128)(2,1)S(1)}, u32[]{:S(2)}, u32[]{:S(2)}) collective-permute-start(bf16[160,1280]{1,0:T(8,128)(2,1)S(1)} %add.33), channel_id=1, source_target_pairs={{3,2},{2,1},{1,0},{7,6},{6,5},{5,4},{11,10},{10,9},{9,8},{15,14},{... | collective-permute-start | bytes 1228808 | tf_op jit(solution)/shard_map/ppermute | solution.py:256
  85.1 17.5 %collective-permute-start.15 = (bf16[160,1280]{1,0:T(8,128)(2,1)S(1)}, bf16[160,1280]{1,0:T(8,128)(2,1)S(1)}, u32[]{:S(2)}, u32[]{:S(2)}) collective-permute-start(bf16[160,1280]{1,0:T(8,128)(2,1)S(1)} %add.31), channel_id=1, source_target_pairs={{0,1},{1,2},{2,3},{4,5},{5,6},{6,7},{8,9},{9,10},{10,11},{12,13},{... | collective-permute-start | bytes 1228808 | tf_op jit(solution)/shard_map/ppermute | solution.py:255
  89.6 13.0 %collective-permute-start.25 = (bf16[160,1280]{1,0:T(8,128)(2,1)S(1)}, bf16[160,1280]{1,0:T(8,128)(2,1)S(1)}, u32[]{:S(2)}, u32[]{:S(2)}) collective-permute-start(bf16[160,1280]{1,0:T(8,128)(2,1)S(1)} %add.38), channel_id=1, source_target_pairs={{3,2},{2,1},{1,0},{7,6},{6,5},{5,4},{11,10},{10,9},{9,8},{15,14},{... | collective-permute-start | bytes 1228808 | tf_op jit(solution)/shard_map/ppermute | solution.py:256
  93.9 13.8 %collective-permute-start.23 = (bf16[160,1280]{1,0:T(8,128)(2,1)S(1)}, bf16[160,1280]{1,0:T(8,128)(2,1)S(1)}, u32[]{:S(2)}, u32[]{:S(2)}) collective-permute-start(bf16[160,1280]{1,0:T(8,128)(2,1)S(1)} %add.36), channel_id=1, source_target_pairs={{0,1},{1,2},{2,3},{4,5},{5,6},{6,7},{8,9},{9,10},{10,11},{12,13},{... | collective-permute-start | bytes 1228808 | tf_op jit(solution)/shard_map/ppermute | solution.py:255
  (8 other events, 96.6 us)

commit v7 on v5

--- a/solution.py
+++ b/solution.py
@@ -125,11 +125,11 @@
     tiles = [(unit, pair) for unit in range(full * rows_part + 1) for pair in pairs]
     scores, last = score(tiles[0]), None
     for i, tile in enumerate(tiles):
+        now = (tile, weigh(tile, scores))
         if last is not None:
             gather(*last)
-        following = score(tiles[i + 1]) if i + 1 < len(tiles) else None
-        last = (tile, weigh(tile, scores))
-        scores = following
+        scores = score(tiles[i + 1]) if i + 1 < len(tiles) else None
+        last = now
     gather(*last)
 
 

time: 109 us -> 109 us (level)
  no operation moved by 1% of the time
where the time goes in v7:
time: 109 us
  waiting for transfers between devices  45 us (41%)
  starting transfers between devices  40.5 us (37%)
  Pallas kernels  21.2 us (19%)
  other arithmetic  1.65 us (2%)
    ppermute x12, waiting for transfers between devices, swap(): lax.ppermute(x, 'tm', [(i, i ^ m) for i in range(partners)])  27.1 us
    ppermute x4, starting transfers between devices, finish_sums(): lax.ppermute(right, axis, [(i, i + 1) for i in range(step)])  15.9 us
    ppermute x12, starting transfers between devices, swap(): lax.ppermute(x, 'tm', [(i, i ^ m) for i in range(partners)])  15.3 us
    ppermute x4, waiting for transfers between devices, finish_sums(): lax.ppermute(right, axis, [(i, i + 1) for i in range(step)])  13.3 us
    pallas_call x2, Pallas kernels, attend(): pl.pallas_call(kernel, out_shape=[jax.ShapeDtypeStruct((rows_out, HD), jn...  11.6 us
    pallas_call x4, Pallas kernels, project(): pl.pallas_call(kernel, out_shape=[jax.ShapeDtypeStruct((part, width // si...  6.56 us
    ppermute x2, starting transfers between devices, begin_sums(): come = lax.ppermute(shares[0], axis, [(0, 1), (size - 1, size - 2)])  4.99 us
    ppermute x2, waiting for transfers between devices, begin_sums(): come = lax.ppermute(shares[0], axis, [(0, 1), (size - 1, size - 2)])  4.58 us
  transfers between devices with their start and end apart: 26, of which 10 were waited for; matrix products, arithmetic and copies ran while one was open for 1% of the time, Pallas kernels for 17%

profile of v7, /device:TPU:0, one launch (start us, length us, event | category | flops | bytes accessed | tf_op | source)
XLA Modules:
  0.0 108.7 jit_solution(514782419447954692)
XLA Ops:
  0.0 2.2 %pack.7 = (bf16[2320,128]{1,0:T(8,128)(2,1)}, bf16[400,128]{1,0:T(8,128)(2,1)}) custom-call(bf16[320,1280]{1,0:T(8,128)(2,1)} %bitcast.4, bf16[320,1280]{1,0:T(8,128)(2,1)} %bitcast.8, bf16[320,1280]{1,0:T(8,128)(2,1)} %bitcast.12), custom_call_target="tpu_custom_call" | custom-call | tf_op jit(solution)/shard_map/pack/pallas_call | solution.py:55
  2.2 4.0 %collective-permute-start.2 = (bf16[2320,128]{1,0:T(8,128)(2,1)}, bf16[2320,128]{1,0:T(8,128)(2,1)S(1)}, u32[]{:S(2)}, u32[]{:S(2)}) collective-permute-start(bf16[2320,128]{1,0:T(8,128)(2,1)} %get-tuple-element.36), channel_id=1, source_target_pairs={{0,24},{8,16},{16,8},{24,0},{1,25},{9,17},{17,9},{25,1},{2,26},{10... | collective-permute-start | bytes 1781768 | tf_op jit(solution)/shard_map/ppermute | solution.py:271
  7.9 12.8 %collective-permute-done.2.refs_4_.refs_8_ = bf16[2320,128]{1,0:T(8,128)(2,1)S(1)} collective-permute-done((bf16[2320,128]{1,0:T(8,128)(2,1)}, bf16[2320,128]{1,0:T(8,128)(2,1)S(1)}, u32[]{:S(2)}, u32[]{:S(2)}) %collective-permute-start.2) | collective-permute-done | bytes 593952 | tf_op jit(solution)/shard_map/ppermute | solution.py:271
  20.7 11.9 %collective-permute-done.1.refs_3_.refs_7_ = bf16[2320,128]{1,0:T(8,128)(2,1)S(1)} collective-permute-done((bf16[2320,128]{1,0:T(8,128)(2,1)S(1)}, bf16[2320,128]{1,0:T(8,128)(2,1)S(1)}, u32[]{:S(2)}, u32[]{:S(2)}) %collective-permute-start.1) | collective-permute-done | bytes 593952 | tf_op jit(solution)/shard_map/ppermute | solution.py:271
  33.1 1.9 %collective-permute-start.12 = (bf16[400,128]{1,0:T(8,128)(2,1)S(1)}, bf16[400,128]{1,0:T(8,128)(2,1)S(1)}, u32[]{:S(2)}, u32[]{:S(2)}) collective-permute-start(bf16[400,128]{1,0:T(8,128)(2,1)S(1)} %copy-done.5), channel_id=1, source_target_pairs={{0,24},{8,16},{16,8},{24,0},{1,25},{9,17},{17,9},{25,1},{2,26},{10... | collective-permute-start | bytes 307208 | tf_op jit(solution)/shard_map/ppermute | solution.py:271
  36.6 5.8 %attend.2 = (bf16[400,128]{1,0:T(8,128)(2,1)S(1)}, bf16[400,128]{1,0:T(8,128)(2,1)S(1)}, bf16[400,128]{1,0:T(8,128)(2,1)S(1)}, bf16[400,128]{1,0:T(8,128)(2,1)S(1)}) custom-call(s32[4,4]{1,0:T(4,128)S(1)} %copy-done.4, bf16[2320,128]{1,0:T(8,128)(2,1)S(1)} %get-tuple-element.33.refs_1_.refs_5_, bf16[2320,128]{1,0:T(8,128)(2,1)S(1)} %collective-permute-done.refs_2_.refs_6_, ...), custom_call_target="tpu_custom_call" | custom-call | flops 2097152000 | bytes 3932160 | tf_op jit(solution)/shard_map/attend/pallas_call | solution.py:157
  42.4 1.7 %collective-permute-start.7 = (bf16[400,128]{1,0:T(8,128)(2,1)S(1)}, bf16[400,128]{1,0:T(8,128)(2,1)S(1)}, u32[]{:S(2)}, u32[]{:S(2)}) collective-permute-start(bf16[400,128]{1,0:T(8,128)(2,1)S(1)} %get-tuple-element.38), channel_id=1, source_target_pairs={{0,8},{8,0},{16,24},{24,16},{1,9},{9,1},{17,25},{25,17},{2,10},{10... | collective-permute-start | bytes 307208 | tf_op jit(solution)/shard_map/ppermute | solution.py:271
  46.0 5.8 %attend.3 = (bf16[400,128]{1,0:T(8,128)(2,1)S(1)}, bf16[400,128]{1,0:T(8,128)(2,1)S(1)}, bf16[400,128]{1,0:T(8,128)(2,1)S(1)}, bf16[400,128]{1,0:T(8,128)(2,1)S(1)}) custom-call(s32[4,4]{1,0:T(4,128)S(1)} %copy-done.4, bf16[400,128]{1,0:T(8,128)(2,1)S(1)} %get-tuple-element.44.refs_1_, bf16[400,128]{1,0:T(8,128)(2,1)S(1)} %collective-permute-done.10.refs_2_, ...), custom_call_target="tpu_custom_call" | custom-call | flops 2097152000 | bytes 3932160 | tf_op jit(solution)/shard_map/attend/pallas_call | solution.py:157
  52.8 3.7 %collective-permute-start.13 = (bf16[160,1280]{1,0:T(8,128)(2,1)S(1)}, bf16[160,1280]{1,0:T(8,128)(2,1)S(1)}, u32[]{:S(2)}, u32[]{:S(2)}) collective-permute-start(bf16[160,1280]{1,0:T(8,128)(2,1)S(1)} %project.5), channel_id=1, source_target_pairs={{0,1},{3,2},{4,5},{7,6},{8,9},{11,10},{12,13},{15,14},{16,17},{19,... | collective-permute-start | bytes 1228808 | tf_op jit(solution)/shard_map/ppermute | solution.py:240
  56.5 1.6 %collective-permute-start.18 = (bf16[400,128]{1,0:T(8,128)(2,1)S(1)}, bf16[400,128]{1,0:T(8,128)(2,1)S(1)}, u32[]{:S(2)}, u32[]{:S(2)}) collective-permute-start(bf16[400,128]{1,0:T(8,128)(2,1)S(1)} %get-tuple-element.54), channel_id=1, source_target_pairs={{0,8},{8,0},{16,24},{24,16},{1,9},{9,1},{17,25},{25,17},{2,10},{10... | collective-permute-start | bytes 307208 | tf_op jit(solution)/shard_map/ppermute | solution.py:271
  60.0 2.4 %project.4 = (bf16[160,1280]{1,0:T(8,128)(2,1)S(1)}, bf16[160,1280]{1,0:T(8,128)(2,1)S(1)}, bf16[160,1280]{1,0:T(8,128)(2,1)S(1)}, bf16[160,1280]{1,0:T(8,128)(2,1)S(1)}) custom-call(bf16[400,128]{1,0:T(8,128)(2,1)S(1)} %get-tuple-element.37.refs_0_, bf16[400,128]{1,0:T(8,128)(2,1)S(1)} %collective-permute-done.7.refs_1_, ...), custom_call_target="tpu_custom_call" | custom-call | flops 2097152000 | bytes 13107200 | tf_op jit(solution)/shard_map/project/pallas_call | solution.py:224
  62.7 1.9 %collective-permute-done.20.refs_3_ = bf16[400,128]{1,0:T(8,128)(2,1)S(1)} collective-permute-done((bf16[400,128]{1,0:T(8,128)(2,1)S(1)}, bf16[400,128]{1,0:T(8,128)(2,1)S(1)}, u32[]{:S(2)}, u32[]{:S(2)}) %collective-permute-start.20) | collective-permute-done | bytes 102432 | tf_op jit(solution)/shard_map/ppermute | solution.py:271
  65.4 1.3 %collective-permute-start.21 = (bf16[160,1280]{1,0:T(8,128)(2,1)S(1)}, bf16[160,1280]{1,0:T(8,128)(2,1)S(1)}, u32[]{:S(2)}, u32[]{:S(2)}) collective-permute-start(bf16[160,1280]{1,0:T(8,128)(2,1)S(1)} %project.7), channel_id=1, source_target_pairs={{0,1},{3,2},{4,5},{7,6},{8,9},{11,10},{12,13},{15,14},{16,17},{19,... | collective-permute-start | bytes 1228808 | tf_op jit(solution)/shard_map/ppermute | solution.py:240
  67.5 2.1 %collective-permute-start.14 = (bf16[160,1280]{1,0:T(8,128)(2,1)S(1)}, bf16[160,1280]{1,0:T(8,128)(2,1)S(1)}, u32[]{:S(2)}, u32[]{:S(2)}) collective-permute-start(bf16[160,1280]{1,0:T(8,128)(2,1)S(1)} %add.30), channel_id=1, source_target_pairs={{0,1},{1,2},{4,5},{5,6},{8,9},{9,10},{12,13},{13,14},{16,17},{17,1... | collective-permute-start | bytes 1228808 | tf_op jit(solution)/shard_map/ppermute | solution.py:255
  69.6 2.4 %project.6 = (bf16[160,1280]{1,0:T(8,128)(2,1)S(1)}, bf16[160,1280]{1,0:T(8,128)(2,1)S(1)}, bf16[160,1280]{1,0:T(8,128)(2,1)S(1)}, bf16[160,1280]{1,0:T(8,128)(2,1)S(1)}) custom-call(bf16[400,128]{1,0:T(8,128)(2,1)S(1)} %get-tuple-element.53.refs_5_.refs_0_, bf16[400,128]{1,0:T(8,128)(2,1)S(1)} %collective-permute-done.18.refs_1_, ...), custom_call_target="tpu_custom_call" | custom-call | flops 2097152000 | bytes 13107200 | tf_op jit(solution)/shard_map/project/pallas_call | solution.py:224
  72.0 4.6 %collective-permute-done.21 = bf16[160,1280]{1,0:T(8,128)(2,1)S(1)} collective-permute-done((bf16[160,1280]{1,0:T(8,128)(2,1)S(1)}, bf16[160,1280]{1,0:T(8,128)(2,1)S(1)}, u32[]{:S(2)}, u32[]{:S(2)}) %collective-permute-start.21) | collective-permute-done | bytes 409632 | tf_op jit(solution)/shard_map/ppermute | solution.py:240
  77.4 5.0 %collective-permute-start.22 = (bf16[160,1280]{1,0:T(8,128)(2,1)S(1)}, bf16[160,1280]{1,0:T(8,128)(2,1)S(1)}, u32[]{:S(2)}, u32[]{:S(2)}) collective-permute-start(bf16[160,1280]{1,0:T(8,128)(2,1)S(1)} %add.35), channel_id=1, source_target_pairs={{0,1},{1,2},{4,5},{5,6},{8,9},{9,10},{12,13},{13,14},{16,17},{17,1... | collective-permute-start | bytes 1228808 | tf_op jit(solution)/shard_map/ppermute | solution.py:255
  82.5 1.3 %collective-permute-start.17 = (bf16[160,1280]{1,0:T(8,128)(2,1)S(1)}, bf16[160,1280]{1,0:T(8,128)(2,1)S(1)}, u32[]{:S(2)}, u32[]{:S(2)}) collective-permute-start(bf16[160,1280]{1,0:T(8,128)(2,1)S(1)} %add.33), channel_id=1, source_target_pairs={{3,2},{2,1},{1,0},{7,6},{6,5},{5,4},{11,10},{10,9},{9,8},{15,14},{... | collective-permute-start | bytes 1228808 | tf_op jit(solution)/shard_map/ppermute | solution.py:256
  83.8 1.5 %collective-permute-done.14 = bf16[160,1280]{1,0:T(8,128)(2,1)S(1)} collective-permute-done((bf16[160,1280]{1,0:T(8,128)(2,1)S(1)}, bf16[160,1280]{1,0:T(8,128)(2,1)S(1)}, u32[]{:S(2)}, u32[]{:S(2)}) %collective-permute-start.14) | collective-permute-done | bytes 409632 | tf_op jit(solution)/shard_map/ppermute | solution.py:255
  85.4 4.4 %collective-permute-start.15 = (bf16[160,1280]{1,0:T(8,128)(2,1)S(1)}, bf16[160,1280]{1,0:T(8,128)(2,1)S(1)}, u32[]{:S(2)}, u32[]{:S(2)}) collective-permute-start(bf16[160,1280]{1,0:T(8,128)(2,1)S(1)} %add.31), channel_id=1, source_target_pairs={{0,1},{1,2},{2,3},{4,5},{5,6},{6,7},{8,9},{9,10},{10,11},{12,13},{... | collective-permute-start | bytes 1228808 | tf_op jit(solution)/shard_map/ppermute | solution.py:255
  91.3 2.8 %collective-permute-done.22 = bf16[160,1280]{1,0:T(8,128)(2,1)S(1)} collective-permute-done((bf16[160,1280]{1,0:T(8,128)(2,1)S(1)}, bf16[160,1280]{1,0:T(8,128)(2,1)S(1)}, u32[]{:S(2)}, u32[]{:S(2)}) %collective-permute-start.22) | collective-permute-done | bytes 409632 | tf_op jit(solution)/shard_map/ppermute | solution.py:255
  94.2 4.4 %collective-permute-start.23 = (bf16[160,1280]{1,0:T(8,128)(2,1)S(1)}, bf16[160,1280]{1,0:T(8,128)(2,1)S(1)}, u32[]{:S(2)}, u32[]{:S(2)}) collective-permute-start(bf16[160,1280]{1,0:T(8,128)(2,1)S(1)} %add.36), channel_id=1, source_target_pairs={{0,1},{1,2},{2,3},{4,5},{5,6},{6,7},{8,9},{9,10},{10,11},{12,13},{... | collective-permute-start | bytes 1228808 | tf_op jit(solution)/shard_map/ppermute | solution.py:255
  98.7 4.2 %collective-permute-done.15 = bf16[160,1280]{1,0:T(8,128)(2,1)S(1)} collective-permute-done((bf16[160,1280]{1,0:T(8,128)(2,1)S(1)}, bf16[160,1280]{1,0:T(8,128)(2,1)S(1)}, u32[]{:S(2)}, u32[]{:S(2)}) %collective-permute-start.15) | collective-permute-done | bytes 409632 | tf_op jit(solution)/shard_map/ppermute | solution.py:255
  103.0 4.7 %collective-permute-done.23 = bf16[160,1280]{1,0:T(8,128)(2,1)S(1)} collective-permute-done((bf16[160,1280]{1,0:T(8,128)(2,1)S(1)}, bf16[160,1280]{1,0:T(8,128)(2,1)S(1)}, u32[]{:S(2)}, u32[]{:S(2)}) %collective-permute-start.23) | collective-permute-done | bytes 409632 | tf_op jit(solution)/shard_map/ppermute | solution.py:255
  (59 shorter events, 13.9 us)
Async XLA Ops:
  2.2 18.5 %collective-permute-start.2 = (bf16[2320,128]{1,0:T(8,128)(2,1)}, bf16[2320,128]{1,0:T(8,128)(2,1)S(1)}, u32[]{:S(2)}, u32[]{:S(2)}) collective-permute-start(bf16[2320,128]{1,0:T(8,128)(2,1)} %get-tuple-element.36), channel_id=1, source_target_pairs={{0,24},{8,16},{16,8},{24,0},{1,25},{9,17},{17,9},{25,1},{2,26},{10... | collective-permute-start | bytes 1781768 | tf_op jit(solution)/shard_map/ppermute | solution.py:271
  6.5 26.1 %collective-permute-start.1 = (bf16[2320,128]{1,0:T(8,128)(2,1)S(1)}, bf16[2320,128]{1,0:T(8,128)(2,1)S(1)}, u32[]{:S(2)}, u32[]{:S(2)}) collective-permute-start(bf16[2320,128]{1,0:T(8,128)(2,1)S(1)} %get-tuple-element.35), channel_id=1, source_target_pairs={{0,16},{8,24},{16,0},{24,8},{1,17},{9,25},{17,1},{25,9},{2,18},{10... | collective-permute-start | bytes 1781768 | tf_op jit(solution)/shard_map/ppermute | solution.py:271
  7.4 25.5 %collective-permute-start = (bf16[2320,128]{1,0:T(8,128)(2,1)S(1)}, bf16[2320,128]{1,0:T(8,128)(2,1)S(1)}, u32[]{:S(2)}, u32[]{:S(2)}) collective-permute-start(bf16[2320,128]{1,0:T(8,128)(2,1)S(1)} %get-tuple-element.34), channel_id=1, source_target_pairs={{0,8},{8,0},{16,24},{24,16},{1,9},{9,1},{17,25},{25,17},{2,10},{10... | collective-permute-start | bytes 1781768 | tf_op jit(solution)/shard_map/ppermute | solution.py:271
  7.8 27.2 %collective-permute-start.3 = (bf16[2320,128]{1,0:T(8,128)(2,1)S(1)}, bf16[2320,128]{1,0:T(8,128)(2,1)S(1)}, u32[]{:S(2)}, u32[]{:S(2)}) collective-permute-start(bf16[2320,128]{1,0:T(8,128)(2,1)S(1)} %get-tuple-element.33.refs_1_.refs_5_), channel_id=1, source_target_pairs={{0,4},{4,0},{1,5},{5,1},{2,6},{6,2},{3,7},{7,3},{8,12},{12,8},{9,1... | collective-permute-start | bytes 1781768 | tf_op jit(solution)/shard_map/ppermute | solution.py:275
  20.7 15.5 %collective-permute-start.6 = (bf16[2320,128]{1,0:T(8,128)(2,1)S(1)}, bf16[2320,128]{1,0:T(8,128)(2,1)S(1)}, u32[]{:S(2)}, u32[]{:S(2)}) collective-permute-start(bf16[2320,128]{1,0:T(8,128)(2,1)S(1)} %collective-permute-done.2.refs_4_.refs_8_), channel_id=1, source_target_pairs={{0,4},{4,0},{1,5},{5,1},{2,6},{6,2},{3,7},{7,3},{8,12},{12,8},{9,1... | collective-permute-start | bytes 1781768 | tf_op jit(solution)/shard_map/ppermute | solution.py:275
  33.1 11.9 %collective-permute-start.12 = (bf16[400,128]{1,0:T(8,128)(2,1)S(1)}, bf16[400,128]{1,0:T(8,128)(2,1)S(1)}, u32[]{:S(2)}, u32[]{:S(2)}) collective-permute-start(bf16[400,128]{1,0:T(8,128)(2,1)S(1)} %copy-done.5), channel_id=1, source_target_pairs={{0,24},{8,16},{16,8},{24,0},{1,25},{9,17},{17,9},{25,1},{2,26},{10... | collective-permute-start | bytes 307208 | tf_op jit(solution)/shard_map/ppermute | solution.py:271
  35.0 11.0 %collective-permute-start.11 = (bf16[400,128]{1,0:T(8,128)(2,1)S(1)}, bf16[400,128]{1,0:T(8,128)(2,1)S(1)}, u32[]{:S(2)}, u32[]{:S(2)}) collective-permute-start(bf16[400,128]{1,0:T(8,128)(2,1)S(1)} %get-tuple-element.46), channel_id=1, source_target_pairs={{0,16},{8,24},{16,0},{24,8},{1,17},{9,25},{17,1},{25,9},{2,18},{10... | collective-permute-start | bytes 307208 | tf_op jit(solution)/shard_map/ppermute | solution.py:271
  36.2 9.8 %collective-permute-start.10 = (bf16[400,128]{1,0:T(8,128)(2,1)S(1)}, bf16[400,128]{1,0:T(8,128)(2,1)S(1)}, u32[]{:S(2)}, u32[]{:S(2)}) collective-permute-start(bf16[400,128]{1,0:T(8,128)(2,1)S(1)} %get-tuple-element.45), channel_id=1, source_target_pairs={{0,8},{8,0},{16,24},{24,16},{1,9},{9,1},{17,25},{25,17},{2,10},{10... | collective-permute-start | bytes 307208 | tf_op jit(solution)/shard_map/ppermute | solution.py:271
  42.4 9.4 %collective-permute-start.7 = (bf16[400,128]{1,0:T(8,128)(2,1)S(1)}, bf16[400,128]{1,0:T(8,128)(2,1)S(1)}, u32[]{:S(2)}, u32[]{:S(2)}) collective-permute-start(bf16[400,128]{1,0:T(8,128)(2,1)S(1)} %get-tuple-element.38), channel_id=1, source_target_pairs={{0,8},{8,0},{16,24},{24,16},{1,9},{9,1},{17,25},{25,17},{2,10},{10... | collective-permute-start | bytes 307208 | tf_op jit(solution)/shard_map/ppermute | solution.py:271
  44.2 7.6 %collective-permute-start.8 = (bf16[400,128]{1,0:T(8,128)(2,1)S(1)}, bf16[400,128]{1,0:T(8,128)(2,1)S(1)}, u32[]{:S(2)}, u32[]{:S(2)}) collective-permute-start(bf16[400,128]{1,0:T(8,128)(2,1)S(1)} %get-tuple-element.39), channel_id=1, source_target_pairs={{0,16},{8,24},{16,0},{24,8},{1,17},{9,25},{17,1},{25,9},{2,18},{10... | collective-permute-start | bytes 307208 | tf_op jit(solution)/shard_map/ppermute | solution.py:271
  45.0 6.8 %collective-permute-start.9 = (bf16[400,128]{1,0:T(8,128)(2,1)S(1)}, bf16[400,128]{1,0:T(8,128)(2,1)S(1)}, u32[]{:S(2)}, u32[]{:S(2)}) collective-permute-start(bf16[400,128]{1,0:T(8,128)(2,1)S(1)} %get-tuple-element.40), channel_id=1, source_target_pairs={{0,24},{8,16},{16,8},{24,0},{1,25},{9,17},{17,9},{25,1},{2,26},{10... | collective-permute-start | bytes 307208 | tf_op jit(solution)/shard_map/ppermute | solution.py:271
  52.8 13.9 %collective-permute-start.13 = (bf16[160,1280]{1,0:T(8,128)(2,1)S(1)}, bf16[160,1280]{1,0:T(8,128)(2,1)S(1)}, u32[]{:S(2)}, u32[]{:S(2)}) collective-permute-start(bf16[160,1280]{1,0:T(8,128)(2,1)S(1)} %project.5), channel_id=1, source_target_pairs={{0,1},{3,2},{4,5},{7,6},{8,9},{11,10},{12,13},{15,14},{16,17},{19,... | collective-permute-start | bytes 1228808 | tf_op jit(solution)/shard_map/ppermute | solution.py:240
  56.5 6.0 %collective-permute-start.18 = (bf16[400,128]{1,0:T(8,128)(2,1)S(1)}, bf16[400,128]{1,0:T(8,128)(2,1)S(1)}, u32[]{:S(2)}, u32[]{:S(2)}) collective-permute-start(bf16[400,128]{1,0:T(8,128)(2,1)S(1)} %get-tuple-element.54), channel_id=1, source_target_pairs={{0,8},{8,0},{16,24},{24,16},{1,9},{9,1},{17,25},{25,17},{2,10},{10... | collective-permute-start | bytes 307208 | tf_op jit(solution)/shard_map/ppermute | solution.py:271
  58.1 4.7 %collective-permute-start.19 = (bf16[400,128]{1,0:T(8,128)(2,1)S(1)}, bf16[400,128]{1,0:T(8,128)(2,1)S(1)}, u32[]{:S(2)}, u32[]{:S(2)}) collective-permute-start(bf16[400,128]{1,0:T(8,128)(2,1)S(1)} %get-tuple-element.55), channel_id=1, source_target_pairs={{0,16},{8,24},{16,0},{24,8},{1,17},{9,25},{17,1},{25,9},{2,18},{10... | collective-permute-start | bytes 307208 | tf_op jit(solution)/shard_map/ppermute | solution.py:271
  59.0 5.6 %collective-permute-start.20 = (bf16[400,128]{1,0:T(8,128)(2,1)S(1)}, bf16[400,128]{1,0:T(8,128)(2,1)S(1)}, u32[]{:S(2)}, u32[]{:S(2)}) collective-permute-start(bf16[400,128]{1,0:T(8,128)(2,1)S(1)} %get-tuple-element.56), channel_id=1, source_target_pairs={{0,24},{8,16},{16,8},{24,0},{1,25},{9,17},{17,9},{25,1},{2,26},{10... | collective-permute-start | bytes 307208 | tf_op jit(solution)/shard_map/ppermute | solution.py:271
  65.4 11.2 %collective-permute-start.21 = (bf16[160,1280]{1,0:T(8,128)(2,1)S(1)}, bf16[160,1280]{1,0:T(8,128)(2,1)S(1)}, u32[]{:S(2)}, u32[]{:S(2)}) collective-permute-start(bf16[160,1280]{1,0:T(8,128)(2,1)S(1)} %project.7), channel_id=1, source_target_pairs={{0,1},{3,2},{4,5},{7,6},{8,9},{11,10},{12,13},{15,14},{16,17},{19,... | collective-permute-start | bytes 1228808 | tf_op jit(solution)/shard_map/ppermute | solution.py:240
  66.8 15.6 %collective-permute-start.16 = (bf16[160,1280]{1,0:T(8,128)(2,1)S(1)}, bf16[160,1280]{1,0:T(8,128)(2,1)S(1)}, u32[]{:S(2)}, u32[]{:S(2)}) collective-permute-start(bf16[160,1280]{1,0:T(8,128)(2,1)S(1)} %add.30), channel_id=1, source_target_pairs={{3,2},{2,1},{7,6},{6,5},{11,10},{10,9},{15,14},{14,13},{19,18},{18... | collective-permute-start | bytes 1228808 | tf_op jit(solution)/shard_map/ppermute | solution.py:256
  67.5 17.8 %collective-permute-start.14 = (bf16[160,1280]{1,0:T(8,128)(2,1)S(1)}, bf16[160,1280]{1,0:T(8,128)(2,1)S(1)}, u32[]{:S(2)}, u32[]{:S(2)}) collective-permute-start(bf16[160,1280]{1,0:T(8,128)(2,1)S(1)} %add.30), channel_id=1, source_target_pairs={{0,1},{1,2},{4,5},{5,6},{8,9},{9,10},{12,13},{13,14},{16,17},{17,1... | collective-permute-start | bytes 1228808 | tf_op jit(solution)/shard_map/ppermute | solution.py:255
  76.7 13.2 %collective-permute-start.24 = (bf16[160,1280]{1,0:T(8,128)(2,1)S(1)}, bf16[160,1280]{1,0:T(8,128)(2,1)S(1)}, u32[]{:S(2)}, u32[]{:S(2)}) collective-permute-start(bf16[160,1280]{1,0:T(8,128)(2,1)S(1)} %add.35), channel_id=1, source_target_pairs={{3,2},{2,1},{7,6},{6,5},{11,10},{10,9},{15,14},{14,13},{19,18},{18... | collective-permute-start | bytes 1228808 | tf_op jit(solution)/shard_map/ppermute | solution.py:256
  77.4 16.8 %collective-permute-start.22 = (bf16[160,1280]{1,0:T(8,128)(2,1)S(1)}, bf16[160,1280]{1,0:T(8,128)(2,1)S(1)}, u32[]{:S(2)}, u32[]{:S(2)}) collective-permute-start(bf16[160,1280]{1,0:T(8,128)(2,1)S(1)} %add.35), channel_id=1, source_target_pairs={{0,1},{1,2},{4,5},{5,6},{8,9},{9,10},{12,13},{13,14},{16,17},{17,1... | collective-permute-start | bytes 1228808 | tf_op jit(solution)/shard_map/ppermute | solution.py:255
  82.5 16.1 %collective-permute-start.17 = (bf16[160,1280]{1,0:T(8,128)(2,1)S(1)}, bf16[160,1280]{1,0:T(8,128)(2,1)S(1)}, u32[]{:S(2)}, u32[]{:S(2)}) collective-permute-start(bf16[160,1280]{1,0:T(8,128)(2,1)S(1)} %add.33), channel_id=1, source_target_pairs={{3,2},{2,1},{1,0},{7,6},{6,5},{5,4},{11,10},{10,9},{9,8},{15,14},{... | collective-permute-start | bytes 1228808 | tf_op jit(solution)/shard_map/ppermute | solution.py:256
  85.4 17.5 %collective-permute-start.15 = (bf16[160,1280]{1,0:T(8,128)(2,1)S(1)}, bf16[160,1280]{1,0:T(8,128)(2,1)S(1)}, u32[]{:S(2)}, u32[]{:S(2)}) collective-permute-start(bf16[160,1280]{1,0:T(8,128)(2,1)S(1)} %add.31), channel_id=1, source_target_pairs={{0,1},{1,2},{2,3},{4,5},{5,6},{6,7},{8,9},{9,10},{10,11},{12,13},{... | collective-permute-start | bytes 1228808 | tf_op jit(solution)/shard_map/ppermute | solution.py:255
  90.0 13.0 %collective-permute-start.25 = (bf16[160,1280]{1,0:T(8,128)(2,1)S(1)}, bf16[160,1280]{1,0:T(8,128)(2,1)S(1)}, u32[]{:S(2)}, u32[]{:S(2)}) collective-permute-start(bf16[160,1280]{1,0:T(8,128)(2,1)S(1)} %add.38), channel_id=1, source_target_pairs={{3,2},{2,1},{1,0},{7,6},{6,5},{5,4},{11,10},{10,9},{9,8},{15,14},{... | collective-permute-start | bytes 1228808 | tf_op jit(solution)/shard_map/ppermute | solution.py:256
  94.2 13.5 %collective-permute-start.23 = (bf16[160,1280]{1,0:T(8,128)(2,1)S(1)}, bf16[160,1280]{1,0:T(8,128)(2,1)S(1)}, u32[]{:S(2)}, u32[]{:S(2)}) collective-permute-start(bf16[160,1280]{1,0:T(8,128)(2,1)S(1)} %add.36), channel_id=1, source_target_pairs={{0,1},{1,2},{2,3},{4,5},{5,6},{6,7},{8,9},{9,10},{10,11},{12,13},{... | collective-permute-start | bytes 1228808 | tf_op jit(solution)/shard_map/ppermute | solution.py:255
  (8 other events, 96.6 us)
